TPU v7x, 32 devices: a whole 2x2x4 slice. The times are simulated.
32 devices in a mesh: out: 16 (over z, y, x), con: 2 (over core).
Axes of the slice: x: 2, y: 2, z: 4, core: 2. Of those that a mesh axis runs over, the one named last changes fastest.
Arguments:
- amplitudes: bfloat16 [512, 9216], P(('out', 'con')), may hold values from -6 to 6
- integrals: bfloat16 [16384, 9216], P('out', 'con'), may hold values from -0.078125 to 0.078125
- block_sizes: int32 [8], replicated, may hold values from 64 to 192, as said below
Outputs:
- ladder: bfloat16 [512, 16384], P('con', 'out')
Inputs may be any that keep to these rules, and one draw needn't show every extreme that they name: `block_sizes`: each entry lies between 64 and 192; the entries sum to 1024; one entry equals 192 and one equals 64.
All inputs are finite; a program needn't handle non-finite values.
Results may differ from a plain program's by a relative error of at most 0.001.
Values may be sent and summed in bfloat16 or wider, within the bound.
No kernel may reach another device: no remote copies, remote signals or barrier semaphores. Data moves between devices by JAX's collectives and lax.ppermute only.
A program may use at most 64 MiB of HBM per device.

v0:
```python
import jax
import jax.numpy as jnp
from jax import lax
from jax.sharding import PartitionSpec as P

DMAX = 192


def mask_slots(amplitudes, block_sizes):
    row_count = amplitudes.shape[0]
    nirrep = block_sizes.shape[0]
    blocked = amplitudes.reshape(row_count, nirrep, -1, DMAX)
    valid_cols = jnp.arange(DMAX, dtype=jnp.int32)[None, :] < block_sizes[:, None]
    masked = jnp.where(valid_cols[None, :, None, :], blocked, jnp.zeros((), amplitudes.dtype))
    return masked.reshape(row_count, -1)


def contract(amp_rows, integrals):
    return lax.dot_general(
        amp_rows, integrals, (((1,), (1,)), ((), ())), preferred_element_type=jnp.float32
    )


def on_device(amplitudes, integrals, block_sizes):
    masked = mask_slots(amplitudes, block_sizes)
    gathered = lax.all_gather(masked, "out", axis=0, tiled=True)
    own_columns = lax.all_to_all(gathered, "con", split_axis=1, concat_axis=0, tiled=True)
    out_count = lax.axis_size("out")
    con_count = lax.axis_size("con")
    per_device = masked.shape[0]
    own_columns = own_columns.reshape(con_count, out_count, per_device, -1)
    own_columns = jnp.transpose(own_columns, (1, 0, 2, 3)).reshape(
        con_count * out_count * per_device, -1
    )
    partial_sums = contract(own_columns, integrals)
    ladder = lax.psum_scatter(partial_sums, "con", scatter_dimension=0, tiled=True)
    return ladder.astype(jnp.bfloat16)


def solution(mesh):
    in_specs = (P(("out", "con"), None), P("out", "con"), P())
    out_specs = P("con", "out")
    return jax.shard_map(
        on_device, mesh=mesh, in_specs=in_specs, out_specs=out_specs, check_vma=False
    )
```

profile of v0, /device:TPU:25, one launch (start us, length us, event | category | flops | bytes accessed | tf_op | source)
XLA Modules:
  0.0 147.4 jit_solution(692062793632357713)
XLA Ops:
  6.5 0.0 all-gather.2.cloned.1.call-start
  6.5 0.7 iota_compare_fusion
  7.3 0.1 broadcast_in_dim.20
  7.4 1.7 %broadcast_select_fusion = bf16[16,9216]{1,0:T(8,128)(2,1)} fusion(bf16[16,9216]{1,0:T(8,128)(2,1)} %param.3, pred[9216]{0:T(1024)(128)(4,1)S(1)} %broadcast_in_dim.20), kind=kLoop, calls=%fused_computation | loop fusion | flops 147456 | bytes 599040 | tf_op jit(solution)/shard_map/jit(_where)/select_n | solution.py:14
  9.1 0.0 all-gather.2.cloned.1.call-update
  9.1 0.0 reduce-scatter.2.cloned.1.call-start
  9.2 81.1 %all-gather.2.cloned.1.call-done = bf16[256,9216]{1,0:T(8,128)(2,1)} async-done(((bf16[16,9216]{1,0:T(8,128)(2,1)}), bf16[256,9216]{1,0:T(8,128)(2,1)}) %all-gather.2.cloned.1.call-update) | async-done | bytes 4718608 | tf_op jit(solution)/shard_map/all_gather | solution.py:26
  90.3 6.6 %copy.8 = bf16[256,9216]{0,1:T(8,128)(2,1)} copy(bf16[256,9216]{1,0:T(8,128)(2,1)} %all-gather.2.cloned.1.call-done) | data formatting | bytes 9437184 | tf_op jit(solution)/shard_map/all_gather | solution.py:26
  96.9 12.9 %all_to_all.16 = bf16[256,2,4608]{0,2,1:T(8,128)(2,1)} all-to-all(bf16[256,2,4608]{0,2,1:T(8,128)(2,1)} %bitcast.8), channel_id=1, replica_groups=mesh['out'=16,'con'=2] {'con'}, dimensions={1} | all-to-all | bytes 9437184 | tf_op jit(solution)/shard_map/all_to_all | solution.py:27
  109.9 6.7 %copy.9 = bf16[2,256,4608]{2,1,0:T(8,128)(2,1)} copy(bf16[2,256,4608]{1,2,0:T(8,128)(2,1)} %bitcast.9) | data formatting | bytes 9437184 | tf_op jit(solution)/shard_map/all_to_all | solution.py:27
  116.6 2.6 %copy.10 = bf16[16,2,16,4608]{3,2,1,0:T(8,128)(2,1)S(1)} copy(bf16[16,2,16,4608]{3,2,0,1:T(8,128)(2,1)} %bitcast.10) | data formatting | bytes 9437184 | tf_op jit(solution)/shard_map/transpose | solution.py:32
  119.3 8.9 %fusion = f32[512,1024]{1,0:T(8,128)} fusion(bf16[512,4608]{1,0:T(8,128)(2,1)S(1)} %bitcast.11, bf16[1024,4608]{1,0:T(8,128)(2,1)} %param.4), kind=kOutput, calls=%fused_computation.2 | convolution fusion | flops 4831838208 | bytes 16252928 | tf_op jit(solution)/shard_map/dot_general | solution.py:19
  128.2 0.0 reduce-scatter.2.cloned.1.call-update
  128.2 10.2 %reduce-scatter.2.cloned.1.call-done = f32[256,1024]{1,0:T(8,128)} async-done(((f32[512,1024]{1,0:T(8,128)}), f32[256,1024]{1,0:T(8,128)}) %reduce-scatter.2.cloned.1.call-update) | async-done | bytes 1048592 | tf_op jit(solution)/shard_map/reduce_scatter | solution.py:36
  138.5 2.1 %convert_element_type.3 = bf16[256,1024]{1,0:T(8,128)(2,1)} convert(f32[256,1024]{1,0:T(8,128)} %reduce-scatter.2.cloned.1.call-done) | non-fusion elementwise | flops 262144 | bytes 1572864 | tf_op jit(solution)/shard_map/convert_element_type | solution.py:37
  (1 shorter events, 0.0 us)
Async XLA Ops:
  6.5 83.8 %all-gather.2.cloned.1.call-start = ((), (), s32[]{:S(2)}) async-start(), calls=%async_computation.2 | async-start | bytes 5013504 | tf_op jit(solution)/shard_map/all_gather | solution.py:26
  9.1 129.3 %reduce-scatter.2.cloned.1.call-start = ((), (), s32[]{:S(2)}) async-start(), calls=%async_computation.3 | async-start | bytes 3145728 | tf_op jit(solution)/shard_map/reduce_scatter | solution.py:36
Sparse Core Ops, SparseCore 0:
  10.2 80.1 all-gather.1
  128.4 10.0 reduce-scatter.1
where the time goes:
time: 149 us; the launch traced here: 147 us
  waiting for transfers between devices  91.4 us (61%)
  local copies, waits for them, and re-layouts  16.1 us (11%)
  between operations  13.4 us (9%)
  blocking collectives  12.9 us (9%)
  matrix products  8.94 us (6%)
  other arithmetic  4.55 us (3%)
    all_gather x1, waiting for transfers between devices, on_device(): gathered = lax.all_gather(masked, 'out', axis=0, tiled=True)  81.1 us
    all_to_all x1, blocking collectives, on_device(): lax.all_to_all(gathered, 'con', split_axis=1, concat_axis=0, tiled=True)  12.9 us
    reduce_scatter x1, waiting for transfers between devices, on_device(): lax.psum_scatter(partial_sums, 'con', scatter_dimension=0, tiled=True)  10.2 us
    dot_general x1, matrix products, contract(): lax.dot_general(amp_rows, integrals, (((1,), (1,)), ((), ())), preferred_...  8.94 us
    all_to_all x1, local copies, waits for them, and re-layouts, on_device(): lax.all_to_all(gathered, 'con', split_axis=1, concat_axis=0, tiled=True)  6.75 us
    all_gather x1, local copies, waits for them, and re-layouts, on_device(): gathered = lax.all_gather(masked, 'out', axis=0, tiled=True)  6.64 us
  transfers between devices with their start and end apart: 2, of which 2 were waited for; matrix products, arithmetic and copies ran while one was open for 0% of the time, Pallas kernels for 0%

commit v1 on v0

--- a/solution.py
+++ b/solution.py
@@ -1,9 +1,16 @@
+import functools
+
 import jax
 import jax.numpy as jnp
 from jax import lax
+from jax.experimental import pallas as pl
+from jax.experimental.pallas import tpu as pltpu
 from jax.sharding import PartitionSpec as P
 
 DMAX = 192
+LANES = 128
+LOW = 64
+ROWS = 16
 
 
 def mask_slots(amplitudes, block_sizes):
@@ -15,13 +22,7 @@
     return masked.reshape(row_count, -1)
 
 
-def contract(amp_rows, integrals):
-    return lax.dot_general(
-        amp_rows, integrals, (((1,), (1,)), ((), ())), preferred_element_type=jnp.float32
-    )
-
-
-def on_device(amplitudes, integrals, block_sizes):
+def general(amplitudes, integrals, block_sizes):
     masked = mask_slots(amplitudes, block_sizes)
     gathered = lax.all_gather(masked, "out", axis=0, tiled=True)
     own_columns = lax.all_to_all(gathered, "con", split_axis=1, concat_axis=0, tiled=True)
@@ -32,9 +33,230 @@
     own_columns = jnp.transpose(own_columns, (1, 0, 2, 3)).reshape(
         con_count * out_count * per_device, -1
     )
-    partial_sums = contract(own_columns, integrals)
+    partial_sums = lax.dot_general(
+        own_columns, integrals, (((1,), (1,)), ((), ())), preferred_element_type=jnp.float32
+    )
     ladder = lax.psum_scatter(partial_sums, "con", scatter_dimension=0, tiled=True)
     return ladder.astype(jnp.bfloat16)
+
+
+def roll(x, shift):
+    return pltpu.roll(x.astype(jnp.float32), shift, 1).astype(x.dtype)
+
+
+def pack_kernel(nirrep, cw, sizes_ref, amp_ref, out_ref):
+    pairs = cw // 2
+    rows = amp_ref.shape[0]
+    lane = lax.broadcasted_iota(jnp.int32, (rows, LANES), 1)
+    low = lane < LOW
+    tiles = nirrep // 2
+    extras = [[jnp.zeros((rows, LANES), amp_ref.dtype)] * tiles for _ in range(cw)]
+    start = jnp.int32(0)
+    for g in range(nirrep):
+        extra = sizes_ref[g] - LOW
+        inside = [
+            (lane + k * LANES >= start) & (lane + k * LANES < start + extra) for k in range(tiles)
+        ]
+        shift = lax.rem(start, LANES)
+        shift_half = lax.rem(start + LOW, LANES)
+        for p in range(pairs):
+            at = (g * pairs + p) * 3 * LANES
+            one = amp_ref[:, at : at + LANES]
+            two = amp_ref[:, at + LANES : at + 2 * LANES]
+            three = amp_ref[:, at + 2 * LANES : at + 3 * LANES]
+            to = (g * pairs + p) * LANES
+            out_ref[:, to : to + LANES] = jnp.where(low, one, two)
+            first = roll(jnp.where(low, two, one), shift_half)
+            second = roll(three, shift)
+            for k in range(tiles):
+                extras[2 * p][k] = jnp.where(inside[k], first, extras[2 * p][k])
+                extras[2 * p + 1][k] = jnp.where(inside[k], second, extras[2 * p + 1][k])
+        start = start + extra
+    base = nirrep * pairs * LANES
+    for c in range(cw):
+        for k in range(tiles):
+            to = base + (c * tiles + k) * LANES
+            out_ref[:, to : to + LANES] = extras[c][k]
+
+
+def pack(amplitudes, block_sizes, cw):
+    nirrep = block_sizes.shape[0]
+    return pl.pallas_call(
+        functools.partial(pack_kernel, nirrep, cw),
+        out_shape=jax.ShapeDtypeStruct(
+            (amplitudes.shape[0], nirrep * cw * LANES), amplitudes.dtype
+        ),
+        in_specs=[
+            pl.BlockSpec(memory_space=pltpu.SMEM),
+            pl.BlockSpec(memory_space=pltpu.VMEM),
+        ],
+        out_specs=pl.BlockSpec(memory_space=pltpu.VMEM),
+        name="pack",
+    )(block_sizes, amplitudes)
+
+
+def unpack_rows(cw, nirrep, sizes_ref, con, piece, places, a_ref):
+    pairs = cw // 2
+    tiles = nirrep // 2
+    base = nirrep * pairs * LANES
+    rows = piece.shape[0]
+    lane = lax.broadcasted_iota(jnp.int32, (rows, LANES), 1)
+    low = lane < LOW
+    own = nirrep // 2
+    zero = jnp.zeros((rows, LANES), piece.dtype)
+    start = jnp.int32(0)
+    for g in range(own):
+        start = start + jnp.where(con > 0, sizes_ref[g] - LOW, 0)
+    for gg in range(own):
+        g = con * own + gg
+        extra = sizes_ref[g] - LOW
+        tile = start // LANES
+        shift = start - tile * LANES
+        after = jnp.minimum(tile + 1, tiles - 1)
+        tile = jnp.minimum(tile, tiles - 1)
+        here = lane >= shift
+        back = lax.rem(LANES - shift, LANES)
+        back_half = lax.rem(LANES + LOW - shift, LANES)
+        valid = lane < extra
+        valid_half = jnp.where(low, lane + LOW, lane - LOW) < extra
+        for p in range(pairs):
+            at = pl.multiple_of((g * pairs + p) * LANES, LANES)
+            both = piece[:, pl.ds(at, LANES)]
+            halves = []
+            for c in (2 * p, 2 * p + 1):
+                one = piece[:, pl.ds(pl.multiple_of(base + (c * tiles + tile) * LANES, LANES), LANES)]
+                two = piece[:, pl.ds(pl.multiple_of(base + (c * tiles + after) * LANES, LANES), LANES)]
+                halves.append(jnp.where(here, one, two))
+            first = jnp.where(valid_half, roll(halves[0], back_half), zero)
+            second = jnp.where(valid, roll(halves[1], back), zero)
+            to = (gg * pairs + p) * 3 * LANES
+            values = (jnp.where(low, both, first), jnp.where(low, first, both), second)
+            for i, place in enumerate(places):
+                for t, value in enumerate(values):
+                    a_ref[pl.ds(place, ROWS), to + t * LANES : to + (t + 1) * LANES] = value[
+                        i * ROWS : (i + 1) * ROWS
+                    ]
+        start = start + extra
+
+
+def contract_kernel(cw, nirrep, count, sizes_ref, con_ref, places_ref, *refs):
+    pieces = refs[:count]
+    w_ref, keep_ref, send_ref, a_ref = refs[count:]
+
+    @pl.when(pl.program_id(0) == 0)
+    def _():
+        for n, piece in enumerate(pieces):
+            places = [
+                pl.multiple_of(places_ref[2 * n + i], ROWS) for i in range(piece.shape[0] // ROWS)
+            ]
+            unpack_rows(cw, nirrep, sizes_ref, con_ref[0], piece, places, a_ref)
+
+    half = a_ref.shape[0] // 2
+    sums = lax.dot_general(
+        a_ref[...], w_ref[...], (((1,), (1,)), ((), ())), preferred_element_type=jnp.float32
+    )
+    keep_ref[...] = sums[:half]
+    send_ref[...] = sums[half:]
+
+
+def contract(sizes, con, places, pieces, integrals, cw):
+    nirrep = sizes.shape[0]
+    total = sum(p.shape[0] for p in pieces)
+    n, k = integrals.shape
+    block = 256
+    half = jax.ShapeDtypeStruct((total // 2, n), jnp.float32)
+    out_spec = pl.BlockSpec((total // 2, block), lambda i, *_: (0, i))
+    return pl.pallas_call(
+        functools.partial(contract_kernel, cw, nirrep, len(pieces)),
+        out_shape=(half, half),
+        grid_spec=pltpu.PrefetchScalarGridSpec(
+            num_scalar_prefetch=3,
+            grid=(n // block,),
+            in_specs=[pl.BlockSpec(p.shape, lambda i, *_: (0, 0)) for p in pieces]
+            + [pl.BlockSpec((block, k), lambda i, *_: (i, 0))],
+            out_specs=(out_spec, out_spec),
+            scratch_shapes=[pltpu.VMEM((total, k), jnp.bfloat16)],
+        ),
+        compiler_params=pltpu.CompilerParams(vmem_limit_bytes=48 * 2**20),
+        name="contract",
+    )(sizes, con.reshape(1), places, *pieces, integrals)
+
+
+RING = (1, 3, 0, 2)
+RING_BACK = (2, 0, 3, 1)
+
+
+def chip_at(x, y, z):
+    return (z * 2 + y) * 2 + x
+
+
+def x_neighbour(o):
+    return o ^ 1
+
+
+def y_neighbour(o):
+    return o ^ 2
+
+
+def z_next(o):
+    return RING[o // 4] * 4 + o % 4
+
+
+def z_previous(o):
+    return RING_BACK[o // 4] * 4 + o % 4
+
+
+def ladder_of_16(amplitudes, integrals, block_sizes):
+    out_count, con_count = lax.axis_size("out"), lax.axis_size("con")
+    con = lax.axis_index("con")
+    chip = lax.axis_index("out")
+
+    def move(value, *by_core):
+        pairs = [
+            (o * con_count + c, by_core[c % len(by_core)](o) * con_count + c)
+            for o in range(out_count)
+            for c in range(con_count)
+        ]
+        return lax.ppermute(value, ("out", "con"), pairs)
+
+    def swap_cores(value):
+        return lax.ppermute(value, "con", [(0, 1), (1, 0)])
+
+    cw = integrals.shape[1] // (block_sizes.shape[0] // con_count * DMAX)
+    own = pack(amplitudes, block_sizes, cw)
+    blocks = {0: own}
+    blocks[1] = move(own, z_next)
+    blocks[3] = move(own, z_previous)
+    blocks[2] = move(blocks[1], z_next)
+    pieces = []
+    for k in (0, 1, 3, 2):
+        there = move(blocks[k], x_neighbour, y_neighbour)
+        both = jnp.concatenate([blocks[k], there])
+        pieces += [both, move(both, y_neighbour, x_neighbour)]
+    others = [swap_cores(piece) for piece in pieces]
+
+    z = chip // 4
+    inside = chip % 4
+    ring_back = jnp.array(RING_BACK)
+    planes = {0: z, 1: ring_back[z], 3: jnp.array(RING)[z], 2: 3 - z}
+    places = []
+    for core in (con, 1 - con):
+        first = jnp.where(core == 0, inside ^ 1, inside ^ 2)
+        second = jnp.where(core == 0, inside ^ 2, inside ^ 1)
+        for k in (0, 1, 3, 2):
+            for where in (inside, first, second, inside ^ 3):
+                place = (planes[k] * 4 + where) * con_count + core
+                places.append(place * ROWS)
+    total = out_count * con_count * ROWS
+    places = lax.rem(jnp.stack(places) + total - con * (total // 2), total)
+    keep, send = contract(block_sizes, con, places, pieces + others, integrals, cw)
+    return (keep + swap_cores(send)).astype(jnp.bfloat16)
+
+
+def on_device(amplitudes, integrals, block_sizes):
+    if amplitudes.shape[0] == ROWS and lax.axis_size("out") == 16:
+        return ladder_of_16(amplitudes, integrals, block_sizes)
+    return general(amplitudes, integrals, block_sizes)
 
 
 def solution(mesh):

time: 149 us -> 69.7 us (0.47)
  the two profiles are of different devices: /device:TPU:25 before, /device:TPU:0 now
where the time goes in v1:
time: 69.7 us; the launch traced here: 69.4 us
  waiting for transfers between devices  30.9 us (44%)
  starting transfers between devices  16.1 us (23%)
  Pallas kernels  14.4 us (21%)
  local copies, waits for them, and re-layouts  3.35 us (5%)
  other arithmetic  3.12 us (4%)
  between operations  1.53 us (2%)
    ppermute x11, waiting for transfers between devices, move(): return lax.ppermute(value, ('out', 'con'), pairs)  28.4 us
    ppermute x11, starting transfers between devices, move(): return lax.ppermute(value, ('out', 'con'), pairs)  14.7 us
    pallas_call x1, Pallas kernels, contract(): pl.pallas_call(functools.partial(contract_kernel, cw, nirrep, len(pieces)...  12.6 us
    ppermute x9, waiting for transfers between devices, swap_cores(): return lax.ppermute(value, 'con', [(0, 1), (1, 0)])  2.52 us
    dynamic_slice x2, local copies, waits for them, and re-layouts, ladder_of_16(): planes = {0: z, 1: ring_back[z], 3: jnp.array(RING)[z], 2: 3 - z}  2.51 us
    convert_element_type x1, other arithmetic, ladder_of_16(): return (keep + swap_cores(send)).astype(jnp.bfloat16)  2.16 us
    pallas_call x1, Pallas kernels, pack(): pl.pallas_call(functools.partial(pack_kernel, nirrep, cw), out_shape=jax....  1.79 us
    ppermute x9, starting transfers between devices, swap_cores(): return lax.ppermute(value, 'con', [(0, 1), (1, 0)])  1.43 us
  transfers between devices with their start and end apart: 20, of which 7 were waited for; matrix products, arithmetic and copies ran while one was open for 5% of the time, Pallas kernels for 0%

profile of v1, /device:TPU:0, one launch (start us, length us, event | category | flops | bytes accessed | tf_op | source)
XLA Modules:
  0.0 69.4 jit_solution(15659042338556588807)
XLA Ops:
  0.0 1.8 %pack.1 = bf16[16,6144]{1,0:T(8,128)(2,1)} custom-call(s32[8]{0:T(128)} %sizes_ref.3, bf16[16,9216]{1,0:T(8,128)(2,1)} %amp_ref.1), custom_call_target="tpu_custom_call" | custom-call | tf_op jit(solution)/shard_map/pack/pallas_call | solution.py:84
  1.8 2.9 %collective-permute-start = (bf16[16,6144]{1,0:T(8,128)(2,1)}, bf16[16,6144]{1,0:T(8,128)(2,1)S(1)}, u32[]{:S(2)}, u32[]{:S(2)}) collective-permute-start(bf16[16,6144]{1,0:T(8,128)(2,1)} %pack.1), channel_id=1, source_target_pairs={{0,2},{1,5},{2,0},{3,7},{4,6},{5,1},{6,4},{7,3},{8,10},{9,13},{10,... | collective-permute-start | bytes 589832 | tf_op jit(solution)/shard_map/ppermute | solution.py:220
  4.7 2.6 %collective-permute-start.5 = (bf16[16,6144]{1,0:T(8,128)(2,1)}, bf16[16,6144]{1,0:T(8,128)(2,1)S(1)}, u32[]{:S(2)}, u32[]{:S(2)}) collective-permute-start(bf16[16,6144]{1,0:T(8,128)(2,1)} %pack.1), channel_id=1, source_target_pairs={{0,16},{1,17},{2,18},{3,19},{4,20},{5,21},{6,22},{7,23},{8,0},{9,1... | collective-permute-start | bytes 589832 | tf_op jit(solution)/shard_map/ppermute | solution.py:220
  7.3 1.3 %collective-permute-done = bf16[16,6144]{1,0:T(8,128)(2,1)S(1)} collective-permute-done((bf16[16,6144]{1,0:T(8,128)(2,1)}, bf16[16,6144]{1,0:T(8,128)(2,1)S(1)}, u32[]{:S(2)}, u32[]{:S(2)}) %collective-permute-start) | collective-permute-done | bytes 196640 | tf_op jit(solution)/shard_map/ppermute | solution.py:220
  8.6 1.0 %pad_maximum_fusion.refs_0_ = bf16[32,6144]{1,0:T(8,128)(2,1)S(1)} fusion(bf16[16,6144]{1,0:T(8,128)(2,1)S(1)} %collective-permute-done, bf16[16,6144]{1,0:T(8,128)(2,1)} %pack.1), kind=kLoop, calls=%fused_computation.1 | loop fusion | flops 786432 | bytes 786432 | tf_op jit(solution)/shard_map/concatenate | solution.py:234
  9.5 0.1 collective-permute-start.11
  9.6 2.1 %collective-permute-start.1 = (bf16[32,6144]{1,0:T(8,128)(2,1)S(1)}, bf16[32,6144]{1,0:T(8,128)(2,1)S(1)}, u32[]{:S(2)}, u32[]{:S(2)}) collective-permute-start(bf16[32,6144]{1,0:T(8,128)(2,1)S(1)} %pad_maximum_fusion.refs_0_), channel_id=1, source_target_pairs={{0,4},{1,3},{2,6},{3,1},{4,0},{5,7},{6,2},{7,5},{8,12},{9,11},{10,... | collective-permute-start | bytes 1179656 | tf_op jit(solution)/shard_map/ppermute | solution.py:220
  11.7 5.7 %collective-permute-done.2 = bf16[16,6144]{1,0:T(8,128)(2,1)S(1)} collective-permute-done((bf16[16,6144]{1,0:T(8,128)(2,1)}, bf16[16,6144]{1,0:T(8,128)(2,1)S(1)}, u32[]{:S(2)}, u32[]{:S(2)}) %collective-permute-start.2) | collective-permute-done | bytes 196640 | tf_op jit(solution)/shard_map/ppermute | solution.py:220
  17.5 0.7 %collective-permute-start.8 = (bf16[16,6144]{1,0:T(8,128)(2,1)S(1)}, bf16[16,6144]{1,0:T(8,128)(2,1)S(1)}, u32[]{:S(2)}, u32[]{:S(2)}) collective-permute-start(bf16[16,6144]{1,0:T(8,128)(2,1)S(1)} %collective-permute-done.2), channel_id=1, source_target_pairs={{0,8},{1,9},{2,10},{3,11},{4,12},{5,13},{6,14},{7,15},{8,24},{9,25... | collective-permute-start | bytes 589832 | tf_op jit(solution)/shard_map/ppermute | solution.py:220
  18.2 1.5 %collective-permute-start.3 = (bf16[16,6144]{1,0:T(8,128)(2,1)S(1)}, bf16[16,6144]{1,0:T(8,128)(2,1)S(1)}, u32[]{:S(2)}, u32[]{:S(2)}) collective-permute-start(bf16[16,6144]{1,0:T(8,128)(2,1)S(1)} %collective-permute-done.2), channel_id=1, source_target_pairs={{0,2},{1,5},{2,0},{3,7},{4,6},{5,1},{6,4},{7,3},{8,10},{9,13},{10,... | collective-permute-start | bytes 589832 | tf_op jit(solution)/shard_map/ppermute | solution.py:220
  19.7 0.6 collective-permute-start.6
  20.3 5.6 %collective-permute-done.6 = bf16[16,6144]{1,0:T(8,128)(2,1)S(1)} collective-permute-done((bf16[16,6144]{1,0:T(8,128)(2,1)S(1)}, bf16[16,6144]{1,0:T(8,128)(2,1)S(1)}, u32[]{:S(2)}, u32[]{:S(2)}) %collective-permute-start.6) | collective-permute-done | bytes 196640 | tf_op jit(solution)/shard_map/ppermute | solution.py:220
  26.0 0.1 collective-permute-start.15
  26.1 0.6 collective-permute-start.7
  26.7 1.6 %collective-permute-start.9 = (bf16[16,6144]{1,0:T(8,128)(2,1)S(1)}, bf16[16,6144]{1,0:T(8,128)(2,1)S(1)}, u32[]{:S(2)}, u32[]{:S(2)}) collective-permute-start(bf16[16,6144]{1,0:T(8,128)(2,1)S(1)} %collective-permute-done.8), channel_id=1, source_target_pairs={{0,2},{1,5},{2,0},{3,7},{4,6},{5,1},{6,4},{7,3},{8,10},{9,13},{10,... | collective-permute-start | bytes 589832 | tf_op jit(solution)/shard_map/ppermute | solution.py:220
  28.2 6.3 %collective-permute-done.9 = bf16[16,6144]{1,0:T(8,128)(2,1)S(1)} collective-permute-done((bf16[16,6144]{1,0:T(8,128)(2,1)S(1)}, bf16[16,6144]{1,0:T(8,128)(2,1)S(1)}, u32[]{:S(2)}, u32[]{:S(2)}) %collective-permute-start.9) | collective-permute-done | bytes 196640 | tf_op jit(solution)/shard_map/ppermute | solution.py:220
  34.5 0.2 collective-permute-start.13
  34.8 1.3 %collective-permute-start.4 = (bf16[32,6144]{1,0:T(8,128)(2,1)S(1)}, bf16[32,6144]{1,0:T(8,128)(2,1)}, u32[]{:S(2)}, u32[]{:S(2)}) collective-permute-start(bf16[32,6144]{1,0:T(8,128)(2,1)S(1)} %constant_dynamic-update-slice_fusion.refs_2_), channel_id=1, source_target_pairs={{0,4},{1,3},{2,6},{3,1},{4,0},{5,7},{6,2},{7,5},{8,12},{9,11},{10,... | collective-permute-start | bytes 1179656 | tf_op jit(solution)/shard_map/ppermute | solution.py:220
  36.1 0.8 %collective-permute-start.10 = (bf16[32,6144]{1,0:T(8,128)(2,1)S(1)}, bf16[32,6144]{1,0:T(8,128)(2,1)}, u32[]{:S(2)}, u32[]{:S(2)}) collective-permute-start(bf16[32,6144]{1,0:T(8,128)(2,1)S(1)} %constant_dynamic-update-slice_fusion.4.refs_6_), channel_id=1, source_target_pairs={{0,4},{1,3},{2,6},{3,1},{4,0},{5,7},{6,2},{7,5},{8,12},{9,11},{10,... | collective-permute-start | bytes 1179656 | tf_op jit(solution)/shard_map/ppermute | solution.py:220
  36.9 0.5 collective-permute-start.12
  37.4 0.1 collective-permute-start.16
  37.5 5.3 %collective-permute-done.4.refs_3_ = bf16[32,6144]{1,0:T(8,128)(2,1)} collective-permute-done((bf16[32,6144]{1,0:T(8,128)(2,1)S(1)}, bf16[32,6144]{1,0:T(8,128)(2,1)}, u32[]{:S(2)}, u32[]{:S(2)}) %collective-permute-start.4) | collective-permute-done | bytes 393248 | tf_op jit(solution)/shard_map/ppermute | solution.py:220
  42.7 4.2 %collective-permute-done.10.refs_7_ = bf16[32,6144]{1,0:T(8,128)(2,1)} collective-permute-done((bf16[32,6144]{1,0:T(8,128)(2,1)S(1)}, bf16[32,6144]{1,0:T(8,128)(2,1)}, u32[]{:S(2)}, u32[]{:S(2)}) %collective-permute-start.10) | collective-permute-done | bytes 393248 | tf_op jit(solution)/shard_map/ppermute | solution.py:220
  46.9 1.3 %dynamic_slice.7 = s32[1]{0:T(128)} dynamic-slice(s32[4]{0:T(128)} %constant.55.clone, s32[]{:T(128)S(6)} %select_n.31), dynamic_slice_sizes={1} | dynamic-slice | bytes 12 | tf_op jit(solution)/shard_map/dynamic_slice | solution.py:241
  48.8 1.3 %dynamic_slice.6 = s32[1]{0:T(128)} dynamic-slice(s32[4]{0:T(128)} %constant.54.clone, s32[]{:T(128)S(6)} %select_n.31), dynamic_slice_sizes={1} | dynamic-slice | bytes 12 | tf_op jit(solution)/shard_map/dynamic_slice | solution.py:241
  50.8 0.1 stack.131
  51.0 0.0 copy-start
  51.0 0.6 copy-done
  51.7 12.6 %contract.1 = (f32[256,1024]{1,0:T(8,128)}, f32[256,1024]{1,0:T(8,128)}) custom-call(s32[8]{0:T(128)S(1)} %copy-done, s32[1]{0:T(128)} %bitcast.con_ref, s32[32]{0:T(128)S(1)} %compare_select_fusion.places_ref, bf16[32,6144]{1,0:T(8,128)(2,1)S(1)} %pad_maximum_fusion.refs_0_, bf16[32,6144]{1,0:T(8,128)(2,1)S(1)} %collective-permute-done.1.refs_1_, ...), custom_call_target="tpu_custom_call" | custom-call | tf_op jit(solution)/shard_map/contract/pallas_call | solution.py:169
  64.2 0.5 collective-permute-start.19
  64.7 2.5 %collective-permute-done.19 = f32[256,1024]{1,0:T(8,128)S(1)} collective-permute-done((f32[256,1024]{1,0:T(8,128)}, f32[256,1024]{1,0:T(8,128)S(1)}, u32[]{:S(2)}, u32[]{:S(2)}) %collective-permute-start.19) | collective-permute-done | bytes 1048608 | tf_op jit(solution)/shard_map/ppermute | solution.py:223
  67.2 2.2 %add_convert_fusion = bf16[256,1024]{1,0:T(8,128)(2,1)} fusion(f32[256,1024]{1,0:T(8,128)} %get-tuple-element.7, f32[256,1024]{1,0:T(8,128)S(1)} %collective-permute-done.19), kind=kLoop, calls=%fused_computation | loop fusion | flops 524288 | bytes 2621440 | tf_op jit(solution)/shard_map/convert_element_type | solution.py:253
  (24 shorter events, 0.1 us)
Async XLA Ops:
  1.8 6.8 %collective-permute-start = (bf16[16,6144]{1,0:T(8,128)(2,1)}, bf16[16,6144]{1,0:T(8,128)(2,1)S(1)}, u32[]{:S(2)}, u32[]{:S(2)}) collective-permute-start(bf16[16,6144]{1,0:T(8,128)(2,1)} %pack.1), channel_id=1, source_target_pairs={{0,2},{1,5},{2,0},{3,7},{4,6},{5,1},{6,4},{7,3},{8,10},{9,13},{10,... | collective-permute-start | bytes 589832 | tf_op jit(solution)/shard_map/ppermute | solution.py:220
  4.7 15.0 %collective-permute-start.5 = (bf16[16,6144]{1,0:T(8,128)(2,1)}, bf16[16,6144]{1,0:T(8,128)(2,1)S(1)}, u32[]{:S(2)}, u32[]{:S(2)}) collective-permute-start(bf16[16,6144]{1,0:T(8,128)(2,1)} %pack.1), channel_id=1, source_target_pairs={{0,16},{1,17},{2,18},{3,19},{4,20},{5,21},{6,22},{7,23},{8,0},{9,1... | collective-permute-start | bytes 589832 | tf_op jit(solution)/shard_map/ppermute | solution.py:220
  7.3 10.2 %collective-permute-start.2 = (bf16[16,6144]{1,0:T(8,128)(2,1)}, bf16[16,6144]{1,0:T(8,128)(2,1)S(1)}, u32[]{:S(2)}, u32[]{:S(2)}) collective-permute-start(bf16[16,6144]{1,0:T(8,128)(2,1)} %pack.1), channel_id=1, source_target_pairs={{0,8},{1,9},{2,10},{3,11},{4,12},{5,13},{6,14},{7,15},{8,24},{9,25... | collective-permute-start | bytes 589832 | tf_op jit(solution)/shard_map/ppermute | solution.py:220
  9.5 25.2 %collective-permute-start.11 = (bf16[32,6144]{1,0:T(8,128)(2,1)S(1)}, bf16[32,6144]{1,0:T(8,128)(2,1)S(1)}, u32[]{:S(2)}, u32[]{:S(2)}) collective-permute-start(bf16[32,6144]{1,0:T(8,128)(2,1)S(1)} %pad_maximum_fusion.refs_0_), channel_id=1, source_target_pairs={{0,1},{1,0},{2,3},{3,2},{4,5},{5,4},{6,7},{7,6},{8,9},{9,8},{10,11... | collective-permute-start | bytes 1179656 | tf_op jit(solution)/shard_map/ppermute | solution.py:223
  9.6 26.4 %collective-permute-start.1 = (bf16[32,6144]{1,0:T(8,128)(2,1)S(1)}, bf16[32,6144]{1,0:T(8,128)(2,1)S(1)}, u32[]{:S(2)}, u32[]{:S(2)}) collective-permute-start(bf16[32,6144]{1,0:T(8,128)(2,1)S(1)} %pad_maximum_fusion.refs_0_), channel_id=1, source_target_pairs={{0,4},{1,3},{2,6},{3,1},{4,0},{5,7},{6,2},{7,5},{8,12},{9,11},{10,... | collective-permute-start | bytes 1179656 | tf_op jit(solution)/shard_map/ppermute | solution.py:220
  17.5 8.6 %collective-permute-start.8 = (bf16[16,6144]{1,0:T(8,128)(2,1)S(1)}, bf16[16,6144]{1,0:T(8,128)(2,1)S(1)}, u32[]{:S(2)}, u32[]{:S(2)}) collective-permute-start(bf16[16,6144]{1,0:T(8,128)(2,1)S(1)} %collective-permute-done.2), channel_id=1, source_target_pairs={{0,8},{1,9},{2,10},{3,11},{4,12},{5,13},{6,14},{7,15},{8,24},{9,25... | collective-permute-start | bytes 589832 | tf_op jit(solution)/shard_map/ppermute | solution.py:220
  18.2 8.5 %collective-permute-start.3 = (bf16[16,6144]{1,0:T(8,128)(2,1)S(1)}, bf16[16,6144]{1,0:T(8,128)(2,1)S(1)}, u32[]{:S(2)}, u32[]{:S(2)}) collective-permute-start(bf16[16,6144]{1,0:T(8,128)(2,1)S(1)} %collective-permute-done.2), channel_id=1, source_target_pairs={{0,2},{1,5},{2,0},{3,7},{4,6},{5,1},{6,4},{7,3},{8,10},{9,13},{10,... | collective-permute-start | bytes 589832 | tf_op jit(solution)/shard_map/ppermute | solution.py:220
  19.7 6.3 %collective-permute-start.6 = (bf16[16,6144]{1,0:T(8,128)(2,1)S(1)}, bf16[16,6144]{1,0:T(8,128)(2,1)S(1)}, u32[]{:S(2)}, u32[]{:S(2)}) collective-permute-start(bf16[16,6144]{1,0:T(8,128)(2,1)S(1)} %collective-permute-done.5), channel_id=1, source_target_pairs={{0,2},{1,5},{2,0},{3,7},{4,6},{5,1},{6,4},{7,3},{8,10},{9,13},{10,... | collective-permute-start | bytes 589832 | tf_op jit(solution)/shard_map/ppermute | solution.py:220
  26.0 10.9 %collective-permute-start.15 = (bf16[32,6144]{1,0:T(8,128)(2,1)S(1)}, bf16[32,6144]{1,0:T(8,128)(2,1)S(1)}, u32[]{:S(2)}, u32[]{:S(2)}) collective-permute-start(bf16[32,6144]{1,0:T(8,128)(2,1)S(1)} %constant_dynamic-update-slice_fusion.2.refs_4_), channel_id=1, source_target_pairs={{0,1},{1,0},{2,3},{3,2},{4,5},{5,4},{6,7},{7,6},{8,9},{9,8},{10,11... | collective-permute-start | bytes 1179656 | tf_op jit(solution)/shard_map/ppermute | solution.py:223
  26.1 10.8 %collective-permute-start.7 = (bf16[32,6144]{1,0:T(8,128)(2,1)S(1)}, bf16[32,6144]{1,0:T(8,128)(2,1)S(1)}, u32[]{:S(2)}, u32[]{:S(2)}) collective-permute-start(bf16[32,6144]{1,0:T(8,128)(2,1)S(1)} %constant_dynamic-update-slice_fusion.2.refs_4_), channel_id=1, source_target_pairs={{0,4},{1,3},{2,6},{3,1},{4,0},{5,7},{6,2},{7,5},{8,12},{9,11},{10,... | collective-permute-start | bytes 1179656 | tf_op jit(solution)/shard_map/ppermute | solution.py:220
  26.7 7.9 %collective-permute-start.9 = (bf16[16,6144]{1,0:T(8,128)(2,1)S(1)}, bf16[16,6144]{1,0:T(8,128)(2,1)S(1)}, u32[]{:S(2)}, u32[]{:S(2)}) collective-permute-start(bf16[16,6144]{1,0:T(8,128)(2,1)S(1)} %collective-permute-done.8), channel_id=1, source_target_pairs={{0,2},{1,5},{2,0},{3,7},{4,6},{5,1},{6,4},{7,3},{8,10},{9,13},{10,... | collective-permute-start | bytes 589832 | tf_op jit(solution)/shard_map/ppermute | solution.py:220
  34.5 2.9 %collective-permute-start.13 = (bf16[32,6144]{1,0:T(8,128)(2,1)S(1)}, bf16[32,6144]{1,0:T(8,128)(2,1)S(1)}, u32[]{:S(2)}, u32[]{:S(2)}) collective-permute-start(bf16[32,6144]{1,0:T(8,128)(2,1)S(1)} %constant_dynamic-update-slice_fusion.refs_2_), channel_id=1, source_target_pairs={{0,1},{1,0},{2,3},{3,2},{4,5},{5,4},{6,7},{7,6},{8,9},{9,8},{10,11... | collective-permute-start | bytes 1179656 | tf_op jit(solution)/shard_map/ppermute | solution.py:223
  34.8 7.9 %collective-permute-start.4 = (bf16[32,6144]{1,0:T(8,128)(2,1)S(1)}, bf16[32,6144]{1,0:T(8,128)(2,1)}, u32[]{:S(2)}, u32[]{:S(2)}) collective-permute-start(bf16[32,6144]{1,0:T(8,128)(2,1)S(1)} %constant_dynamic-update-slice_fusion.refs_2_), channel_id=1, source_target_pairs={{0,4},{1,3},{2,6},{3,1},{4,0},{5,7},{6,2},{7,5},{8,12},{9,11},{10,... | collective-permute-start | bytes 1179656 | tf_op jit(solution)/shard_map/ppermute | solution.py:220
  36.1 10.9 %collective-permute-start.10 = (bf16[32,6144]{1,0:T(8,128)(2,1)S(1)}, bf16[32,6144]{1,0:T(8,128)(2,1)}, u32[]{:S(2)}, u32[]{:S(2)}) collective-permute-start(bf16[32,6144]{1,0:T(8,128)(2,1)S(1)} %constant_dynamic-update-slice_fusion.4.refs_6_), channel_id=1, source_target_pairs={{0,4},{1,3},{2,6},{3,1},{4,0},{5,7},{6,2},{7,5},{8,12},{9,11},{10,... | collective-permute-start | bytes 1179656 | tf_op jit(solution)/shard_map/ppermute | solution.py:220
  36.9 14.1 %collective-permute-start.17 = (bf16[32,6144]{1,0:T(8,128)(2,1)S(1)}, bf16[32,6144]{1,0:T(8,128)(2,1)}, u32[]{:S(2)}, u32[]{:S(2)}) collective-permute-start(bf16[32,6144]{1,0:T(8,128)(2,1)S(1)} %constant_dynamic-update-slice_fusion.4.refs_6_), channel_id=1, source_target_pairs={{0,1},{1,0},{2,3},{3,2},{4,5},{5,4},{6,7},{7,6},{8,9},{9,8},{10,11... | collective-permute-start | bytes 1179656 | tf_op jit(solution)/shard_map/ppermute | solution.py:223
  36.9 14.1 %collective-permute-start.12 = (bf16[32,6144]{1,0:T(8,128)(2,1)S(1)}, bf16[32,6144]{1,0:T(8,128)(2,1)}, u32[]{:S(2)}, u32[]{:S(2)}) collective-permute-start(bf16[32,6144]{1,0:T(8,128)(2,1)S(1)} %collective-permute-done.1.refs_1_), channel_id=1, source_target_pairs={{0,1},{1,0},{2,3},{3,2},{4,5},{5,4},{6,7},{7,6},{8,9},{9,8},{10,11... | collective-permute-start | bytes 1179656 | tf_op jit(solution)/shard_map/ppermute | solution.py:223
  37.4 13.6 %collective-permute-start.16 = (bf16[32,6144]{1,0:T(8,128)(2,1)S(1)}, bf16[32,6144]{1,0:T(8,128)(2,1)}, u32[]{:S(2)}, u32[]{:S(2)}) collective-permute-start(bf16[32,6144]{1,0:T(8,128)(2,1)S(1)} %collective-permute-done.7.refs_5_), channel_id=1, source_target_pairs={{0,1},{1,0},{2,3},{3,2},{4,5},{5,4},{6,7},{7,6},{8,9},{9,8},{10,11... | collective-permute-start | bytes 1179656 | tf_op jit(solution)/shard_map/ppermute | solution.py:223
  42.7 8.3 %collective-permute-start.14 = (bf16[32,6144]{1,0:T(8,128)(2,1)}, bf16[32,6144]{1,0:T(8,128)(2,1)}, u32[]{:S(2)}, u32[]{:S(2)}) collective-permute-start(bf16[32,6144]{1,0:T(8,128)(2,1)} %collective-permute-done.4.refs_3_), channel_id=1, source_target_pairs={{0,1},{1,0},{2,3},{3,2},{4,5},{5,4},{6,7},{7,6},{8,9},{9,8},{10,11... | collective-permute-start | bytes 1179656 | tf_op jit(solution)/shard_map/ppermute | solution.py:223
  46.9 4.1 %collective-permute-start.18 = (bf16[32,6144]{1,0:T(8,128)(2,1)}, bf16[32,6144]{1,0:T(8,128)(2,1)}, u32[]{:S(2)}, u32[]{:S(2)}) collective-permute-start(bf16[32,6144]{1,0:T(8,128)(2,1)} %collective-permute-done.10.refs_7_), channel_id=1, source_target_pairs={{0,1},{1,0},{2,3},{3,2},{4,5},{5,4},{6,7},{7,6},{8,9},{9,8},{10,11... | collective-permute-start | bytes 1179656 | tf_op jit(solution)/shard_map/ppermute | solution.py:223
  51.0 0.7 copy-start
  64.2 3.0 %collective-permute-start.19 = (f32[256,1024]{1,0:T(8,128)}, f32[256,1024]{1,0:T(8,128)S(1)}, u32[]{:S(2)}, u32[]{:S(2)}) collective-permute-start(f32[256,1024]{1,0:T(8,128)} %get-tuple-element.8), channel_id=1, source_target_pairs={{0,1},{1,0},{2,3},{3,2},{4,5},{5,4},{6,7},{7,6},{8,9},{9,8},{10,11... | collective-permute-start | bytes 3145736 | tf_op jit(solution)/shard_map/ppermute | solution.py:223

commit v2 on v1

v2 whole, which is shorter than its diff:
```python
import functools

import jax
import jax.numpy as jnp
from jax import lax
from jax.experimental import pallas as pl
from jax.experimental.pallas import tpu as pltpu
from jax.sharding import PartitionSpec as P

DMAX = 192
LANES = 128
LOW = 64
ROWS = 16


def mask_slots(amplitudes, block_sizes):
    row_count = amplitudes.shape[0]
    nirrep = block_sizes.shape[0]
    blocked = amplitudes.reshape(row_count, nirrep, -1, DMAX)
    valid_cols = jnp.arange(DMAX, dtype=jnp.int32)[None, :] < block_sizes[:, None]
    masked = jnp.where(valid_cols[None, :, None, :], blocked, jnp.zeros((), amplitudes.dtype))
    return masked.reshape(row_count, -1)


def general(amplitudes, integrals, block_sizes):
    masked = mask_slots(amplitudes, block_sizes)
    gathered = lax.all_gather(masked, "out", axis=0, tiled=True)
    own_columns = lax.all_to_all(gathered, "con", split_axis=1, concat_axis=0, tiled=True)
    out_count = lax.axis_size("out")
    con_count = lax.axis_size("con")
    per_device = masked.shape[0]
    own_columns = own_columns.reshape(con_count, out_count, per_device, -1)
    own_columns = jnp.transpose(own_columns, (1, 0, 2, 3)).reshape(
        con_count * out_count * per_device, -1
    )
    partial_sums = lax.dot_general(
        own_columns, integrals, (((1,), (1,)), ((), ())), preferred_element_type=jnp.float32
    )
    ladder = lax.psum_scatter(partial_sums, "con", scatter_dimension=0, tiled=True)
    return ladder.astype(jnp.bfloat16)


def roll(x, shift):
    return pltpu.roll(x.astype(jnp.float32), shift, 1).astype(x.dtype)


def pack_kernel(nirrep, cw, sizes_ref, amp_ref, out_ref, both_ref):
    pairs = cw // 2
    rows = amp_ref.shape[0]
    lane = lax.broadcasted_iota(jnp.int32, (rows, LANES), 1)
    low = lane < LOW
    tiles = nirrep // 2
    extras = [[jnp.zeros((rows, LANES), amp_ref.dtype)] * tiles for _ in range(cw)]
    start = jnp.int32(0)
    for g in range(nirrep):
        extra = sizes_ref[g] - LOW
        inside = [
            (lane + k * LANES >= start) & (lane + k * LANES < start + extra) for k in range(tiles)
        ]
        shift = lax.rem(start, LANES)
        shift_half = lax.rem(start + LOW, LANES)
        for p in range(pairs):
            at = (g * pairs + p) * 3 * LANES
            one = amp_ref[:, at : at + LANES]
            two = amp_ref[:, at + LANES : at + 2 * LANES]
            three = amp_ref[:, at + 2 * LANES : at + 3 * LANES]
            to = (g * pairs + p) * LANES
            value = jnp.where(low, one, two)
            out_ref[:, to : to + LANES] = value
            both_ref[:rows, to : to + LANES] = value
            first = roll(jnp.where(low, two, one), shift_half)
            second = roll(three, shift)
            for k in range(tiles):
                extras[2 * p][k] = jnp.where(inside[k], first, extras[2 * p][k])
                extras[2 * p + 1][k] = jnp.where(inside[k], second, extras[2 * p + 1][k])
        start = start + extra
    base = nirrep * pairs * LANES
    for c in range(cw):
        for k in range(tiles):
            to = base + (c * tiles + k) * LANES
            out_ref[:, to : to + LANES] = extras[c][k]
            both_ref[:rows, to : to + LANES] = extras[c][k]


def pack(amplitudes, block_sizes, cw):
    nirrep = block_sizes.shape[0]
    rows, dtype = amplitudes.shape[0], amplitudes.dtype
    return pl.pallas_call(
        functools.partial(pack_kernel, nirrep, cw),
        out_shape=(
            jax.ShapeDtypeStruct((rows, nirrep * cw * LANES), dtype),
            jax.ShapeDtypeStruct((2 * rows, nirrep * cw * LANES), dtype),
        ),
        in_specs=[
            pl.BlockSpec(memory_space=pltpu.SMEM),
            pl.BlockSpec(memory_space=pltpu.VMEM),
        ],
        out_specs=(
            pl.BlockSpec(memory_space=pltpu.VMEM),
            pl.BlockSpec(memory_space=pltpu.VMEM),
        ),
        name="pack",
    )(block_sizes, amplitudes)


def unpack_rows(cw, nirrep, sizes_ref, con, packed, places, a_ref):
    pairs = cw // 2
    tiles = nirrep // 2
    own = nirrep // 2
    base = own * pairs * LANES
    rows = packed.shape[0]
    lane = lax.broadcasted_iota(jnp.int32, (rows, LANES), 1)
    low = lane < LOW
    zero = jnp.zeros((rows, LANES), packed.dtype)

    def one_irrep(g, start):
        extra = sizes_ref[con * own + g] - LOW
        tile = start // LANES
        shift = start - tile * LANES
        after = jnp.minimum(tile + 1, tiles - 1)
        tile = jnp.minimum(tile, tiles - 1)
        here = lane >= shift
        back = lax.rem(LANES - shift, LANES)
        back_half = lax.rem(LANES + LOW - shift, LANES)
        valid = lane < extra
        valid_half = jnp.where(low, lane + LOW, lane - LOW) < extra
        for p in range(pairs):
            at = pl.multiple_of((g * pairs + p) * LANES, LANES)
            both = packed[:, pl.ds(at, LANES)]
            halves = []
            for c in (2 * p, 2 * p + 1):
                one = packed[:, pl.ds(pl.multiple_of(base + (c * tiles + tile) * LANES, LANES), LANES)]
                two = packed[:, pl.ds(pl.multiple_of(base + (c * tiles + after) * LANES, LANES), LANES)]
                halves.append(jnp.where(here, one, two))
            first = jnp.where(valid_half, roll(halves[0], back_half), zero)
            second = jnp.where(valid, roll(halves[1], back), zero)
            to = pl.multiple_of((g * pairs + p) * 3 * LANES, LANES)
            values = (jnp.where(low, both, first), jnp.where(low, first, both), second)
            for i, place in enumerate(places):
                for t, value in enumerate(values):
                    a_ref[pl.ds(place, ROWS), pl.ds(to + t * LANES, LANES)] = value[
                        i * ROWS : (i + 1) * ROWS
                    ]
        return start + extra

    start = jnp.int32(0)
    for g in range(own):
        start = start + jnp.where(con > 0, sizes_ref[g] - LOW, 0)
    lax.fori_loop(0, own, one_irrep, start)


PLANE = 4 * 2 * ROWS
SMEM = pl.BlockSpec(memory_space=pltpu.SMEM)
VMEM = pl.BlockSpec(memory_space=pltpu.VMEM)
HBM = pl.BlockSpec(memory_space=pltpu.HBM)
ANY = pl.BlockSpec(memory_space=pl.ANY)


def contract_kernel(cw, nirrep, count, numbers_ref, *refs):
    sizes_ref = numbers_ref
    chip, con = numbers_ref[nirrep], numbers_ref[nirrep + 1]
    z, inside = chip // 4, chip % 4
    pieces = refs[:count]
    w_hbm, keep_ref, send_out, a_ref, w_ref, pieces_ref, send_ref, sems, w_sems, out_sems = refs[count:]
    block = w_ref.shape[0] // w_sems.shape[0]
    half = send_ref.shape[0]
    total = 2 * half
    depth = pieces[0].shape[0]
    per_plane = PLANE // depth
    width = w_ref.shape[1] // 3
    copies = []
    for n, piece in enumerate(pieces):
        rows = pl.ds(n % per_plane * depth, depth)
        to = pieces_ref.at[n // per_plane]
        copies += [
            pltpu.make_async_copy(
                piece.at[:, pl.ds(pl.multiple_of(con * width, LANES), width)],
                to.at[rows, pl.ds(0, width)],
                sems.at[n, 0],
            ),
            pltpu.make_async_copy(
                piece.at[:, pl.ds(2 * width, 2 * width)],
                to.at[rows, pl.ds(width, 2 * width)],
                sems.at[n, 1],
            ),
        ]
    w_copies = [
        pltpu.make_async_copy(
            w_hbm.at[pl.ds(n * block, block)], w_ref.at[pl.ds(n * block, block)], w_sems.at[n]
        )
        for n in range(w_sems.shape[0])
    ]
    for copy in copies + w_copies:
        copy.start()
    plane_before = jnp.where(z == 0, 2, jnp.where(z == 1, 0, jnp.where(z == 2, 3, 1)))
    planes = (z, plane_before, 3 - plane_before, 3 - z)

    @pl.loop(0, count // per_plane)
    def _(k):
        plane = jnp.where(
            k == 0, planes[0], jnp.where(k == 1, planes[1], jnp.where(k == 2, planes[2], planes[3]))
        )
        places = []
        for n in range(per_plane):
            core = con if n < 2 else 1 - con
            chips = (inside, inside ^ (1 + core)) if n % 2 == 0 else (inside ^ (2 - core), inside ^ 3)
            for c in chips:
                place = ((plane * 4 + c) * 2 + core) * ROWS + total - con * half
                places.append(pl.multiple_of(lax.rem(place, total), ROWS))
            rows = pieces_ref.at[k, pl.ds(n * depth, depth)]
            for i, part in enumerate((pl.ds(0, width), pl.ds(width, 2 * width))):
                at = rows.at[:, part]
                pltpu.make_async_copy(at, at, sems.at[k * per_plane + n, i]).wait()
        unpack_rows(cw, nirrep, sizes_ref, con, pieces_ref.at[k], places, a_ref)

    def send_copy(n):
        columns = pl.ds(pl.multiple_of(n * block, block), block)
        return pltpu.make_async_copy(
            send_ref.at[:, columns], send_out.at[:, columns], out_sems.at[n]
        )

    @pl.loop(0, w_sems.shape[0])
    def _(n):
        columns = pl.ds(pl.multiple_of(n * block, block), block)
        pltpu.make_async_copy(w_ref.at[columns], w_ref.at[columns], w_sems.at[n]).wait()
        sums = lax.dot_general(
            a_ref[...],
            w_ref[columns, :],
            (((1,), (1,)), ((), ())),
            preferred_element_type=jnp.float32,
        )
        keep_ref[:, columns] = sums[:half]
        send_ref[:, columns] = sums[half:]
        send_copy(n).start()

    @pl.loop(0, w_sems.shape[0])
    def _(n):
        send_copy(n).wait()


def contract(numbers, pieces, integrals, cw, nirrep):
    n, k = integrals.shape
    count = len(pieces)
    total = sum(piece.shape[0] for piece in pieces)
    half = jax.ShapeDtypeStruct((total // 2, n), jnp.float32)
    return pl.pallas_call(
        functools.partial(contract_kernel, cw, nirrep, count),
        out_shape=(pltpu.VMEM(half.shape, half.dtype), half),
        in_specs=[SMEM] + [ANY] * count + [HBM],
        out_specs=(VMEM, HBM),
        scratch_shapes=[
            pltpu.VMEM((total, k), jnp.bfloat16),
            pltpu.VMEM((n, k), jnp.bfloat16),
            pltpu.VMEM((total // PLANE, PLANE, k), jnp.bfloat16),
            pltpu.VMEM((total // 2, n), jnp.float32),
            pltpu.SemaphoreType.DMA((count, 2)),
            pltpu.SemaphoreType.DMA((n // 256,)),
            pltpu.SemaphoreType.DMA((n // 256,)),
        ],
        compiler_params=pltpu.CompilerParams(vmem_limit_bytes=44 * 2**20),
        name="contract",
    )(numbers, *pieces, integrals)


def add_kernel(keep_ref, got_ref, out, out_ref, sems):
    parts = sems.shape[0]
    rows = out_ref.shape[0] // parts

    def copy_out(n):
        part = pl.ds(pl.multiple_of(n * rows, rows), rows)
        return pltpu.make_async_copy(out_ref.at[part], out.at[part], sems.at[n])

    @pl.loop(0, parts)
    def _(n):
        part = pl.ds(pl.multiple_of(n * rows, rows), rows)
        out_ref[part] = (keep_ref[part] + got_ref[part]).astype(out_ref.dtype)
        copy_out(n).start()

    @pl.loop(0, parts)
    def _(n):
        copy_out(n).wait()


def add(keep, got):
    keep, got = (pltpu.with_memory_space_constraint(x, pltpu.VMEM) for x in (keep, got))
    return pl.pallas_call(
        add_kernel,
        out_shape=jax.ShapeDtypeStruct(keep.shape, jnp.bfloat16),
        in_specs=[VMEM, VMEM],
        out_specs=HBM,
        scratch_shapes=[pltpu.VMEM(keep.shape, jnp.bfloat16), pltpu.SemaphoreType.DMA((4,))],
        compiler_params=pltpu.CompilerParams(vmem_limit_bytes=4 * 2**20),
        name="add",
    )(keep, got)


RING = (1, 3, 0, 2)
RING_BACK = (2, 0, 3, 1)


def x_neighbour(o):
    return o ^ 1


def y_neighbour(o):
    return o ^ 2


def z_next(o):
    return RING[o // 4] * 4 + o % 4


def z_previous(o):
    return RING_BACK[o // 4] * 4 + o % 4


def after(value, *others):
    return lax.optimization_barrier((value, *others))[0]


STEPS = {
    "z1": (("own",), "next"),
    "f0": (("own",), "first"),
    "z3": (("own",), "previous"),
    "s0": (("own", "f0"), "second"),
    "z2": (("z1",), "next"),
    "f1": (("z1",), "first"),
    "f3": (("z3",), "first"),
    "s1": (("s0",), "next"),
    "f2": (("z2",), "first"),
    "s3": (("z3", "f3"), "second"),
    "s2": (("z2", "f2"), "second"),
}
AFTER = {"z3": ("f0",), "f3": ("s0",), "f2": ("f1",)}


def ladder_of_16(amplitudes, integrals, block_sizes):
    out_count, con_count = lax.axis_size("out"), lax.axis_size("con")
    ways = {
        "next": (z_next,),
        "previous": (z_previous,),
        "first": (x_neighbour, y_neighbour),
        "second": (y_neighbour, x_neighbour),
    }

    def move(value, way):
        by_core = ways[way]
        pairs = [
            (o * con_count + c, by_core[c % len(by_core)](o) * con_count + c)
            for o in range(out_count)
            for c in range(con_count)
        ]
        return lax.ppermute(value, ("out", "con"), pairs)

    def swap_cores(value):
        return lax.ppermute(value, "con", [(0, 1), (1, 0)])

    cw = integrals.shape[1] // (block_sizes.shape[0] // con_count * DMAX)
    here = jnp.stack([lax.axis_index("out"), lax.axis_index("con")]).astype(jnp.int32)
    numbers = jnp.concatenate([block_sizes, here])
    own, own_top = pack(amplitudes, block_sizes, cw)
    arrays = {("own",): own}

    def get(names):
        if names not in arrays:
            one, two = (arrays[(name,)] for name in names)
            if names[0] == "own":
                arrays[names] = lax.dynamic_update_slice(own_top, two, (ROWS, 0))
            else:
                arrays[names] = jnp.concatenate([one, two])
        return arrays[names]

    steps = dict(STEPS)
    while steps:
        name = next(
            n
            for n, (sent, _) in steps.items()
            if all((o,) in arrays for o in sent + AFTER.get(n, ()))
        )
        sent, way = steps.pop(name)
        others = [arrays[(o,)] for o in AFTER.get(name, ())]
        if name == "z2":
            others.append(numbers)
        value = get(sent)
        arrays[(name,)] = move(after(value, *others) if others else value, way)

    pieces = []
    for k, z in enumerate(("own", "z1", "z3", "z2")):
        f, s = f"f{z[1:]}" if k else "f0", f"s{z[1:]}" if k else "s0"
        plane = [get((z, f)), arrays[(s,)]]
        pieces += plane + [swap_cores(piece) for piece in plane]
    keep, send = contract(numbers, pieces, integrals, cw, block_sizes.shape[0])
    return add(keep, swap_cores(send))


def on_device(amplitudes, integrals, block_sizes):
    if amplitudes.shape[0] == ROWS and lax.axis_size("out") == 16:
        return ladder_of_16(amplitudes, integrals, block_sizes)
    return general(amplitudes, integrals, block_sizes)


def solution(mesh):
    in_specs = (P(("out", "con"), None), P("out", "con"), P())
    out_specs = P("con", "out")
    return jax.shard_map(
        on_device, mesh=mesh, in_specs=in_specs, out_specs=out_specs, check_vma=False
    )
```

time: 69.7 us -> 60.5 us (0.87)
  the two profiles are of different devices: /device:TPU:0 before, /device:TPU:25 now
where the time goes in v2:
time: 60.5 us; the launch traced here: 60.3 us
  starting transfers between devices  22.4 us (37%)
  waiting for transfers between devices  21.4 us (35%)
  Pallas kernels  13.9 us (23%)
  local copies, waits for them, and re-layouts  1.77 us (3%)
  other arithmetic  0.73 us (1%)
    ppermute x11, waiting for transfers between devices, move(): return lax.ppermute(value, ('out', 'con'), pairs)  17.2 us
    ppermute x11, starting transfers between devices, move(): return lax.ppermute(value, ('out', 'con'), pairs)  11.9 us
    pallas_call x1, Pallas kernels, contract(): pl.pallas_call(functools.partial(contract_kernel, cw, nirrep, count), out...  11.1 us
    ppermute x9, starting transfers between devices, swap_cores(): return lax.ppermute(value, 'con', [(0, 1), (1, 0)])  10.5 us
    ppermute x9, waiting for transfers between devices, swap_cores(): return lax.ppermute(value, 'con', [(0, 1), (1, 0)])  4.2 us
    pallas_call x1, Pallas kernels, pack(): pl.pallas_call(functools.partial(pack_kernel, nirrep, cw), out_shape=(jax...  1.94 us
  transfers between devices with their start and end apart: 20, of which 9 were waited for; matrix products, arithmetic and copies ran while one was open for 2% of the time, Pallas kernels for 0%

profile of v2, /device:TPU:25, one launch (start us, length us, event | category | flops | bytes accessed | tf_op | source)
XLA Modules:
  0.0 60.3 jit_solution(15350188273350645111)
XLA Ops:
  0.0 1.9 %pack.1 = (bf16[16,6144]{1,0:T(8,128)(2,1)}, bf16[32,6144]{1,0:T(8,128)(2,1)}) custom-call(s32[8]{0:T(128)} %sizes_ref.1, bf16[16,9216]{1,0:T(8,128)(2,1)} %amp_ref.1), custom_call_target="tpu_custom_call" | custom-call | tf_op jit(solution)/shard_map/pack/pallas_call | solution.py:88
  1.9 1.2 %collective-permute-start = (bf16[16,6144]{1,0:T(8,128)(2,1)}, bf16[16,6144]{1,0:T(8,128)(2,1)S(1)}, u32[]{:S(2)}, u32[]{:S(2)}) collective-permute-start(bf16[16,6144]{1,0:T(8,128)(2,1)} %get-tuple-element.15), channel_id=1, source_target_pairs={{0,2},{1,5},{2,0},{3,7},{4,6},{5,1},{6,4},{7,3},{8,10},{9,13},{10,... | collective-permute-start | bytes 589832 | tf_op jit(solution)/shard_map/ppermute | solution.py:353
  3.2 0.2 collective-permute-start.4
  3.4 0.7 %pad_add_fusion.numbers_ref = s32[10]{0:T(128)S(1)} fusion(s32[1]{0:T(128)} %bitcast.1, s32[1]{0:T(128)} %bitcast, s32[8]{0:T(128)} %sizes_ref.1), kind=kLoop, calls=%fused_computation.6 | loop fusion | flops 20 | bytes 80 | tf_op jit(solution)/shard_map/concatenate | solution.py:360
  4.1 2.9 %collective-permute-done = bf16[16,6144]{1,0:T(8,128)(2,1)S(1)} collective-permute-done((bf16[16,6144]{1,0:T(8,128)(2,1)}, bf16[16,6144]{1,0:T(8,128)(2,1)S(1)}, u32[]{:S(2)}, u32[]{:S(2)}) %collective-permute-start) | collective-permute-done | bytes 196640 | tf_op jit(solution)/shard_map/ppermute | solution.py:353
  7.0 0.7 %constant_dynamic-update-slice_fusion.6.refs_0_ = bf16[32,6144]{1,0:T(8,128)(2,1)} fusion(bf16[32,6144]{1,0:T(8,128)(2,1)} %get-tuple-element.13, bf16[16,6144]{1,0:T(8,128)(2,1)S(1)} %collective-permute-done), kind=kLoop, calls=%fused_computation.7 | loop fusion | bytes 393216 | tf_op jit(solution)/shard_map/dynamic_update_slice | solution.py:368
  7.7 1.5 %collective-permute-start.2 = (bf16[32,6144]{1,0:T(8,128)(2,1)}, bf16[32,6144]{1,0:T(8,128)(2,1)S(1)}, u32[]{:S(2)}, u32[]{:S(2)}) collective-permute-start(bf16[32,6144]{1,0:T(8,128)(2,1)} %constant_dynamic-update-slice_fusion.6.refs_0_), channel_id=1, source_target_pairs={{0,1},{1,0},{2,3},{3,2},{4,5},{5,4},{6,7},{7,6},{8,9},{9,8},{10,11... | collective-permute-start | bytes 1179656 | tf_op jit(solution)/shard_map/ppermute | solution.py:356
  9.2 1.2 %collective-permute-start.1 = (bf16[32,6144]{1,0:T(8,128)(2,1)}, bf16[32,6144]{1,0:T(8,128)(2,1)S(1)}, u32[]{:S(2)}, u32[]{:S(2)}) collective-permute-start(bf16[32,6144]{1,0:T(8,128)(2,1)} %constant_dynamic-update-slice_fusion.6.refs_0_), channel_id=1, source_target_pairs={{0,4},{1,3},{2,6},{3,1},{4,0},{5,7},{6,2},{7,5},{8,12},{9,11},{10,... | collective-permute-start | bytes 1179656 | tf_op jit(solution)/shard_map/ppermute | solution.py:353
  10.4 0.2 collective-permute-start.14
  10.6 2.2 %collective-permute-start.9 = (bf16[16,6144]{1,0:T(8,128)(2,1)}, bf16[16,6144]{1,0:T(8,128)(2,1)S(1)}, u32[]{:S(2)}, u32[]{:S(2)}) collective-permute-start(bf16[16,6144]{1,0:T(8,128)(2,1)} %get-tuple-element.15), channel_id=1, source_target_pairs={{0,16},{1,17},{2,18},{3,19},{4,20},{5,21},{6,22},{7,23},{8,0},{9,1... | collective-permute-start | bytes 589832 | tf_op jit(solution)/shard_map/ppermute | solution.py:353
  12.8 1.2 %collective-permute-start.5 = (bf16[16,6144]{1,0:T(8,128)(2,1)S(1)}, bf16[16,6144]{1,0:T(8,128)(2,1)S(1)}, u32[]{:S(2)}, u32[]{:S(2)}) collective-permute-start(bf16[16,6144]{1,0:T(8,128)(2,1)S(1)} %collective-permute-done.4), channel_id=1, source_target_pairs={{0,2},{1,5},{2,0},{3,7},{4,6},{5,1},{6,4},{7,3},{8,10},{9,13},{10,... | collective-permute-start | bytes 589832 | tf_op jit(solution)/shard_map/ppermute | solution.py:353
  14.0 3.0 %collective-permute-done.14 = bf16[16,6144]{1,0:T(8,128)(2,1)S(1)} collective-permute-done((bf16[16,6144]{1,0:T(8,128)(2,1)S(1)}, bf16[16,6144]{1,0:T(8,128)(2,1)S(1)}, u32[]{:S(2)}, u32[]{:S(2)}) %collective-permute-start.14) | collective-permute-done | bytes 196640 | tf_op jit(solution)/shard_map/ppermute | solution.py:353
  17.0 1.8 %collective-permute-done.5 = bf16[16,6144]{1,0:T(8,128)(2,1)S(1)} collective-permute-done((bf16[16,6144]{1,0:T(8,128)(2,1)S(1)}, bf16[16,6144]{1,0:T(8,128)(2,1)S(1)}, u32[]{:S(2)}, u32[]{:S(2)}) %collective-permute-start.5) | collective-permute-done | bytes 196640 | tf_op jit(solution)/shard_map/ppermute | solution.py:353
  18.9 3.9 %collective-permute-start.15 = (bf16[16,6144]{1,0:T(8,128)(2,1)S(1)}, bf16[16,6144]{1,0:T(8,128)(2,1)S(1)}, u32[]{:S(2)}, u32[]{:S(2)}) collective-permute-start(bf16[16,6144]{1,0:T(8,128)(2,1)S(1)} %collective-permute-done.14), channel_id=1, source_target_pairs={{0,2},{1,5},{2,0},{3,7},{4,6},{5,1},{6,4},{7,3},{8,10},{9,13},{10,... | collective-permute-start | bytes 589832 | tf_op jit(solution)/shard_map/ppermute | solution.py:353
  22.8 2.1 %collective-permute-start.7 = (bf16[32,6144]{1,0:T(8,128)(2,1)S(1)}, bf16[32,6144]{1,0:T(8,128)(2,1)S(1)}, u32[]{:S(2)}, u32[]{:S(2)}) collective-permute-start(bf16[32,6144]{1,0:T(8,128)(2,1)S(1)} %constant_dynamic-update-slice_fusion.refs_4_), channel_id=1, source_target_pairs={{0,1},{1,0},{2,3},{3,2},{4,5},{5,4},{6,7},{7,6},{8,9},{9,8},{10,11... | collective-permute-start | bytes 1179656 | tf_op jit(solution)/shard_map/ppermute | solution.py:356
  25.0 0.1 collective-permute-start.10
  25.1 1.1 %collective-permute-done.15 = bf16[16,6144]{1,0:T(8,128)(2,1)S(1)} collective-permute-done((bf16[16,6144]{1,0:T(8,128)(2,1)S(1)}, bf16[16,6144]{1,0:T(8,128)(2,1)S(1)}, u32[]{:S(2)}, u32[]{:S(2)}) %collective-permute-start.15) | collective-permute-done | bytes 196640 | tf_op jit(solution)/shard_map/ppermute | solution.py:353
  26.2 2.5 %collective-permute-start.17 = (bf16[32,6144]{1,0:T(8,128)(2,1)S(1)}, bf16[32,6144]{1,0:T(8,128)(2,1)S(1)}, u32[]{:S(2)}, u32[]{:S(2)}) collective-permute-start(bf16[32,6144]{1,0:T(8,128)(2,1)S(1)} %constant_dynamic-update-slice_fusion.4.refs_12_), channel_id=1, source_target_pairs={{0,1},{1,0},{2,3},{3,2},{4,5},{5,4},{6,7},{7,6},{8,9},{9,8},{10,11... | collective-permute-start | bytes 1179656 | tf_op jit(solution)/shard_map/ppermute | solution.py:356
  28.6 1.7 %collective-permute-start.16 = (bf16[32,6144]{1,0:T(8,128)(2,1)S(1)}, bf16[32,6144]{1,0:T(8,128)(2,1)S(1)}, u32[]{:S(2)}, u32[]{:S(2)}) collective-permute-start(bf16[32,6144]{1,0:T(8,128)(2,1)S(1)} %constant_dynamic-update-slice_fusion.4.refs_12_), channel_id=1, source_target_pairs={{0,4},{1,3},{2,6},{3,1},{4,0},{5,7},{6,2},{7,5},{8,12},{9,11},{10,... | collective-permute-start | bytes 1179656 | tf_op jit(solution)/shard_map/ppermute | solution.py:353
  30.3 0.1 collective-permute-start.11
  30.4 1.9 %collective-permute-start.3 = (bf16[32,6144]{1,0:T(8,128)(2,1)S(1)}, bf16[32,6144]{1,0:T(8,128)(2,1)S(1)}, u32[]{:S(2)}, u32[]{:S(2)}) collective-permute-start(bf16[32,6144]{1,0:T(8,128)(2,1)S(1)} %collective-permute-done.1.refs_1_), channel_id=1, source_target_pairs={{0,1},{1,0},{2,3},{3,2},{4,5},{5,4},{6,7},{7,6},{8,9},{9,8},{10,11... | collective-permute-start | bytes 1179656 | tf_op jit(solution)/shard_map/ppermute | solution.py:356
  32.4 3.4 %collective-permute-done.16.refs_13_ = bf16[32,6144]{1,0:T(8,128)(2,1)S(1)} collective-permute-done((bf16[32,6144]{1,0:T(8,128)(2,1)S(1)}, bf16[32,6144]{1,0:T(8,128)(2,1)S(1)}, u32[]{:S(2)}, u32[]{:S(2)}) %collective-permute-start.16) | collective-permute-done | bytes 393248 | tf_op jit(solution)/shard_map/ppermute | solution.py:353
  35.8 0.7 %collective-permute-start.18 = (bf16[32,6144]{1,0:T(8,128)(2,1)S(1)}, bf16[32,6144]{1,0:T(8,128)(2,1)S(1)}, u32[]{:S(2)}, u32[]{:S(2)}) collective-permute-start(bf16[32,6144]{1,0:T(8,128)(2,1)S(1)} %collective-permute-done.16.refs_13_), channel_id=1, source_target_pairs={{0,1},{1,0},{2,3},{3,2},{4,5},{5,4},{6,7},{7,6},{8,9},{9,8},{10,11... | collective-permute-start | bytes 1179656 | tf_op jit(solution)/shard_map/ppermute | solution.py:356
  36.5 5.0 %collective-permute-done.6.refs_5_ = bf16[32,6144]{1,0:T(8,128)(2,1)S(1)} collective-permute-done((bf16[32,6144]{1,0:T(8,128)(2,1)S(1)}, bf16[32,6144]{1,0:T(8,128)(2,1)S(1)}, u32[]{:S(2)}, u32[]{:S(2)}) %collective-permute-start.6) | collective-permute-done | bytes 393248 | tf_op jit(solution)/shard_map/ppermute | solution.py:353
  41.5 1.3 %collective-permute-start.8 = (bf16[32,6144]{1,0:T(8,128)(2,1)S(1)}, bf16[32,6144]{1,0:T(8,128)(2,1)S(1)}, u32[]{:S(2)}, u32[]{:S(2)}) collective-permute-start(bf16[32,6144]{1,0:T(8,128)(2,1)S(1)} %collective-permute-done.6.refs_5_), channel_id=1, source_target_pairs={{0,1},{1,0},{2,3},{3,2},{4,5},{5,4},{6,7},{7,6},{8,9},{9,8},{10,11... | collective-permute-start | bytes 1179656 | tf_op jit(solution)/shard_map/ppermute | solution.py:356
  42.8 1.3 %collective-permute-done.8.refs_7_ = bf16[32,6144]{1,0:T(8,128)(2,1)S(1)} collective-permute-done((bf16[32,6144]{1,0:T(8,128)(2,1)S(1)}, bf16[32,6144]{1,0:T(8,128)(2,1)S(1)}, u32[]{:S(2)}, u32[]{:S(2)}) %collective-permute-start.8) | collective-permute-done | bytes 393248 | tf_op jit(solution)/shard_map/ppermute | solution.py:356
  44.1 0.6 collective-permute-done.13.refs_11_
  44.7 1.0 %copy-done = bf16[32,6144]{1,0:T(8,128)(2,1)S(1)} copy-done((bf16[32,6144]{1,0:T(8,128)(2,1)S(1)}, bf16[32,6144]{1,0:T(8,128)(2,1)}, u32[]{:S(2)}) %copy-start) | copy-done | bytes 393240
  45.6 11.1 %contract.1 = (f32[256,1024]{1,0:T(8,128)S(1)}, f32[256,1024]{1,0:T(8,128)S(1)}) custom-call(s32[10]{0:T(128)S(1)} %pad_add_fusion.numbers_ref, bf16[32,6144]{1,0:T(8,128)(2,1)S(1)} %copy-done, bf16[32,6144]{1,0:T(8,128)(2,1)S(1)} %collective-permute-done.1.refs_1_, bf16[32,6144]{1,0:T(8,128)(2,1)S(1)} %collective-permute-done.2.refs_2_, ...), custom_call_target="tpu_custom_call" | custom-call | tf_op jit(solution)/shard_map/contract/pallas_call | solution.py:246
  56.8 0.4 collective-permute-start.19
  57.2 2.3 %collective-permute-done.19.got_ref = f32[256,1024]{1,0:T(8,128)S(1)} collective-permute-done((f32[256,1024]{1,0:T(8,128)S(1)}, f32[256,1024]{1,0:T(8,128)S(1)}, u32[]{:S(2)}, u32[]{:S(2)}) %collective-permute-start.19) | collective-permute-done | bytes 1048608 | tf_op jit(solution)/shard_map/ppermute | solution.py:356
  59.5 0.8 %add.5 = bf16[256,1024]{1,0:T(8,128)(2,1)} custom-call(f32[256,1024]{1,0:T(8,128)S(1)} %get-tuple-element.19.keep_ref, f32[256,1024]{1,0:T(8,128)S(1)} %collective-permute-done.19.got_ref), custom_call_target="tpu_custom_call" | custom-call | tf_op jit(solution)/shard_map/add/pallas_call | solution.py:286
  (21 shorter events, 0.2 us)
Async XLA Ops:
  1.9 5.0 %collective-permute-start = (bf16[16,6144]{1,0:T(8,128)(2,1)}, bf16[16,6144]{1,0:T(8,128)(2,1)S(1)}, u32[]{:S(2)}, u32[]{:S(2)}) collective-permute-start(bf16[16,6144]{1,0:T(8,128)(2,1)} %get-tuple-element.15), channel_id=1, source_target_pairs={{0,2},{1,5},{2,0},{3,7},{4,6},{5,1},{6,4},{7,3},{8,10},{9,13},{10,... | collective-permute-start | bytes 589832 | tf_op jit(solution)/shard_map/ppermute | solution.py:353
  3.2 7.2 %collective-permute-start.4 = (bf16[16,6144]{1,0:T(8,128)(2,1)}, bf16[16,6144]{1,0:T(8,128)(2,1)S(1)}, u32[]{:S(2)}, u32[]{:S(2)}) collective-permute-start(bf16[16,6144]{1,0:T(8,128)(2,1)} %get-tuple-element.15), channel_id=1, source_target_pairs={{0,8},{1,9},{2,10},{3,11},{4,12},{5,13},{6,14},{7,15},{8,24},{9,25... | collective-permute-start | bytes 589832 | tf_op jit(solution)/shard_map/ppermute | solution.py:353
  7.7 22.7 %collective-permute-start.2 = (bf16[32,6144]{1,0:T(8,128)(2,1)}, bf16[32,6144]{1,0:T(8,128)(2,1)S(1)}, u32[]{:S(2)}, u32[]{:S(2)}) collective-permute-start(bf16[32,6144]{1,0:T(8,128)(2,1)} %constant_dynamic-update-slice_fusion.6.refs_0_), channel_id=1, source_target_pairs={{0,1},{1,0},{2,3},{3,2},{4,5},{5,4},{6,7},{7,6},{8,9},{9,8},{10,11... | collective-permute-start | bytes 1179656 | tf_op jit(solution)/shard_map/ppermute | solution.py:356
  9.2 15.8 %collective-permute-start.1 = (bf16[32,6144]{1,0:T(8,128)(2,1)}, bf16[32,6144]{1,0:T(8,128)(2,1)S(1)}, u32[]{:S(2)}, u32[]{:S(2)}) collective-permute-start(bf16[32,6144]{1,0:T(8,128)(2,1)} %constant_dynamic-update-slice_fusion.6.refs_0_), channel_id=1, source_target_pairs={{0,4},{1,3},{2,6},{3,1},{4,0},{5,7},{6,2},{7,5},{8,12},{9,11},{10,... | collective-permute-start | bytes 1179656 | tf_op jit(solution)/shard_map/ppermute | solution.py:353
  10.4 6.6 %collective-permute-start.14 = (bf16[16,6144]{1,0:T(8,128)(2,1)S(1)}, bf16[16,6144]{1,0:T(8,128)(2,1)S(1)}, u32[]{:S(2)}, u32[]{:S(2)}) collective-permute-start(bf16[16,6144]{1,0:T(8,128)(2,1)S(1)} %collective-permute-done.4), channel_id=1, source_target_pairs={{0,8},{1,9},{2,10},{3,11},{4,12},{5,13},{6,14},{7,15},{8,24},{9,25... | collective-permute-start | bytes 589832 | tf_op jit(solution)/shard_map/ppermute | solution.py:353
  10.6 14.4 %collective-permute-start.9 = (bf16[16,6144]{1,0:T(8,128)(2,1)}, bf16[16,6144]{1,0:T(8,128)(2,1)S(1)}, u32[]{:S(2)}, u32[]{:S(2)}) collective-permute-start(bf16[16,6144]{1,0:T(8,128)(2,1)} %get-tuple-element.15), channel_id=1, source_target_pairs={{0,16},{1,17},{2,18},{3,19},{4,20},{5,21},{6,22},{7,23},{8,0},{9,1... | collective-permute-start | bytes 589832 | tf_op jit(solution)/shard_map/ppermute | solution.py:353
  12.8 6.1 %collective-permute-start.5 = (bf16[16,6144]{1,0:T(8,128)(2,1)S(1)}, bf16[16,6144]{1,0:T(8,128)(2,1)S(1)}, u32[]{:S(2)}, u32[]{:S(2)}) collective-permute-start(bf16[16,6144]{1,0:T(8,128)(2,1)S(1)} %collective-permute-done.4), channel_id=1, source_target_pairs={{0,2},{1,5},{2,0},{3,7},{4,6},{5,1},{6,4},{7,3},{8,10},{9,13},{10,... | collective-permute-start | bytes 589832 | tf_op jit(solution)/shard_map/ppermute | solution.py:353
  18.9 7.3 %collective-permute-start.15 = (bf16[16,6144]{1,0:T(8,128)(2,1)S(1)}, bf16[16,6144]{1,0:T(8,128)(2,1)S(1)}, u32[]{:S(2)}, u32[]{:S(2)}) collective-permute-start(bf16[16,6144]{1,0:T(8,128)(2,1)S(1)} %collective-permute-done.14), channel_id=1, source_target_pairs={{0,2},{1,5},{2,0},{3,7},{4,6},{5,1},{6,4},{7,3},{8,10},{9,13},{10,... | collective-permute-start | bytes 589832 | tf_op jit(solution)/shard_map/ppermute | solution.py:353
  22.8 7.6 %collective-permute-start.7 = (bf16[32,6144]{1,0:T(8,128)(2,1)S(1)}, bf16[32,6144]{1,0:T(8,128)(2,1)S(1)}, u32[]{:S(2)}, u32[]{:S(2)}) collective-permute-start(bf16[32,6144]{1,0:T(8,128)(2,1)S(1)} %constant_dynamic-update-slice_fusion.refs_4_), channel_id=1, source_target_pairs={{0,1},{1,0},{2,3},{3,2},{4,5},{5,4},{6,7},{7,6},{8,9},{9,8},{10,11... | collective-permute-start | bytes 1179656 | tf_op jit(solution)/shard_map/ppermute | solution.py:356
  25.0 5.3 %collective-permute-start.10 = (bf16[16,6144]{1,0:T(8,128)(2,1)S(1)}, bf16[16,6144]{1,0:T(8,128)(2,1)S(1)}, u32[]{:S(2)}, u32[]{:S(2)}) collective-permute-start(bf16[16,6144]{1,0:T(8,128)(2,1)S(1)} %collective-permute-done.9), channel_id=1, source_target_pairs={{0,2},{1,5},{2,0},{3,7},{4,6},{5,1},{6,4},{7,3},{8,10},{9,13},{10,... | collective-permute-start | bytes 589832 | tf_op jit(solution)/shard_map/ppermute | solution.py:353
  26.2 6.1 %collective-permute-start.17 = (bf16[32,6144]{1,0:T(8,128)(2,1)S(1)}, bf16[32,6144]{1,0:T(8,128)(2,1)S(1)}, u32[]{:S(2)}, u32[]{:S(2)}) collective-permute-start(bf16[32,6144]{1,0:T(8,128)(2,1)S(1)} %constant_dynamic-update-slice_fusion.4.refs_12_), channel_id=1, source_target_pairs={{0,1},{1,0},{2,3},{3,2},{4,5},{5,4},{6,7},{7,6},{8,9},{9,8},{10,11... | collective-permute-start | bytes 1179656 | tf_op jit(solution)/shard_map/ppermute | solution.py:356
  28.6 7.1 %collective-permute-start.16 = (bf16[32,6144]{1,0:T(8,128)(2,1)S(1)}, bf16[32,6144]{1,0:T(8,128)(2,1)S(1)}, u32[]{:S(2)}, u32[]{:S(2)}) collective-permute-start(bf16[32,6144]{1,0:T(8,128)(2,1)S(1)} %constant_dynamic-update-slice_fusion.4.refs_12_), channel_id=1, source_target_pairs={{0,4},{1,3},{2,6},{3,1},{4,0},{5,7},{6,2},{7,5},{8,12},{9,11},{10,... | collective-permute-start | bytes 1179656 | tf_op jit(solution)/shard_map/ppermute | solution.py:353
  30.3 11.2 %collective-permute-start.6 = (bf16[32,6144]{1,0:T(8,128)(2,1)S(1)}, bf16[32,6144]{1,0:T(8,128)(2,1)S(1)}, u32[]{:S(2)}, u32[]{:S(2)}) collective-permute-start(bf16[32,6144]{1,0:T(8,128)(2,1)S(1)} %collective-permute-done.1.refs_1_), channel_id=1, source_target_pairs={{0,8},{1,9},{2,10},{3,11},{4,12},{5,13},{6,14},{7,15},{8,24},{9,25... | collective-permute-start | bytes 1179656 | tf_op jit(solution)/shard_map/ppermute | solution.py:353
  30.3 12.4 %collective-permute-start.11 = (bf16[32,6144]{1,0:T(8,128)(2,1)S(1)}, bf16[32,6144]{1,0:T(8,128)(2,1)S(1)}, u32[]{:S(2)}, u32[]{:S(2)}) collective-permute-start(bf16[32,6144]{1,0:T(8,128)(2,1)S(1)} %constant_dynamic-update-slice_fusion.2.refs_8_), channel_id=1, source_target_pairs={{0,4},{1,3},{2,6},{3,1},{4,0},{5,7},{6,2},{7,5},{8,12},{9,11},{10,... | collective-permute-start | bytes 1179656 | tf_op jit(solution)/shard_map/ppermute | solution.py:353
  30.4 12.3 %collective-permute-start.3 = (bf16[32,6144]{1,0:T(8,128)(2,1)S(1)}, bf16[32,6144]{1,0:T(8,128)(2,1)S(1)}, u32[]{:S(2)}, u32[]{:S(2)}) collective-permute-start(bf16[32,6144]{1,0:T(8,128)(2,1)S(1)} %collective-permute-done.1.refs_1_), channel_id=1, source_target_pairs={{0,1},{1,0},{2,3},{3,2},{4,5},{5,4},{6,7},{7,6},{8,9},{9,8},{10,11... | collective-permute-start | bytes 1179656 | tf_op jit(solution)/shard_map/ppermute | solution.py:356
  32.3 10.5 %collective-permute-start.12 = (bf16[32,6144]{1,0:T(8,128)(2,1)S(1)}, bf16[32,6144]{1,0:T(8,128)(2,1)S(1)}, u32[]{:S(2)}, u32[]{:S(2)}) collective-permute-start(bf16[32,6144]{1,0:T(8,128)(2,1)S(1)} %constant_dynamic-update-slice_fusion.2.refs_8_), channel_id=1, source_target_pairs={{0,1},{1,0},{2,3},{3,2},{4,5},{5,4},{6,7},{7,6},{8,9},{9,8},{10,11... | collective-permute-start | bytes 1179656 | tf_op jit(solution)/shard_map/ppermute | solution.py:356
  35.8 7.0 %collective-permute-start.18 = (bf16[32,6144]{1,0:T(8,128)(2,1)S(1)}, bf16[32,6144]{1,0:T(8,128)(2,1)S(1)}, u32[]{:S(2)}, u32[]{:S(2)}) collective-permute-start(bf16[32,6144]{1,0:T(8,128)(2,1)S(1)} %collective-permute-done.16.refs_13_), channel_id=1, source_target_pairs={{0,1},{1,0},{2,3},{3,2},{4,5},{5,4},{6,7},{7,6},{8,9},{9,8},{10,11... | collective-permute-start | bytes 1179656 | tf_op jit(solution)/shard_map/ppermute | solution.py:356
  41.5 2.6 %collective-permute-start.8 = (bf16[32,6144]{1,0:T(8,128)(2,1)S(1)}, bf16[32,6144]{1,0:T(8,128)(2,1)S(1)}, u32[]{:S(2)}, u32[]{:S(2)}) collective-permute-start(bf16[32,6144]{1,0:T(8,128)(2,1)S(1)} %collective-permute-done.6.refs_5_), channel_id=1, source_target_pairs={{0,1},{1,0},{2,3},{3,2},{4,5},{5,4},{6,7},{7,6},{8,9},{9,8},{10,11... | collective-permute-start | bytes 1179656 | tf_op jit(solution)/shard_map/ppermute | solution.py:356
  42.7 1.9 %collective-permute-start.13 = (bf16[32,6144]{1,0:T(8,128)(2,1)S(1)}, bf16[32,6144]{1,0:T(8,128)(2,1)S(1)}, u32[]{:S(2)}, u32[]{:S(2)}) collective-permute-start(bf16[32,6144]{1,0:T(8,128)(2,1)S(1)} %collective-permute-done.11.refs_9_), channel_id=1, source_target_pairs={{0,1},{1,0},{2,3},{3,2},{4,5},{5,4},{6,7},{7,6},{8,9},{9,8},{10,11... | collective-permute-start | bytes 1179656 | tf_op jit(solution)/shard_map/ppermute | solution.py:356
  44.7 1.0 %copy-start = (bf16[32,6144]{1,0:T(8,128)(2,1)S(1)}, bf16[32,6144]{1,0:T(8,128)(2,1)}, u32[]{:S(2)}) copy-start(bf16[32,6144]{1,0:T(8,128)(2,1)} %constant_dynamic-update-slice_fusion.6.refs_0_) | copy-start | bytes 1179652
  56.8 2.7 %collective-permute-start.19 = (f32[256,1024]{1,0:T(8,128)S(1)}, f32[256,1024]{1,0:T(8,128)S(1)}, u32[]{:S(2)}, u32[]{:S(2)}) collective-permute-start(f32[256,1024]{1,0:T(8,128)S(1)} %get-tuple-element.20), channel_id=1, source_target_pairs={{0,1},{1,0},{2,3},{3,2},{4,5},{5,4},{6,7},{7,6},{8,9},{9,8},{10,11... | collective-permute-start | bytes 3145736 | tf_op jit(solution)/shard_map/ppermute | solution.py:356

commit v3 on v2

--- a/solution.py
+++ b/solution.py
@@ -156,62 +156,115 @@
 ANY = pl.BlockSpec(memory_space=pl.ANY)
 
 
-def contract_kernel(cw, nirrep, count, numbers_ref, *refs):
-    sizes_ref = numbers_ref
-    chip, con = numbers_ref[nirrep], numbers_ref[nirrep + 1]
-    z, inside = chip // 4, chip % 4
-    pieces = refs[:count]
-    w_hbm, keep_ref, send_out, a_ref, w_ref, pieces_ref, send_ref, sems, w_sems, out_sems = refs[count:]
-    block = w_ref.shape[0] // w_sems.shape[0]
-    half = send_ref.shape[0]
-    total = 2 * half
+def fetch(con, width, pieces, packed_ref, sems):
     depth = pieces[0].shape[0]
-    per_plane = PLANE // depth
-    width = w_ref.shape[1] // 3
     copies = []
     for n, piece in enumerate(pieces):
-        rows = pl.ds(n % per_plane * depth, depth)
-        to = pieces_ref.at[n // per_plane]
+        rows = pl.ds(n * depth, depth)
         copies += [
             pltpu.make_async_copy(
                 piece.at[:, pl.ds(pl.multiple_of(con * width, LANES), width)],
-                to.at[rows, pl.ds(0, width)],
+                packed_ref.at[rows, pl.ds(0, width)],
                 sems.at[n, 0],
             ),
             pltpu.make_async_copy(
                 piece.at[:, pl.ds(2 * width, 2 * width)],
-                to.at[rows, pl.ds(width, 2 * width)],
+                packed_ref.at[rows, pl.ds(width, 2 * width)],
                 sems.at[n, 1],
             ),
         ]
+    return copies
+
+
+def places_in_plane(chip, con):
+    inside = chip % 4
+    places = []
+    for core in (con, 1 - con):
+        for c in (inside, inside ^ (1 + core), inside ^ (2 - core), inside ^ 3):
+            places.append((c * 2 + core) * ROWS)
+    return places
+
+
+def unpack_kernel(cw, nirrep, numbers_ref, *refs):
+    pieces = refs[:4]
+    out, a_ref, packed_ref, sems, out_sem = refs[4:]
+    chip, con = numbers_ref[nirrep], numbers_ref[nirrep + 1]
+    copies = fetch(con, a_ref.shape[1] // 3, pieces, packed_ref, sems)
+    for copy in copies:
+        copy.start()
+    for copy in copies:
+        copy.wait()
+    places = [pl.multiple_of(place, ROWS) for place in places_in_plane(chip, con)]
+    unpack_rows(cw, nirrep, numbers_ref, con, packed_ref, places, a_ref)
+    copy = pltpu.make_async_copy(a_ref, out, out_sem)
+    copy.start()
+    copy.wait()
+
+
+def unpack(numbers, pieces, cw, nirrep, flops):
+    k = nirrep // 2 * cw * DMAX
+    return pl.pallas_call(
+        functools.partial(unpack_kernel, cw, nirrep),
+        out_shape=jax.ShapeDtypeStruct((PLANE, k), jnp.bfloat16),
+        in_specs=[SMEM] + [ANY] * 4,
+        out_specs=HBM,
+        scratch_shapes=[
+            pltpu.VMEM((PLANE, k), jnp.bfloat16),
+            pltpu.VMEM((PLANE, k), jnp.bfloat16),
+            pltpu.SemaphoreType.DMA((4, 2)),
+            pltpu.SemaphoreType.DMA,
+        ],
+        compiler_params=pltpu.CompilerParams(vmem_limit_bytes=44 * 2**20),
+        cost_estimate=pl.CostEstimate(flops=flops, bytes_accessed=4 * PLANE * k, transcendentals=0),
+        name="unpack",
+    )(numbers, *pieces)
+
+
+def contract_kernel(cw, nirrep, ready, packed, numbers_ref, *refs):
+    chip, con = numbers_ref[nirrep], numbers_ref[nirrep + 1]
+    z = chip // 4
+    rows_ready, pieces = refs[: len(ready)], refs[len(ready) : len(ready) + 4 * len(packed)]
+    refs = refs[len(ready) + 4 * len(packed) :]
+    w_hbm, keep_ref, send_out, a_ref, w_ref, packed_ref, send_ref, sems, r_sems, w_sems, out_sems = refs
+    block = w_ref.shape[0] // w_sems.shape[0]
+    half = send_ref.shape[0]
+    total = 2 * half
+    width = w_ref.shape[1] // 3
+    before = jnp.where(z == 0, 2, jnp.where(z == 1, 0, jnp.where(z == 2, 3, 1)))
+    planes = {0: z, 1: before, 3: 3 - before, 2: 3 - z}
+
+    def start_of(plane):
+        return pl.multiple_of(lax.rem(plane * PLANE + total - con * half, total), PLANE)
+
+    copies = []
+    for n in range(len(packed)):
+        copies += fetch(con, width, pieces[4 * n : 4 * n + 4], packed_ref.at[n], sems.at[n])
+    r_copies = [
+        pltpu.make_async_copy(rows, a_ref.at[pl.ds(start_of(planes[k]), PLANE)], r_sems.at[n])
+        for n, (k, rows) in enumerate(zip(ready, rows_ready))
+    ]
     w_copies = [
         pltpu.make_async_copy(
             w_hbm.at[pl.ds(n * block, block)], w_ref.at[pl.ds(n * block, block)], w_sems.at[n]
         )
         for n in range(w_sems.shape[0])
     ]
-    for copy in copies + w_copies:
+    for copy in copies + w_copies[:1] + r_copies + w_copies[1:]:
         copy.start()
-    plane_before = jnp.where(z == 0, 2, jnp.where(z == 1, 0, jnp.where(z == 2, 3, 1)))
-    planes = (z, plane_before, 3 - plane_before, 3 - z)
-
-    @pl.loop(0, count // per_plane)
-    def _(k):
-        plane = jnp.where(
-            k == 0, planes[0], jnp.where(k == 1, planes[1], jnp.where(k == 2, planes[2], planes[3]))
-        )
-        places = []
-        for n in range(per_plane):
-            core = con if n < 2 else 1 - con
-            chips = (inside, inside ^ (1 + core)) if n % 2 == 0 else (inside ^ (2 - core), inside ^ 3)
-            for c in chips:
-                place = ((plane * 4 + c) * 2 + core) * ROWS + total - con * half
-                places.append(pl.multiple_of(lax.rem(place, total), ROWS))
-            rows = pieces_ref.at[k, pl.ds(n * depth, depth)]
-            for i, part in enumerate((pl.ds(0, width), pl.ds(width, 2 * width))):
-                at = rows.at[:, part]
-                pltpu.make_async_copy(at, at, sems.at[k * per_plane + n, i]).wait()
-        unpack_rows(cw, nirrep, sizes_ref, con, pieces_ref.at[k], places, a_ref)
+    inner = places_in_plane(chip, con)
+
+    @pl.loop(0, len(packed))
+    def _(n):
+        plane = planes[packed[0]]
+        for i, k in enumerate(packed[1:]):
+            plane = jnp.where(n == i + 1, planes[k], plane)
+        places = [pl.multiple_of(start_of(plane) + place, ROWS) for place in inner]
+        for copy in fetch(con, width, pieces[:4], packed_ref.at[n], sems.at[n]):
+            copy.wait()
+        unpack_rows(cw, nirrep, numbers_ref, con, packed_ref.at[n], places, a_ref)
+
+    for copy in r_copies:
+        copy.wait()
 
     def send_copy(n):
         columns = pl.ds(pl.multiple_of(n * block, block), block)
@@ -238,28 +291,29 @@
         send_copy(n).wait()
 
 
-def contract(numbers, pieces, integrals, cw, nirrep):
+def contract(numbers, ready, packed, integrals, cw, nirrep):
     n, k = integrals.shape
-    count = len(pieces)
-    total = sum(piece.shape[0] for piece in pieces)
+    total = PLANE * (len(ready) + len(packed))
     half = jax.ShapeDtypeStruct((total // 2, n), jnp.float32)
+    pieces = [piece for plane in packed.values() for piece in plane]
     return pl.pallas_call(
-        functools.partial(contract_kernel, cw, nirrep, count),
+        functools.partial(contract_kernel, cw, nirrep, tuple(ready), tuple(packed)),
         out_shape=(pltpu.VMEM(half.shape, half.dtype), half),
-        in_specs=[SMEM] + [ANY] * count + [HBM],
+        in_specs=[SMEM] + [HBM] * len(ready) + [ANY] * len(pieces) + [HBM],
         out_specs=(VMEM, HBM),
         scratch_shapes=[
             pltpu.VMEM((total, k), jnp.bfloat16),
             pltpu.VMEM((n, k), jnp.bfloat16),
-            pltpu.VMEM((total // PLANE, PLANE, k), jnp.bfloat16),
+            pltpu.VMEM((len(packed), PLANE, k), jnp.bfloat16),
             pltpu.VMEM((total // 2, n), jnp.float32),
-            pltpu.SemaphoreType.DMA((count, 2)),
+            pltpu.SemaphoreType.DMA((len(packed), 4, 2)),
+            pltpu.SemaphoreType.DMA((len(ready) + 1,)),
             pltpu.SemaphoreType.DMA((n // 256,)),
             pltpu.SemaphoreType.DMA((n // 256,)),
         ],
         compiler_params=pltpu.CompilerParams(vmem_limit_bytes=44 * 2**20),
         name="contract",
-    )(numbers, *pieces, integrals)
+    )(numbers, *ready.values(), *pieces, integrals)
 
 
 def add_kernel(keep_ref, got_ref, out, out_ref, sems):
@@ -332,6 +386,7 @@
     "s2": (("z2", "f2"), "second"),
 }
 AFTER = {"z3": ("f0",), "f3": ("s0",), "f2": ("f1",)}
+READY = {0: 10**10}
 
 
 def ladder_of_16(amplitudes, integrals, block_sizes):
@@ -384,12 +439,16 @@
         value = get(sent)
         arrays[(name,)] = move(after(value, *others) if others else value, way)
 
-    pieces = []
-    for k, z in enumerate(("own", "z1", "z3", "z2")):
-        f, s = f"f{z[1:]}" if k else "f0", f"s{z[1:]}" if k else "s0"
-        plane = [get((z, f)), arrays[(s,)]]
-        pieces += plane + [swap_cores(piece) for piece in plane]
-    keep, send = contract(numbers, pieces, integrals, cw, block_sizes.shape[0])
+    nirrep = block_sizes.shape[0]
+    ready, packed = {}, {}
+    for k, z in ((0, "own"), (1, "z1"), (3, "z3"), (2, "z2")):
+        plane = [get((z, f"f{k}")), arrays[(f"s{k}",)]]
+        plane += [swap_cores(piece) for piece in plane]
+        if k in READY:
+            ready[k] = unpack(numbers, plane, cw, nirrep, READY[k])
+        else:
+            packed[k] = plane
+    keep, send = contract(numbers, ready, packed, integrals, cw, nirrep)
     return add(keep, swap_cores(send))
 
 

time: 60.5 us -> 58 us (0.959)
  waiting for transfers between devices: 21.4 us -> 15 us
  starting transfers between devices: 22.4 us -> 25.1 us
  Pallas kernels: 13.9 us -> 14.9 us
    ppermute x11, waiting for transfers between devices: 17.2 us -> 12.4 us  [move(): return lax.ppermute(value, ('out', 'con'), pairs)]
    ppermute x11, starting transfers between devices: 11.9 us -> 13.6 us  [move(): return lax.ppermute(value, ('out', 'con'), pairs)]
    ppermute x9, waiting for transfers between devices: 4.2 us -> 2.63 us  [swap_cores(): return lax.ppermute(value, 'con', [(0, 1), (1, 0)])]
    ppermute x9, starting transfers between devices: 10.5 us -> 11.4 us  [swap_cores(): return lax.ppermute(value, 'con', [(0, 1), (1, 0)])]
    pallas_call x1 -> x2, Pallas kernels: 11.1 us -> 12.1 us  [the longest x1 10.1 us: contract(): pl.pallas_call(functools.partial(contract_kernel, cw, nirrep, tuple(ready...]
  transfers between devices with their start and end apart: 20 -> 20, of which waited for: 9 -> 8; matrix products, arithmetic and copies ran while one was open for 2% -> 3% of each run, Pallas kernels for 0% -> 3%
where the time goes in v3:
time: 58 us; the launch traced here: 57.5 us
  starting transfers between devices  25.1 us (43%)
  waiting for transfers between devices  15 us (26%)
  Pallas kernels  14.9 us (26%)
  local copies, waits for them, and re-layouts  1.77 us (3%)
  other arithmetic  0.73 us (1%)
    ppermute x11, starting transfers between devices, move(): return lax.ppermute(value, ('out', 'con'), pairs)  13.6 us
    ppermute x11, waiting for transfers between devices, move(): return lax.ppermute(value, ('out', 'con'), pairs)  12.4 us
    ppermute x9, starting transfers between devices, swap_cores(): return lax.ppermute(value, 'con', [(0, 1), (1, 0)])  11.4 us
    pallas_call x1, Pallas kernels, contract(): pl.pallas_call(functools.partial(contract_kernel, cw, nirrep, tuple(ready...  10.1 us
    ppermute x9, waiting for transfers between devices, swap_cores(): return lax.ppermute(value, 'con', [(0, 1), (1, 0)])  2.63 us
    pallas_call x1, Pallas kernels, unpack(): pl.pallas_call(functools.partial(unpack_kernel, cw, nirrep), out_shape=ja...  1.96 us
    pallas_call x1, Pallas kernels, pack(): pl.pallas_call(functools.partial(pack_kernel, nirrep, cw), out_shape=(jax...  1.94 us
  transfers between devices with their start and end apart: 20, of which 8 were waited for; matrix products, arithmetic and copies ran while one was open for 3% of the time, Pallas kernels for 3%

profile of v3, /device:TPU:25, one launch (start us, length us, event | category | flops | bytes accessed | tf_op | source)
XLA Modules:
  0.0 57.5 jit_solution(18135211408836095354)
XLA Ops:
  0.0 1.9 %pack.1 = (bf16[16,6144]{1,0:T(8,128)(2,1)}, bf16[32,6144]{1,0:T(8,128)(2,1)}) custom-call(s32[8]{0:T(128)} %sizes_ref.1, bf16[16,9216]{1,0:T(8,128)(2,1)} %amp_ref.1), custom_call_target="tpu_custom_call" | custom-call | tf_op jit(solution)/shard_map/pack/pallas_call | solution.py:88
  1.9 1.2 %collective-permute-start = (bf16[16,6144]{1,0:T(8,128)(2,1)}, bf16[16,6144]{1,0:T(8,128)(2,1)S(1)}, u32[]{:S(2)}, u32[]{:S(2)}) collective-permute-start(bf16[16,6144]{1,0:T(8,128)(2,1)} %get-tuple-element.15), channel_id=1, source_target_pairs={{0,2},{1,5},{2,0},{3,7},{4,6},{5,1},{6,4},{7,3},{8,10},{9,13},{10,... | collective-permute-start | bytes 589832 | tf_op jit(solution)/shard_map/ppermute | solution.py:408
  3.2 0.2 collective-permute-start.4
  3.4 0.7 %pad_add_fusion.numbers_ref = s32[10]{0:T(128)S(1)} fusion(s32[1]{0:T(128)} %bitcast.1, s32[1]{0:T(128)} %bitcast, s32[8]{0:T(128)} %sizes_ref.1), kind=kLoop, calls=%fused_computation.6 | loop fusion | flops 20 | bytes 80 | tf_op jit(solution)/shard_map/concatenate | solution.py:415
  4.1 2.9 %collective-permute-done = bf16[16,6144]{1,0:T(8,128)(2,1)S(1)} collective-permute-done((bf16[16,6144]{1,0:T(8,128)(2,1)}, bf16[16,6144]{1,0:T(8,128)(2,1)S(1)}, u32[]{:S(2)}, u32[]{:S(2)}) %collective-permute-start) | collective-permute-done | bytes 196640 | tf_op jit(solution)/shard_map/ppermute | solution.py:408
  7.0 0.7 %constant_dynamic-update-slice_fusion.6.refs_0_ = bf16[32,6144]{1,0:T(8,128)(2,1)} fusion(bf16[32,6144]{1,0:T(8,128)(2,1)} %get-tuple-element.13, bf16[16,6144]{1,0:T(8,128)(2,1)S(1)} %collective-permute-done), kind=kLoop, calls=%fused_computation.7 | loop fusion | bytes 393216 | tf_op jit(solution)/shard_map/dynamic_update_slice | solution.py:423
  7.7 1.5 %collective-permute-start.2 = (bf16[32,6144]{1,0:T(8,128)(2,1)}, bf16[32,6144]{1,0:T(8,128)(2,1)S(1)}, u32[]{:S(2)}, u32[]{:S(2)}) collective-permute-start(bf16[32,6144]{1,0:T(8,128)(2,1)} %constant_dynamic-update-slice_fusion.6.refs_0_), channel_id=1, source_target_pairs={{0,1},{1,0},{2,3},{3,2},{4,5},{5,4},{6,7},{7,6},{8,9},{9,8},{10,11... | collective-permute-start | bytes 1179656 | tf_op jit(solution)/shard_map/ppermute | solution.py:411
  9.2 1.2 %collective-permute-start.1 = (bf16[32,6144]{1,0:T(8,128)(2,1)}, bf16[32,6144]{1,0:T(8,128)(2,1)S(1)}, u32[]{:S(2)}, u32[]{:S(2)}) collective-permute-start(bf16[32,6144]{1,0:T(8,128)(2,1)} %constant_dynamic-update-slice_fusion.6.refs_0_), channel_id=1, source_target_pairs={{0,4},{1,3},{2,6},{3,1},{4,0},{5,7},{6,2},{7,5},{8,12},{9,11},{10,... | collective-permute-start | bytes 1179656 | tf_op jit(solution)/shard_map/ppermute | solution.py:408
  10.4 0.2 collective-permute-start.14
  10.6 2.2 %collective-permute-start.9 = (bf16[16,6144]{1,0:T(8,128)(2,1)}, bf16[16,6144]{1,0:T(8,128)(2,1)S(1)}, u32[]{:S(2)}, u32[]{:S(2)}) collective-permute-start(bf16[16,6144]{1,0:T(8,128)(2,1)} %get-tuple-element.15), channel_id=1, source_target_pairs={{0,16},{1,17},{2,18},{3,19},{4,20},{5,21},{6,22},{7,23},{8,0},{9,1... | collective-permute-start | bytes 589832 | tf_op jit(solution)/shard_map/ppermute | solution.py:408
  12.8 1.2 %collective-permute-start.5 = (bf16[16,6144]{1,0:T(8,128)(2,1)S(1)}, bf16[16,6144]{1,0:T(8,128)(2,1)S(1)}, u32[]{:S(2)}, u32[]{:S(2)}) collective-permute-start(bf16[16,6144]{1,0:T(8,128)(2,1)S(1)} %collective-permute-done.4), channel_id=1, source_target_pairs={{0,2},{1,5},{2,0},{3,7},{4,6},{5,1},{6,4},{7,3},{8,10},{9,13},{10,... | collective-permute-start | bytes 589832 | tf_op jit(solution)/shard_map/ppermute | solution.py:408
  14.0 3.0 %collective-permute-done.14 = bf16[16,6144]{1,0:T(8,128)(2,1)S(1)} collective-permute-done((bf16[16,6144]{1,0:T(8,128)(2,1)S(1)}, bf16[16,6144]{1,0:T(8,128)(2,1)S(1)}, u32[]{:S(2)}, u32[]{:S(2)}) %collective-permute-start.14) | collective-permute-done | bytes 196640 | tf_op jit(solution)/shard_map/ppermute | solution.py:408
  17.0 1.8 %collective-permute-done.5 = bf16[16,6144]{1,0:T(8,128)(2,1)S(1)} collective-permute-done((bf16[16,6144]{1,0:T(8,128)(2,1)S(1)}, bf16[16,6144]{1,0:T(8,128)(2,1)S(1)}, u32[]{:S(2)}, u32[]{:S(2)}) %collective-permute-start.5) | collective-permute-done | bytes 196640 | tf_op jit(solution)/shard_map/ppermute | solution.py:408
  18.9 3.9 %collective-permute-start.15 = (bf16[16,6144]{1,0:T(8,128)(2,1)S(1)}, bf16[16,6144]{1,0:T(8,128)(2,1)S(1)}, u32[]{:S(2)}, u32[]{:S(2)}) collective-permute-start(bf16[16,6144]{1,0:T(8,128)(2,1)S(1)} %collective-permute-done.14), channel_id=1, source_target_pairs={{0,2},{1,5},{2,0},{3,7},{4,6},{5,1},{6,4},{7,3},{8,10},{9,13},{10,... | collective-permute-start | bytes 589832 | tf_op jit(solution)/shard_map/ppermute | solution.py:408
  22.8 2.1 %collective-permute-start.7 = (bf16[32,6144]{1,0:T(8,128)(2,1)S(1)}, bf16[32,6144]{1,0:T(8,128)(2,1)S(1)}, u32[]{:S(2)}, u32[]{:S(2)}) collective-permute-start(bf16[32,6144]{1,0:T(8,128)(2,1)S(1)} %constant_dynamic-update-slice_fusion.refs_1_), channel_id=1, source_target_pairs={{0,1},{1,0},{2,3},{3,2},{4,5},{5,4},{6,7},{7,6},{8,9},{9,8},{10,11... | collective-permute-start | bytes 1179656 | tf_op jit(solution)/shard_map/ppermute | solution.py:411
  25.0 0.1 collective-permute-start.10
  25.1 1.1 %collective-permute-done.15 = bf16[16,6144]{1,0:T(8,128)(2,1)S(1)} collective-permute-done((bf16[16,6144]{1,0:T(8,128)(2,1)S(1)}, bf16[16,6144]{1,0:T(8,128)(2,1)S(1)}, u32[]{:S(2)}, u32[]{:S(2)}) %collective-permute-start.15) | collective-permute-done | bytes 196640 | tf_op jit(solution)/shard_map/ppermute | solution.py:408
  26.2 1.7 %collective-permute-start.16 = (bf16[32,6144]{1,0:T(8,128)(2,1)S(1)}, bf16[32,6144]{1,0:T(8,128)(2,1)S(1)}, u32[]{:S(2)}, u32[]{:S(2)}) collective-permute-start(bf16[32,6144]{1,0:T(8,128)(2,1)S(1)} %constant_dynamic-update-slice_fusion.4.refs_9_), channel_id=1, source_target_pairs={{0,4},{1,3},{2,6},{3,1},{4,0},{5,7},{6,2},{7,5},{8,12},{9,11},{10,... | collective-permute-start | bytes 1179656 | tf_op jit(solution)/shard_map/ppermute | solution.py:408
  27.9 2.0 %collective-permute-done.10 = bf16[16,6144]{1,0:T(8,128)(2,1)S(1)} collective-permute-done((bf16[16,6144]{1,0:T(8,128)(2,1)S(1)}, bf16[16,6144]{1,0:T(8,128)(2,1)S(1)}, u32[]{:S(2)}, u32[]{:S(2)}) %collective-permute-start.10) | collective-permute-done | bytes 196640 | tf_op jit(solution)/shard_map/ppermute | solution.py:408
  29.9 2.1 %collective-permute-start.3 = (bf16[32,6144]{1,0:T(8,128)(2,1)S(1)}, bf16[32,6144]{1,0:T(8,128)(2,1)S(1)}, u32[]{:S(2)}, u32[]{:S(2)}) collective-permute-start(bf16[32,6144]{1,0:T(8,128)(2,1)S(1)} %collective-permute-done.1.refs_1_), channel_id=1, source_target_pairs={{0,1},{1,0},{2,3},{3,2},{4,5},{5,4},{6,7},{7,6},{8,9},{9,8},{10,11... | collective-permute-start | bytes 1179656 | tf_op jit(solution)/shard_map/ppermute | solution.py:411
  32.0 1.7 %collective-permute-start.11 = (bf16[32,6144]{1,0:T(8,128)(2,1)S(1)}, bf16[32,6144]{1,0:T(8,128)(2,1)S(1)}, u32[]{:S(2)}, u32[]{:S(2)}) collective-permute-start(bf16[32,6144]{1,0:T(8,128)(2,1)S(1)} %constant_dynamic-update-slice_fusion.2.refs_5_), channel_id=1, source_target_pairs={{0,4},{1,3},{2,6},{3,1},{4,0},{5,7},{6,2},{7,5},{8,12},{9,11},{10,... | collective-permute-start | bytes 1179656 | tf_op jit(solution)/shard_map/ppermute | solution.py:408
  33.7 0.8 %collective-permute-done.16.refs_10_ = bf16[32,6144]{1,0:T(8,128)(2,1)S(1)} collective-permute-done((bf16[32,6144]{1,0:T(8,128)(2,1)S(1)}, bf16[32,6144]{1,0:T(8,128)(2,1)S(1)}, u32[]{:S(2)}, u32[]{:S(2)}) %collective-permute-start.16) | collective-permute-done | bytes 393248 | tf_op jit(solution)/shard_map/ppermute | solution.py:408
  34.5 1.9 %collective-permute-start.12 = (bf16[32,6144]{1,0:T(8,128)(2,1)S(1)}, bf16[32,6144]{1,0:T(8,128)(2,1)S(1)}, u32[]{:S(2)}, u32[]{:S(2)}) collective-permute-start(bf16[32,6144]{1,0:T(8,128)(2,1)S(1)} %constant_dynamic-update-slice_fusion.2.refs_5_), channel_id=1, source_target_pairs={{0,1},{1,0},{2,3},{3,2},{4,5},{5,4},{6,7},{7,6},{8,9},{9,8},{10,11... | collective-permute-start | bytes 1179656 | tf_op jit(solution)/shard_map/ppermute | solution.py:411
  36.4 0.7 %collective-permute-done.6.refs_2_ = bf16[32,6144]{1,0:T(8,128)(2,1)S(1)} collective-permute-done((bf16[32,6144]{1,0:T(8,128)(2,1)S(1)}, bf16[32,6144]{1,0:T(8,128)(2,1)S(1)}, u32[]{:S(2)}, u32[]{:S(2)}) %collective-permute-start.6) | collective-permute-done | bytes 393248 | tf_op jit(solution)/shard_map/ppermute | solution.py:408
  37.1 3.2 %collective-permute-start.18 = (bf16[32,6144]{1,0:T(8,128)(2,1)S(1)}, bf16[32,6144]{1,0:T(8,128)(2,1)S(1)}, u32[]{:S(2)}, u32[]{:S(2)}) collective-permute-start(bf16[32,6144]{1,0:T(8,128)(2,1)S(1)} %collective-permute-done.16.refs_10_), channel_id=1, source_target_pairs={{0,1},{1,0},{2,3},{3,2},{4,5},{5,4},{6,7},{7,6},{8,9},{9,8},{10,11... | collective-permute-start | bytes 1179656 | tf_op jit(solution)/shard_map/ppermute | solution.py:411
  40.3 0.5 collective-permute-start.13
  40.8 1.0 %copy-done = bf16[32,6144]{1,0:T(8,128)(2,1)S(1)} copy-done((bf16[32,6144]{1,0:T(8,128)(2,1)S(1)}, bf16[32,6144]{1,0:T(8,128)(2,1)}, u32[]{:S(2)}) %copy-start) | copy-done | bytes 393240
  41.8 2.0 %unpack.1.refs_0_ = bf16[128,4608]{1,0:T(8,128)(2,1)S(1)} custom-call(s32[10]{0:T(128)S(1)} %pad_add_fusion.numbers_ref, bf16[32,6144]{1,0:T(8,128)(2,1)S(1)} %copy-done, bf16[32,6144]{1,0:T(8,128)(2,1)S(1)} %collective-permute-done.1.refs_1_, bf16[32,6144]{1,0:T(8,128)(2,1)S(1)} %collective-permute-done.2.refs_2_, ...), custom_call_target="tpu_custom_call" | custom-call | flops 10000000000 | bytes 2359296 | tf_op jit(solution)/shard_map/unpack/pallas_call | solution.py:206
  43.8 10.1 %contract.1 = (f32[256,1024]{1,0:T(8,128)S(1)}, f32[256,1024]{1,0:T(8,128)S(1)}) custom-call(s32[10]{0:T(128)S(1)} %pad_add_fusion.numbers_ref, bf16[128,4608]{1,0:T(8,128)(2,1)S(1)} %unpack.1.refs_0_, bf16[32,6144]{1,0:T(8,128)(2,1)S(1)} %constant_dynamic-update-slice_fusion.refs_1_, bf16[32,6144]{1,0:T(8,128)(2,1)S(1)} %collective-permute-done.6.refs_2_, ...), custom_call_target="tpu_custom_call" | custom-call | tf_op jit(solution)/shard_map/contract/pallas_call | solution.py:299
  54.0 0.1 collective-permute-start.19
  54.1 2.6 %collective-permute-done.19.got_ref = f32[256,1024]{1,0:T(8,128)S(1)} collective-permute-done((f32[256,1024]{1,0:T(8,128)S(1)}, f32[256,1024]{1,0:T(8,128)S(1)}, u32[]{:S(2)}, u32[]{:S(2)}) %collective-permute-start.19) | collective-permute-done | bytes 1048608 | tf_op jit(solution)/shard_map/ppermute | solution.py:411
  56.7 0.8 %add.5 = bf16[256,1024]{1,0:T(8,128)(2,1)} custom-call(f32[256,1024]{1,0:T(8,128)S(1)} %get-tuple-element.19.keep_ref, f32[256,1024]{1,0:T(8,128)S(1)} %collective-permute-done.19.got_ref), custom_call_target="tpu_custom_call" | custom-call | tf_op jit(solution)/shard_map/add/pallas_call | solution.py:340
  (22 shorter events, 0.1 us)
Async XLA Ops:
  1.9 5.0 %collective-permute-start = (bf16[16,6144]{1,0:T(8,128)(2,1)}, bf16[16,6144]{1,0:T(8,128)(2,1)S(1)}, u32[]{:S(2)}, u32[]{:S(2)}) collective-permute-start(bf16[16,6144]{1,0:T(8,128)(2,1)} %get-tuple-element.15), channel_id=1, source_target_pairs={{0,2},{1,5},{2,0},{3,7},{4,6},{5,1},{6,4},{7,3},{8,10},{9,13},{10,... | collective-permute-start | bytes 589832 | tf_op jit(solution)/shard_map/ppermute | solution.py:408
  3.2 7.2 %collective-permute-start.4 = (bf16[16,6144]{1,0:T(8,128)(2,1)}, bf16[16,6144]{1,0:T(8,128)(2,1)S(1)}, u32[]{:S(2)}, u32[]{:S(2)}) collective-permute-start(bf16[16,6144]{1,0:T(8,128)(2,1)} %get-tuple-element.15), channel_id=1, source_target_pairs={{0,8},{1,9},{2,10},{3,11},{4,12},{5,13},{6,14},{7,15},{8,24},{9,25... | collective-permute-start | bytes 589832 | tf_op jit(solution)/shard_map/ppermute | solution.py:408
  7.7 24.3 %collective-permute-start.2 = (bf16[32,6144]{1,0:T(8,128)(2,1)}, bf16[32,6144]{1,0:T(8,128)(2,1)S(1)}, u32[]{:S(2)}, u32[]{:S(2)}) collective-permute-start(bf16[32,6144]{1,0:T(8,128)(2,1)} %constant_dynamic-update-slice_fusion.6.refs_0_), channel_id=1, source_target_pairs={{0,1},{1,0},{2,3},{3,2},{4,5},{5,4},{6,7},{7,6},{8,9},{9,8},{10,11... | collective-permute-start | bytes 1179656 | tf_op jit(solution)/shard_map/ppermute | solution.py:411
  9.2 15.8 %collective-permute-start.1 = (bf16[32,6144]{1,0:T(8,128)(2,1)}, bf16[32,6144]{1,0:T(8,128)(2,1)S(1)}, u32[]{:S(2)}, u32[]{:S(2)}) collective-permute-start(bf16[32,6144]{1,0:T(8,128)(2,1)} %constant_dynamic-update-slice_fusion.6.refs_0_), channel_id=1, source_target_pairs={{0,4},{1,3},{2,6},{3,1},{4,0},{5,7},{6,2},{7,5},{8,12},{9,11},{10,... | collective-permute-start | bytes 1179656 | tf_op jit(solution)/shard_map/ppermute | solution.py:408
  10.4 6.6 %collective-permute-start.14 = (bf16[16,6144]{1,0:T(8,128)(2,1)S(1)}, bf16[16,6144]{1,0:T(8,128)(2,1)S(1)}, u32[]{:S(2)}, u32[]{:S(2)}) collective-permute-start(bf16[16,6144]{1,0:T(8,128)(2,1)S(1)} %collective-permute-done.4), channel_id=1, source_target_pairs={{0,8},{1,9},{2,10},{3,11},{4,12},{5,13},{6,14},{7,15},{8,24},{9,25... | collective-permute-start | bytes 589832 | tf_op jit(solution)/shard_map/ppermute | solution.py:408
  10.6 14.4 %collective-permute-start.9 = (bf16[16,6144]{1,0:T(8,128)(2,1)}, bf16[16,6144]{1,0:T(8,128)(2,1)S(1)}, u32[]{:S(2)}, u32[]{:S(2)}) collective-permute-start(bf16[16,6144]{1,0:T(8,128)(2,1)} %get-tuple-element.15), channel_id=1, source_target_pairs={{0,16},{1,17},{2,18},{3,19},{4,20},{5,21},{6,22},{7,23},{8,0},{9,1... | collective-permute-start | bytes 589832 | tf_op jit(solution)/shard_map/ppermute | solution.py:408
  12.8 6.1 %collective-permute-start.5 = (bf16[16,6144]{1,0:T(8,128)(2,1)S(1)}, bf16[16,6144]{1,0:T(8,128)(2,1)S(1)}, u32[]{:S(2)}, u32[]{:S(2)}) collective-permute-start(bf16[16,6144]{1,0:T(8,128)(2,1)S(1)} %collective-permute-done.4), channel_id=1, source_target_pairs={{0,2},{1,5},{2,0},{3,7},{4,6},{5,1},{6,4},{7,3},{8,10},{9,13},{10,... | collective-permute-start | bytes 589832 | tf_op jit(solution)/shard_map/ppermute | solution.py:408
  18.9 7.3 %collective-permute-start.15 = (bf16[16,6144]{1,0:T(8,128)(2,1)S(1)}, bf16[16,6144]{1,0:T(8,128)(2,1)S(1)}, u32[]{:S(2)}, u32[]{:S(2)}) collective-permute-start(bf16[16,6144]{1,0:T(8,128)(2,1)S(1)} %collective-permute-done.14), channel_id=1, source_target_pairs={{0,2},{1,5},{2,0},{3,7},{4,6},{5,1},{6,4},{7,3},{8,10},{9,13},{10,... | collective-permute-start | bytes 589832 | tf_op jit(solution)/shard_map/ppermute | solution.py:408
  22.8 10.9 %collective-permute-start.7 = (bf16[32,6144]{1,0:T(8,128)(2,1)S(1)}, bf16[32,6144]{1,0:T(8,128)(2,1)S(1)}, u32[]{:S(2)}, u32[]{:S(2)}) collective-permute-start(bf16[32,6144]{1,0:T(8,128)(2,1)S(1)} %constant_dynamic-update-slice_fusion.refs_1_), channel_id=1, source_target_pairs={{0,1},{1,0},{2,3},{3,2},{4,5},{5,4},{6,7},{7,6},{8,9},{9,8},{10,11... | collective-permute-start | bytes 1179656 | tf_op jit(solution)/shard_map/ppermute | solution.py:411
  25.0 4.9 %collective-permute-start.10 = (bf16[16,6144]{1,0:T(8,128)(2,1)S(1)}, bf16[16,6144]{1,0:T(8,128)(2,1)S(1)}, u32[]{:S(2)}, u32[]{:S(2)}) collective-permute-start(bf16[16,6144]{1,0:T(8,128)(2,1)S(1)} %collective-permute-done.9), channel_id=1, source_target_pairs={{0,2},{1,5},{2,0},{3,7},{4,6},{5,1},{6,4},{7,3},{8,10},{9,13},{10,... | collective-permute-start | bytes 589832 | tf_op jit(solution)/shard_map/ppermute | solution.py:408
  26.2 8.4 %collective-permute-start.16 = (bf16[32,6144]{1,0:T(8,128)(2,1)S(1)}, bf16[32,6144]{1,0:T(8,128)(2,1)S(1)}, u32[]{:S(2)}, u32[]{:S(2)}) collective-permute-start(bf16[32,6144]{1,0:T(8,128)(2,1)S(1)} %constant_dynamic-update-slice_fusion.4.refs_9_), channel_id=1, source_target_pairs={{0,4},{1,3},{2,6},{3,1},{4,0},{5,7},{6,2},{7,5},{8,12},{9,11},{10,... | collective-permute-start | bytes 1179656 | tf_op jit(solution)/shard_map/ppermute | solution.py:408
  27.9 9.2 %collective-permute-start.6 = (bf16[32,6144]{1,0:T(8,128)(2,1)S(1)}, bf16[32,6144]{1,0:T(8,128)(2,1)S(1)}, u32[]{:S(2)}, u32[]{:S(2)}) collective-permute-start(bf16[32,6144]{1,0:T(8,128)(2,1)S(1)} %collective-permute-done.1.refs_1_), channel_id=1, source_target_pairs={{0,8},{1,9},{2,10},{3,11},{4,12},{5,13},{6,14},{7,15},{8,24},{9,25... | collective-permute-start | bytes 1179656 | tf_op jit(solution)/shard_map/ppermute | solution.py:408
  29.9 10.5 %collective-permute-start.3 = (bf16[32,6144]{1,0:T(8,128)(2,1)S(1)}, bf16[32,6144]{1,0:T(8,128)(2,1)S(1)}, u32[]{:S(2)}, u32[]{:S(2)}) collective-permute-start(bf16[32,6144]{1,0:T(8,128)(2,1)S(1)} %collective-permute-done.1.refs_1_), channel_id=1, source_target_pairs={{0,1},{1,0},{2,3},{3,2},{4,5},{5,4},{6,7},{7,6},{8,9},{9,8},{10,11... | collective-permute-start | bytes 1179656 | tf_op jit(solution)/shard_map/ppermute | solution.py:411
  32.0 8.3 %collective-permute-start.11 = (bf16[32,6144]{1,0:T(8,128)(2,1)S(1)}, bf16[32,6144]{1,0:T(8,128)(2,1)S(1)}, u32[]{:S(2)}, u32[]{:S(2)}) collective-permute-start(bf16[32,6144]{1,0:T(8,128)(2,1)S(1)} %constant_dynamic-update-slice_fusion.2.refs_5_), channel_id=1, source_target_pairs={{0,4},{1,3},{2,6},{3,1},{4,0},{5,7},{6,2},{7,5},{8,12},{9,11},{10,... | collective-permute-start | bytes 1179656 | tf_op jit(solution)/shard_map/ppermute | solution.py:408
  33.7 10.1 %collective-permute-start.17 = (bf16[32,6144]{1,0:T(8,128)(2,1)S(1)}, bf16[32,6144]{1,0:T(8,128)(2,1)S(1)}, u32[]{:S(2)}, u32[]{:S(2)}) collective-permute-start(bf16[32,6144]{1,0:T(8,128)(2,1)S(1)} %constant_dynamic-update-slice_fusion.4.refs_9_), channel_id=1, source_target_pairs={{0,1},{1,0},{2,3},{3,2},{4,5},{5,4},{6,7},{7,6},{8,9},{9,8},{10,11... | collective-permute-start | bytes 1179656 | tf_op jit(solution)/shard_map/ppermute | solution.py:411
  34.5 9.3 %collective-permute-start.12 = (bf16[32,6144]{1,0:T(8,128)(2,1)S(1)}, bf16[32,6144]{1,0:T(8,128)(2,1)S(1)}, u32[]{:S(2)}, u32[]{:S(2)}) collective-permute-start(bf16[32,6144]{1,0:T(8,128)(2,1)S(1)} %constant_dynamic-update-slice_fusion.2.refs_5_), channel_id=1, source_target_pairs={{0,1},{1,0},{2,3},{3,2},{4,5},{5,4},{6,7},{7,6},{8,9},{9,8},{10,11... | collective-permute-start | bytes 1179656 | tf_op jit(solution)/shard_map/ppermute | solution.py:411
  37.1 6.7 %collective-permute-start.18 = (bf16[32,6144]{1,0:T(8,128)(2,1)S(1)}, bf16[32,6144]{1,0:T(8,128)(2,1)S(1)}, u32[]{:S(2)}, u32[]{:S(2)}) collective-permute-start(bf16[32,6144]{1,0:T(8,128)(2,1)S(1)} %collective-permute-done.16.refs_10_), channel_id=1, source_target_pairs={{0,1},{1,0},{2,3},{3,2},{4,5},{5,4},{6,7},{7,6},{8,9},{9,8},{10,11... | collective-permute-start | bytes 1179656 | tf_op jit(solution)/shard_map/ppermute | solution.py:411
  40.3 3.5 %collective-permute-start.8 = (bf16[32,6144]{1,0:T(8,128)(2,1)S(1)}, bf16[32,6144]{1,0:T(8,128)(2,1)S(1)}, u32[]{:S(2)}, u32[]{:S(2)}) collective-permute-start(bf16[32,6144]{1,0:T(8,128)(2,1)S(1)} %collective-permute-done.6.refs_2_), channel_id=1, source_target_pairs={{0,1},{1,0},{2,3},{3,2},{4,5},{5,4},{6,7},{7,6},{8,9},{9,8},{10,11... | collective-permute-start | bytes 1179656 | tf_op jit(solution)/shard_map/ppermute | solution.py:411
  40.3 3.5 %collective-permute-start.13 = (bf16[32,6144]{1,0:T(8,128)(2,1)S(1)}, bf16[32,6144]{1,0:T(8,128)(2,1)S(1)}, u32[]{:S(2)}, u32[]{:S(2)}) collective-permute-start(bf16[32,6144]{1,0:T(8,128)(2,1)S(1)} %collective-permute-done.11.refs_6_), channel_id=1, source_target_pairs={{0,1},{1,0},{2,3},{3,2},{4,5},{5,4},{6,7},{7,6},{8,9},{9,8},{10,11... | collective-permute-start | bytes 1179656 | tf_op jit(solution)/shard_map/ppermute | solution.py:411
  40.8 1.0 %copy-start = (bf16[32,6144]{1,0:T(8,128)(2,1)S(1)}, bf16[32,6144]{1,0:T(8,128)(2,1)}, u32[]{:S(2)}) copy-start(bf16[32,6144]{1,0:T(8,128)(2,1)} %constant_dynamic-update-slice_fusion.6.refs_0_) | copy-start | bytes 1179652
  54.0 2.7 %collective-permute-start.19 = (f32[256,1024]{1,0:T(8,128)S(1)}, f32[256,1024]{1,0:T(8,128)S(1)}, u32[]{:S(2)}, u32[]{:S(2)}) collective-permute-start(f32[256,1024]{1,0:T(8,128)S(1)} %get-tuple-element.20), channel_id=1, source_target_pairs={{0,1},{1,0},{2,3},{3,2},{4,5},{5,4},{6,7},{7,6},{8,9},{9,8},{10,11... | collective-permute-start | bytes 3145736 | tf_op jit(solution)/shard_map/ppermute | solution.py:411

commit v4 on v3

--- a/solution.py
+++ b/solution.py
@@ -41,7 +41,7 @@
 
 
 def roll(x, shift):
-    return pltpu.roll(x.astype(jnp.float32), shift, 1).astype(x.dtype)
+    return pltpu.roll(x, shift, 1)
 
 
 def pack_kernel(nirrep, cw, sizes_ref, amp_ref, out_ref, both_ref):
@@ -187,7 +187,7 @@
 
 def unpack_kernel(cw, nirrep, numbers_ref, *refs):
     pieces = refs[:4]
-    out, a_ref, packed_ref, sems, out_sem = refs[4:]
+    a_ref, packed_ref, sems = refs[4:]
     chip, con = numbers_ref[nirrep], numbers_ref[nirrep + 1]
     copies = fetch(con, a_ref.shape[1] // 3, pieces, packed_ref, sems)
     for copy in copies:
@@ -196,23 +196,18 @@
         copy.wait()
     places = [pl.multiple_of(place, ROWS) for place in places_in_plane(chip, con)]
     unpack_rows(cw, nirrep, numbers_ref, con, packed_ref, places, a_ref)
-    copy = pltpu.make_async_copy(a_ref, out, out_sem)
-    copy.start()
-    copy.wait()
 
 
 def unpack(numbers, pieces, cw, nirrep, flops):
     k = nirrep // 2 * cw * DMAX
     return pl.pallas_call(
         functools.partial(unpack_kernel, cw, nirrep),
-        out_shape=jax.ShapeDtypeStruct((PLANE, k), jnp.bfloat16),
+        out_shape=pltpu.VMEM((PLANE, k), jnp.bfloat16),
         in_specs=[SMEM] + [ANY] * 4,
-        out_specs=HBM,
+        out_specs=VMEM,
         scratch_shapes=[
             pltpu.VMEM((PLANE, k), jnp.bfloat16),
-            pltpu.VMEM((PLANE, k), jnp.bfloat16),
             pltpu.SemaphoreType.DMA((4, 2)),
-            pltpu.SemaphoreType.DMA,
         ],
         compiler_params=pltpu.CompilerParams(vmem_limit_bytes=44 * 2**20),
         cost_estimate=pl.CostEstimate(flops=flops, bytes_accessed=4 * PLANE * k, transcendentals=0),
@@ -225,7 +220,7 @@
     z = chip // 4
     rows_ready, pieces = refs[: len(ready)], refs[len(ready) : len(ready) + 4 * len(packed)]
     refs = refs[len(ready) + 4 * len(packed) :]
-    w_hbm, keep_ref, send_out, a_ref, w_ref, packed_ref, send_ref, sems, r_sems, w_sems, out_sems = refs
+    w_hbm, keep_ref, send_out, a_ref, w_ref, packed_ref, send_ref, sems, w_sems, out_sems = refs
     block = w_ref.shape[0] // w_sems.shape[0]
     half = send_ref.shape[0]
     total = 2 * half
@@ -239,19 +234,17 @@
     copies = []
     for n in range(len(packed)):
         copies += fetch(con, width, pieces[4 * n : 4 * n + 4], packed_ref.at[n], sems.at[n])
-    r_copies = [
-        pltpu.make_async_copy(rows, a_ref.at[pl.ds(start_of(planes[k]), PLANE)], r_sems.at[n])
-        for n, (k, rows) in enumerate(zip(ready, rows_ready))
-    ]
     w_copies = [
         pltpu.make_async_copy(
             w_hbm.at[pl.ds(n * block, block)], w_ref.at[pl.ds(n * block, block)], w_sems.at[n]
         )
         for n in range(w_sems.shape[0])
     ]
-    for copy in copies + w_copies[:1] + r_copies + w_copies[1:]:
+    for copy in copies + w_copies:
         copy.start()
     inner = places_in_plane(chip, con)
+    for k, rows in zip(ready, rows_ready):
+        a_ref[pl.ds(start_of(planes[k]), PLANE)] = rows[...]
 
     @pl.loop(0, len(packed))
     def _(n):
@@ -262,9 +255,6 @@
         for copy in fetch(con, width, pieces[:4], packed_ref.at[n], sems.at[n]):
             copy.wait()
         unpack_rows(cw, nirrep, numbers_ref, con, packed_ref.at[n], places, a_ref)
-
-    for copy in r_copies:
-        copy.wait()
 
     def send_copy(n):
         columns = pl.ds(pl.multiple_of(n * block, block), block)
@@ -299,7 +289,7 @@
     return pl.pallas_call(
         functools.partial(contract_kernel, cw, nirrep, tuple(ready), tuple(packed)),
         out_shape=(pltpu.VMEM(half.shape, half.dtype), half),
-        in_specs=[SMEM] + [HBM] * len(ready) + [ANY] * len(pieces) + [HBM],
+        in_specs=[SMEM] + [VMEM] * len(ready) + [ANY] * len(pieces) + [HBM],
         out_specs=(VMEM, HBM),
         scratch_shapes=[
             pltpu.VMEM((total, k), jnp.bfloat16),
@@ -307,13 +297,17 @@
             pltpu.VMEM((len(packed), PLANE, k), jnp.bfloat16),
             pltpu.VMEM((total // 2, n), jnp.float32),
             pltpu.SemaphoreType.DMA((len(packed), 4, 2)),
-            pltpu.SemaphoreType.DMA((len(ready) + 1,)),
             pltpu.SemaphoreType.DMA((n // 256,)),
             pltpu.SemaphoreType.DMA((n // 256,)),
         ],
         compiler_params=pltpu.CompilerParams(vmem_limit_bytes=44 * 2**20),
         name="contract",
-    )(numbers, *ready.values(), *pieces, integrals)
+    )(
+        numbers,
+        *(pltpu.with_memory_space_constraint(rows, pltpu.VMEM) for rows in ready.values()),
+        *pieces,
+        integrals,
+    )
 
 
 def add_kernel(keep_ref, got_ref, out, out_ref, sems):
@@ -386,7 +380,8 @@
     "s2": (("z2", "f2"), "second"),
 }
 AFTER = {"z3": ("f0",), "f3": ("s0",), "f2": ("f1",)}
-READY = {0: 10**10}
+READY = {0: 10**9}
+LATE = (1,)
 
 
 def ladder_of_16(amplitudes, integrals, block_sizes):
@@ -441,8 +436,11 @@
 
     nirrep = block_sizes.shape[0]
     ready, packed = {}, {}
-    for k, z in ((0, "own"), (1, "z1"), (3, "z3"), (2, "z2")):
-        plane = [get((z, f"f{k}")), arrays[(f"s{k}",)]]
+    for k, z in ((0, "own"), (2, "z2"), (1, "z1"), (3, "z3")):
+        last = arrays[(f"s{k}",)]
+        if k in LATE:
+            last = after(last, *ready.values())
+        plane = [get((z, f"f{k}")), last]
         plane += [swap_cores(piece) for piece in plane]
         if k in READY:
             ready[k] = unpack(numbers, plane, cw, nirrep, READY[k])

time: 58 us -> 57 us (0.983)
  starting transfers between devices: 25.1 us -> 23.6 us
  waiting for transfers between devices: 15 us -> 16.3 us
    ppermute x9, waiting for transfers between devices: 2.63 us -> 4.74 us  [swap_cores(): return lax.ppermute(value, 'con', [(0, 1), (1, 0)])]
    ppermute x9, starting transfers between devices: 11.4 us -> 9.94 us  [swap_cores(): return lax.ppermute(value, 'con', [(0, 1), (1, 0)])]
    ppermute x11, waiting for transfers between devices: 12.4 us -> 11.6 us  [move(): return lax.ppermute(value, ('out', 'con'), pairs)]
  transfers between devices with their start and end apart: 20 -> 20, of which waited for: 8 -> 10; matrix products, arithmetic and copies ran while one was open for 3% -> 3% of each run, Pallas kernels for 3% -> 3%
where the time goes in v4:
time: 57 us; the launch traced here: 56.8 us
  starting transfers between devices  23.6 us (41%)
  waiting for transfers between devices  16.3 us (29%)
  Pallas kernels  14.4 us (25%)
  local copies, waits for them, and re-layouts  1.77 us (3%)
  other arithmetic  0.73 us (1%)
    ppermute x11, starting transfers between devices, move(): return lax.ppermute(value, ('out', 'con'), pairs)  13.6 us
    ppermute x11, waiting for transfers between devices, move(): return lax.ppermute(value, ('out', 'con'), pairs)  11.6 us
    ppermute x9, starting transfers between devices, swap_cores(): return lax.ppermute(value, 'con', [(0, 1), (1, 0)])  9.94 us
    pallas_call x1, Pallas kernels, contract(): pl.pallas_call(functools.partial(contract_kernel, cw, nirrep, tuple(ready...  9.92 us
    ppermute x9, waiting for transfers between devices, swap_cores(): return lax.ppermute(value, 'con', [(0, 1), (1, 0)])  4.74 us
    pallas_call x1, Pallas kernels, pack(): pl.pallas_call(functools.partial(pack_kernel, nirrep, cw), out_shape=(jax...  1.94 us
    pallas_call x1, Pallas kernels, unpack(): pl.pallas_call(functools.partial(unpack_kernel, cw, nirrep), out_shape=pl...  1.66 us
  transfers between devices with their start and end apart: 20, of which 10 were waited for; matrix products, arithmetic and copies ran while one was open for 3% of the time, Pallas kernels for 3%

profile of v4, /device:TPU:25, one launch (start us, length us, event | category | flops | bytes accessed | tf_op | source)
XLA Modules:
  0.0 56.8 jit_solution(10933418975496478301)
XLA Ops:
  0.0 1.9 %pack.1 = (bf16[16,6144]{1,0:T(8,128)(2,1)}, bf16[32,6144]{1,0:T(8,128)(2,1)}) custom-call(s32[8]{0:T(128)} %sizes_ref.1, bf16[16,9216]{1,0:T(8,128)(2,1)} %amp_ref.1), custom_call_target="tpu_custom_call" | custom-call | tf_op jit(solution)/shard_map/pack/pallas_call | solution.py:88
  1.9 1.2 %collective-permute-start = (bf16[16,6144]{1,0:T(8,128)(2,1)}, bf16[16,6144]{1,0:T(8,128)(2,1)S(1)}, u32[]{:S(2)}, u32[]{:S(2)}) collective-permute-start(bf16[16,6144]{1,0:T(8,128)(2,1)} %get-tuple-element.19), channel_id=1, source_target_pairs={{0,2},{1,5},{2,0},{3,7},{4,6},{5,1},{6,4},{7,3},{8,10},{9,13},{10,... | collective-permute-start | bytes 589832 | tf_op jit(solution)/shard_map/ppermute | solution.py:403
  3.2 0.2 collective-permute-start.4
  3.3 0.7 %pad_add_fusion.numbers_ref = s32[10]{0:T(128)S(1)} fusion(s32[1]{0:T(128)} %bitcast.1, s32[1]{0:T(128)} %bitcast, s32[8]{0:T(128)} %sizes_ref.1), kind=kLoop, calls=%fused_computation.6 | loop fusion | flops 20 | bytes 80 | tf_op jit(solution)/shard_map/concatenate | solution.py:410
  4.1 2.9 %collective-permute-done = bf16[16,6144]{1,0:T(8,128)(2,1)S(1)} collective-permute-done((bf16[16,6144]{1,0:T(8,128)(2,1)}, bf16[16,6144]{1,0:T(8,128)(2,1)S(1)}, u32[]{:S(2)}, u32[]{:S(2)}) %collective-permute-start) | collective-permute-done | bytes 196640 | tf_op jit(solution)/shard_map/ppermute | solution.py:403
  7.0 0.7 %constant_dynamic-update-slice_fusion.6.refs_0_ = bf16[32,6144]{1,0:T(8,128)(2,1)} fusion(bf16[32,6144]{1,0:T(8,128)(2,1)} %get-tuple-element.14, bf16[16,6144]{1,0:T(8,128)(2,1)S(1)} %collective-permute-done), kind=kLoop, calls=%fused_computation.7 | loop fusion | bytes 393216 | tf_op jit(solution)/shard_map/dynamic_update_slice | solution.py:418
  7.7 1.5 %collective-permute-start.2 = (bf16[32,6144]{1,0:T(8,128)(2,1)}, bf16[32,6144]{1,0:T(8,128)(2,1)S(1)}, u32[]{:S(2)}, u32[]{:S(2)}) collective-permute-start(bf16[32,6144]{1,0:T(8,128)(2,1)} %constant_dynamic-update-slice_fusion.6.refs_0_), channel_id=1, source_target_pairs={{0,1},{1,0},{2,3},{3,2},{4,5},{5,4},{6,7},{7,6},{8,9},{9,8},{10,11... | collective-permute-start | bytes 1179656 | tf_op jit(solution)/shard_map/ppermute | solution.py:406
  9.2 1.2 %collective-permute-start.1 = (bf16[32,6144]{1,0:T(8,128)(2,1)}, bf16[32,6144]{1,0:T(8,128)(2,1)S(1)}, u32[]{:S(2)}, u32[]{:S(2)}) collective-permute-start(bf16[32,6144]{1,0:T(8,128)(2,1)} %constant_dynamic-update-slice_fusion.6.refs_0_), channel_id=1, source_target_pairs={{0,4},{1,3},{2,6},{3,1},{4,0},{5,7},{6,2},{7,5},{8,12},{9,11},{10,... | collective-permute-start | bytes 1179656 | tf_op jit(solution)/shard_map/ppermute | solution.py:403
  10.4 0.2 collective-permute-start.5
  10.6 2.2 %collective-permute-start.14 = (bf16[16,6144]{1,0:T(8,128)(2,1)}, bf16[16,6144]{1,0:T(8,128)(2,1)S(1)}, u32[]{:S(2)}, u32[]{:S(2)}) collective-permute-start(bf16[16,6144]{1,0:T(8,128)(2,1)} %get-tuple-element.19), channel_id=1, source_target_pairs={{0,16},{1,17},{2,18},{3,19},{4,20},{5,21},{6,22},{7,23},{8,0},{9,1... | collective-permute-start | bytes 589832 | tf_op jit(solution)/shard_map/ppermute | solution.py:403
  12.8 1.2 %collective-permute-start.6 = (bf16[16,6144]{1,0:T(8,128)(2,1)S(1)}, bf16[16,6144]{1,0:T(8,128)(2,1)S(1)}, u32[]{:S(2)}, u32[]{:S(2)}) collective-permute-start(bf16[16,6144]{1,0:T(8,128)(2,1)S(1)} %collective-permute-done.4), channel_id=1, source_target_pairs={{0,2},{1,5},{2,0},{3,7},{4,6},{5,1},{6,4},{7,3},{8,10},{9,13},{10,... | collective-permute-start | bytes 589832 | tf_op jit(solution)/shard_map/ppermute | solution.py:403
  14.0 3.0 %collective-permute-done.5 = bf16[16,6144]{1,0:T(8,128)(2,1)S(1)} collective-permute-done((bf16[16,6144]{1,0:T(8,128)(2,1)S(1)}, bf16[16,6144]{1,0:T(8,128)(2,1)S(1)}, u32[]{:S(2)}, u32[]{:S(2)}) %collective-permute-start.5) | collective-permute-done | bytes 196640 | tf_op jit(solution)/shard_map/ppermute | solution.py:403
  17.0 1.8 %collective-permute-done.6 = bf16[16,6144]{1,0:T(8,128)(2,1)S(1)} collective-permute-done((bf16[16,6144]{1,0:T(8,128)(2,1)S(1)}, bf16[16,6144]{1,0:T(8,128)(2,1)S(1)}, u32[]{:S(2)}, u32[]{:S(2)}) %collective-permute-start.6) | collective-permute-done | bytes 196640 | tf_op jit(solution)/shard_map/ppermute | solution.py:403
  18.9 3.9 %collective-permute-start.7 = (bf16[16,6144]{1,0:T(8,128)(2,1)S(1)}, bf16[16,6144]{1,0:T(8,128)(2,1)S(1)}, u32[]{:S(2)}, u32[]{:S(2)}) collective-permute-start(bf16[16,6144]{1,0:T(8,128)(2,1)S(1)} %collective-permute-done.5), channel_id=1, source_target_pairs={{0,2},{1,5},{2,0},{3,7},{4,6},{5,1},{6,4},{7,3},{8,10},{9,13},{10,... | collective-permute-start | bytes 589832 | tf_op jit(solution)/shard_map/ppermute | solution.py:403
  22.8 2.1 %collective-permute-start.12 = (bf16[32,6144]{1,0:T(8,128)(2,1)S(1)}, bf16[32,6144]{1,0:T(8,128)(2,1)S(1)}, u32[]{:S(2)}, u32[]{:S(2)}) collective-permute-start(bf16[32,6144]{1,0:T(8,128)(2,1)S(1)} %constant_dynamic-update-slice_fusion.2.refs_5_), channel_id=1, source_target_pairs={{0,1},{1,0},{2,3},{3,2},{4,5},{5,4},{6,7},{7,6},{8,9},{9,8},{10,11... | collective-permute-start | bytes 1179656 | tf_op jit(solution)/shard_map/ppermute | solution.py:406
  25.1 1.1 %collective-permute-done.7 = bf16[16,6144]{1,0:T(8,128)(2,1)S(1)} collective-permute-done((bf16[16,6144]{1,0:T(8,128)(2,1)S(1)}, bf16[16,6144]{1,0:T(8,128)(2,1)S(1)}, u32[]{:S(2)}, u32[]{:S(2)}) %collective-permute-start.7) | collective-permute-done | bytes 196640 | tf_op jit(solution)/shard_map/ppermute | solution.py:403
  26.2 1.7 %collective-permute-start.8 = (bf16[32,6144]{1,0:T(8,128)(2,1)S(1)}, bf16[32,6144]{1,0:T(8,128)(2,1)S(1)}, u32[]{:S(2)}, u32[]{:S(2)}) collective-permute-start(bf16[32,6144]{1,0:T(8,128)(2,1)S(1)} %constant_dynamic-update-slice_fusion.refs_1_), channel_id=1, source_target_pairs={{0,4},{1,3},{2,6},{3,1},{4,0},{5,7},{6,2},{7,5},{8,12},{9,11},{10,... | collective-permute-start | bytes 1179656 | tf_op jit(solution)/shard_map/ppermute | solution.py:403
  27.9 2.0 %collective-permute-done.15 = bf16[16,6144]{1,0:T(8,128)(2,1)S(1)} collective-permute-done((bf16[16,6144]{1,0:T(8,128)(2,1)S(1)}, bf16[16,6144]{1,0:T(8,128)(2,1)S(1)}, u32[]{:S(2)}, u32[]{:S(2)}) %collective-permute-start.15) | collective-permute-done | bytes 196640 | tf_op jit(solution)/shard_map/ppermute | solution.py:403
  29.9 2.1 %collective-permute-start.3 = (bf16[32,6144]{1,0:T(8,128)(2,1)S(1)}, bf16[32,6144]{1,0:T(8,128)(2,1)S(1)}, u32[]{:S(2)}, u32[]{:S(2)}) collective-permute-start(bf16[32,6144]{1,0:T(8,128)(2,1)S(1)} %collective-permute-done.1.refs_1_), channel_id=1, source_target_pairs={{0,1},{1,0},{2,3},{3,2},{4,5},{5,4},{6,7},{7,6},{8,9},{9,8},{10,11... | collective-permute-start | bytes 1179656 | tf_op jit(solution)/shard_map/ppermute | solution.py:406
  32.0 1.7 %collective-permute-start.16 = (bf16[32,6144]{1,0:T(8,128)(2,1)S(1)}, bf16[32,6144]{1,0:T(8,128)(2,1)S(1)}, u32[]{:S(2)}, u32[]{:S(2)}) collective-permute-start(bf16[32,6144]{1,0:T(8,128)(2,1)S(1)} %constant_dynamic-update-slice_fusion.4.refs_9_), channel_id=1, source_target_pairs={{0,4},{1,3},{2,6},{3,1},{4,0},{5,7},{6,2},{7,5},{8,12},{9,11},{10,... | collective-permute-start | bytes 1179656 | tf_op jit(solution)/shard_map/ppermute | solution.py:403
  33.7 1.0 %copy-done = bf16[32,6144]{1,0:T(8,128)(2,1)S(1)} copy-done((bf16[32,6144]{1,0:T(8,128)(2,1)S(1)}, bf16[32,6144]{1,0:T(8,128)(2,1)}, u32[]{:S(2)}) %copy-start) | copy-done | bytes 393240
  34.7 1.7 %unpack.1.refs_0_ = bf16[128,4608]{1,0:T(8,128)(2,1)S(1)} custom-call(s32[10]{0:T(128)S(1)} %pad_add_fusion.numbers_ref, bf16[32,6144]{1,0:T(8,128)(2,1)S(1)} %copy-done, bf16[32,6144]{1,0:T(8,128)(2,1)S(1)} %collective-permute-done.1.refs_1_, bf16[32,6144]{1,0:T(8,128)(2,1)S(1)} %collective-permute-done.2.refs_2_, ...), custom_call_target="tpu_custom_call" | custom-call | flops 1000000000 | bytes 2359296 | tf_op jit(solution)/shard_map/unpack/pallas_call | solution.py:203
  36.4 0.7 %collective-permute-done.11.refs_6_ = bf16[32,6144]{1,0:T(8,128)(2,1)S(1)} collective-permute-done((bf16[32,6144]{1,0:T(8,128)(2,1)S(1)}, bf16[32,6144]{1,0:T(8,128)(2,1)S(1)}, u32[]{:S(2)}, u32[]{:S(2)}) %collective-permute-start.11) | collective-permute-done | bytes 393248 | tf_op jit(solution)/shard_map/ppermute | solution.py:403
  37.1 3.2 %collective-permute-start.17 = (bf16[32,6144]{1,0:T(8,128)(2,1)S(1)}, bf16[32,6144]{1,0:T(8,128)(2,1)S(1)}, u32[]{:S(2)}, u32[]{:S(2)}) collective-permute-start(bf16[32,6144]{1,0:T(8,128)(2,1)S(1)} %constant_dynamic-update-slice_fusion.4.refs_9_), channel_id=1, source_target_pairs={{0,1},{1,0},{2,3},{3,2},{4,5},{5,4},{6,7},{7,6},{8,9},{9,8},{10,11... | collective-permute-start | bytes 1179656 | tf_op jit(solution)/shard_map/ppermute | solution.py:406
  40.3 0.5 collective-permute-start.10
  40.9 0.8 %collective-permute-done.17.refs_11_ = bf16[32,6144]{1,0:T(8,128)(2,1)S(1)} collective-permute-done((bf16[32,6144]{1,0:T(8,128)(2,1)S(1)}, bf16[32,6144]{1,0:T(8,128)(2,1)S(1)}, u32[]{:S(2)}, u32[]{:S(2)}) %collective-permute-start.17) | collective-permute-done | bytes 393248 | tf_op jit(solution)/shard_map/ppermute | solution.py:406
  41.7 1.1 %collective-permute-done.10.refs_4_ = bf16[32,6144]{1,0:T(8,128)(2,1)S(1)} collective-permute-done((bf16[32,6144]{1,0:T(8,128)(2,1)S(1)}, bf16[32,6144]{1,0:T(8,128)(2,1)S(1)}, u32[]{:S(2)}, u32[]{:S(2)}) %collective-permute-start.10) | collective-permute-done | bytes 393248 | tf_op jit(solution)/shard_map/ppermute | solution.py:406
  42.8 0.6 collective-permute-done.18.refs_12_
  43.3 9.9 %contract.1 = (f32[256,1024]{1,0:T(8,128)S(1)}, f32[256,1024]{1,0:T(8,128)S(1)}) custom-call(s32[10]{0:T(128)S(1)} %pad_add_fusion.numbers_ref, bf16[128,4608]{1,0:T(8,128)(2,1)S(1)} %unpack.1.refs_0_, bf16[32,6144]{1,0:T(8,128)(2,1)S(1)} %constant_dynamic-update-slice_fusion.refs_1_, bf16[32,6144]{1,0:T(8,128)(2,1)S(1)} %collective-permute-done.8.refs_2_, ...), custom_call_target="tpu_custom_call" | custom-call | tf_op jit(solution)/shard_map/contract/pallas_call | solution.py:289
  53.3 0.4 collective-permute-start.19
  53.7 2.3 %collective-permute-done.19.got_ref = f32[256,1024]{1,0:T(8,128)S(1)} collective-permute-done((f32[256,1024]{1,0:T(8,128)S(1)}, f32[256,1024]{1,0:T(8,128)S(1)}, u32[]{:S(2)}, u32[]{:S(2)}) %collective-permute-start.19) | collective-permute-done | bytes 1048608 | tf_op jit(solution)/shard_map/ppermute | solution.py:406
  56.0 0.8 %add.5 = bf16[256,1024]{1,0:T(8,128)(2,1)} custom-call(f32[256,1024]{1,0:T(8,128)S(1)} %get-tuple-element.21.keep_ref, f32[256,1024]{1,0:T(8,128)S(1)} %collective-permute-done.19.got_ref), custom_call_target="tpu_custom_call" | custom-call | tf_op jit(solution)/shard_map/add/pallas_call | solution.py:334
  (22 shorter events, 0.3 us)
Async XLA Ops:
  1.9 5.0 %collective-permute-start = (bf16[16,6144]{1,0:T(8,128)(2,1)}, bf16[16,6144]{1,0:T(8,128)(2,1)S(1)}, u32[]{:S(2)}, u32[]{:S(2)}) collective-permute-start(bf16[16,6144]{1,0:T(8,128)(2,1)} %get-tuple-element.19), channel_id=1, source_target_pairs={{0,2},{1,5},{2,0},{3,7},{4,6},{5,1},{6,4},{7,3},{8,10},{9,13},{10,... | collective-permute-start | bytes 589832 | tf_op jit(solution)/shard_map/ppermute | solution.py:403
  3.2 7.2 %collective-permute-start.4 = (bf16[16,6144]{1,0:T(8,128)(2,1)}, bf16[16,6144]{1,0:T(8,128)(2,1)S(1)}, u32[]{:S(2)}, u32[]{:S(2)}) collective-permute-start(bf16[16,6144]{1,0:T(8,128)(2,1)} %get-tuple-element.19), channel_id=1, source_target_pairs={{0,8},{1,9},{2,10},{3,11},{4,12},{5,13},{6,14},{7,15},{8,24},{9,25... | collective-permute-start | bytes 589832 | tf_op jit(solution)/shard_map/ppermute | solution.py:403
  7.7 24.3 %collective-permute-start.2 = (bf16[32,6144]{1,0:T(8,128)(2,1)}, bf16[32,6144]{1,0:T(8,128)(2,1)S(1)}, u32[]{:S(2)}, u32[]{:S(2)}) collective-permute-start(bf16[32,6144]{1,0:T(8,128)(2,1)} %constant_dynamic-update-slice_fusion.6.refs_0_), channel_id=1, source_target_pairs={{0,1},{1,0},{2,3},{3,2},{4,5},{5,4},{6,7},{7,6},{8,9},{9,8},{10,11... | collective-permute-start | bytes 1179656 | tf_op jit(solution)/shard_map/ppermute | solution.py:406
  9.2 15.8 %collective-permute-start.1 = (bf16[32,6144]{1,0:T(8,128)(2,1)}, bf16[32,6144]{1,0:T(8,128)(2,1)S(1)}, u32[]{:S(2)}, u32[]{:S(2)}) collective-permute-start(bf16[32,6144]{1,0:T(8,128)(2,1)} %constant_dynamic-update-slice_fusion.6.refs_0_), channel_id=1, source_target_pairs={{0,4},{1,3},{2,6},{3,1},{4,0},{5,7},{6,2},{7,5},{8,12},{9,11},{10,... | collective-permute-start | bytes 1179656 | tf_op jit(solution)/shard_map/ppermute | solution.py:403
  10.4 6.6 %collective-permute-start.5 = (bf16[16,6144]{1,0:T(8,128)(2,1)S(1)}, bf16[16,6144]{1,0:T(8,128)(2,1)S(1)}, u32[]{:S(2)}, u32[]{:S(2)}) collective-permute-start(bf16[16,6144]{1,0:T(8,128)(2,1)S(1)} %collective-permute-done.4), channel_id=1, source_target_pairs={{0,8},{1,9},{2,10},{3,11},{4,12},{5,13},{6,14},{7,15},{8,24},{9,25... | collective-permute-start | bytes 589832 | tf_op jit(solution)/shard_map/ppermute | solution.py:403
  10.6 14.4 %collective-permute-start.14 = (bf16[16,6144]{1,0:T(8,128)(2,1)}, bf16[16,6144]{1,0:T(8,128)(2,1)S(1)}, u32[]{:S(2)}, u32[]{:S(2)}) collective-permute-start(bf16[16,6144]{1,0:T(8,128)(2,1)} %get-tuple-element.19), channel_id=1, source_target_pairs={{0,16},{1,17},{2,18},{3,19},{4,20},{5,21},{6,22},{7,23},{8,0},{9,1... | collective-permute-start | bytes 589832 | tf_op jit(solution)/shard_map/ppermute | solution.py:403
  12.8 6.1 %collective-permute-start.6 = (bf16[16,6144]{1,0:T(8,128)(2,1)S(1)}, bf16[16,6144]{1,0:T(8,128)(2,1)S(1)}, u32[]{:S(2)}, u32[]{:S(2)}) collective-permute-start(bf16[16,6144]{1,0:T(8,128)(2,1)S(1)} %collective-permute-done.4), channel_id=1, source_target_pairs={{0,2},{1,5},{2,0},{3,7},{4,6},{5,1},{6,4},{7,3},{8,10},{9,13},{10,... | collective-permute-start | bytes 589832 | tf_op jit(solution)/shard_map/ppermute | solution.py:403
  18.9 7.3 %collective-permute-start.7 = (bf16[16,6144]{1,0:T(8,128)(2,1)S(1)}, bf16[16,6144]{1,0:T(8,128)(2,1)S(1)}, u32[]{:S(2)}, u32[]{:S(2)}) collective-permute-start(bf16[16,6144]{1,0:T(8,128)(2,1)S(1)} %collective-permute-done.5), channel_id=1, source_target_pairs={{0,2},{1,5},{2,0},{3,7},{4,6},{5,1},{6,4},{7,3},{8,10},{9,13},{10,... | collective-permute-start | bytes 589832 | tf_op jit(solution)/shard_map/ppermute | solution.py:403
  22.8 17.5 %collective-permute-start.12 = (bf16[32,6144]{1,0:T(8,128)(2,1)S(1)}, bf16[32,6144]{1,0:T(8,128)(2,1)S(1)}, u32[]{:S(2)}, u32[]{:S(2)}) collective-permute-start(bf16[32,6144]{1,0:T(8,128)(2,1)S(1)} %constant_dynamic-update-slice_fusion.2.refs_5_), channel_id=1, source_target_pairs={{0,1},{1,0},{2,3},{3,2},{4,5},{5,4},{6,7},{7,6},{8,9},{9,8},{10,11... | collective-permute-start | bytes 1179656 | tf_op jit(solution)/shard_map/ppermute | solution.py:406
  25.0 4.9 %collective-permute-start.15 = (bf16[16,6144]{1,0:T(8,128)(2,1)S(1)}, bf16[16,6144]{1,0:T(8,128)(2,1)S(1)}, u32[]{:S(2)}, u32[]{:S(2)}) collective-permute-start(bf16[16,6144]{1,0:T(8,128)(2,1)S(1)} %collective-permute-done.14), channel_id=1, source_target_pairs={{0,2},{1,5},{2,0},{3,7},{4,6},{5,1},{6,4},{7,3},{8,10},{9,13},{10,... | collective-permute-start | bytes 589832 | tf_op jit(solution)/shard_map/ppermute | solution.py:403
  26.2 14.2 %collective-permute-start.8 = (bf16[32,6144]{1,0:T(8,128)(2,1)S(1)}, bf16[32,6144]{1,0:T(8,128)(2,1)S(1)}, u32[]{:S(2)}, u32[]{:S(2)}) collective-permute-start(bf16[32,6144]{1,0:T(8,128)(2,1)S(1)} %constant_dynamic-update-slice_fusion.refs_1_), channel_id=1, source_target_pairs={{0,4},{1,3},{2,6},{3,1},{4,0},{5,7},{6,2},{7,5},{8,12},{9,11},{10,... | collective-permute-start | bytes 1179656 | tf_op jit(solution)/shard_map/ppermute | solution.py:403
  27.9 9.2 %collective-permute-start.11 = (bf16[32,6144]{1,0:T(8,128)(2,1)S(1)}, bf16[32,6144]{1,0:T(8,128)(2,1)S(1)}, u32[]{:S(2)}, u32[]{:S(2)}) collective-permute-start(bf16[32,6144]{1,0:T(8,128)(2,1)S(1)} %collective-permute-done.1.refs_1_), channel_id=1, source_target_pairs={{0,8},{1,9},{2,10},{3,11},{4,12},{5,13},{6,14},{7,15},{8,24},{9,25... | collective-permute-start | bytes 1179656 | tf_op jit(solution)/shard_map/ppermute | solution.py:403
  29.9 3.8 %collective-permute-start.3 = (bf16[32,6144]{1,0:T(8,128)(2,1)S(1)}, bf16[32,6144]{1,0:T(8,128)(2,1)S(1)}, u32[]{:S(2)}, u32[]{:S(2)}) collective-permute-start(bf16[32,6144]{1,0:T(8,128)(2,1)S(1)} %collective-permute-done.1.refs_1_), channel_id=1, source_target_pairs={{0,1},{1,0},{2,3},{3,2},{4,5},{5,4},{6,7},{7,6},{8,9},{9,8},{10,11... | collective-permute-start | bytes 1179656 | tf_op jit(solution)/shard_map/ppermute | solution.py:406
  32.0 8.9 %collective-permute-start.16 = (bf16[32,6144]{1,0:T(8,128)(2,1)S(1)}, bf16[32,6144]{1,0:T(8,128)(2,1)S(1)}, u32[]{:S(2)}, u32[]{:S(2)}) collective-permute-start(bf16[32,6144]{1,0:T(8,128)(2,1)S(1)} %constant_dynamic-update-slice_fusion.4.refs_9_), channel_id=1, source_target_pairs={{0,4},{1,3},{2,6},{3,1},{4,0},{5,7},{6,2},{7,5},{8,12},{9,11},{10,... | collective-permute-start | bytes 1179656 | tf_op jit(solution)/shard_map/ppermute | solution.py:403
  33.7 7.2 %collective-permute-start.9 = (bf16[32,6144]{1,0:T(8,128)(2,1)S(1)}, bf16[32,6144]{1,0:T(8,128)(2,1)S(1)}, u32[]{:S(2)}, u32[]{:S(2)}) collective-permute-start(bf16[32,6144]{1,0:T(8,128)(2,1)S(1)} %constant_dynamic-update-slice_fusion.refs_1_), channel_id=1, source_target_pairs={{0,1},{1,0},{2,3},{3,2},{4,5},{5,4},{6,7},{7,6},{8,9},{9,8},{10,11... | collective-permute-start | bytes 1179656 | tf_op jit(solution)/shard_map/ppermute | solution.py:406
  33.7 1.0 %copy-start = (bf16[32,6144]{1,0:T(8,128)(2,1)S(1)}, bf16[32,6144]{1,0:T(8,128)(2,1)}, u32[]{:S(2)}) copy-start(bf16[32,6144]{1,0:T(8,128)(2,1)} %constant_dynamic-update-slice_fusion.6.refs_0_) | copy-start | bytes 1179652
  37.1 4.5 %collective-permute-start.17 = (bf16[32,6144]{1,0:T(8,128)(2,1)S(1)}, bf16[32,6144]{1,0:T(8,128)(2,1)S(1)}, u32[]{:S(2)}, u32[]{:S(2)}) collective-permute-start(bf16[32,6144]{1,0:T(8,128)(2,1)S(1)} %constant_dynamic-update-slice_fusion.4.refs_9_), channel_id=1, source_target_pairs={{0,1},{1,0},{2,3},{3,2},{4,5},{5,4},{6,7},{7,6},{8,9},{9,8},{10,11... | collective-permute-start | bytes 1179656 | tf_op jit(solution)/shard_map/ppermute | solution.py:406
  40.3 2.5 %collective-permute-start.13 = (bf16[32,6144]{1,0:T(8,128)(2,1)S(1)}, bf16[32,6144]{1,0:T(8,128)(2,1)S(1)}, u32[]{:S(2)}, u32[]{:S(2)}) collective-permute-start(bf16[32,6144]{1,0:T(8,128)(2,1)S(1)} %collective-permute-done.11.refs_6_), channel_id=1, source_target_pairs={{0,1},{1,0},{2,3},{3,2},{4,5},{5,4},{6,7},{7,6},{8,9},{9,8},{10,11... | collective-permute-start | bytes 1179656 | tf_op jit(solution)/shard_map/ppermute | solution.py:406
  40.3 2.5 %collective-permute-start.10 = (bf16[32,6144]{1,0:T(8,128)(2,1)S(1)}, bf16[32,6144]{1,0:T(8,128)(2,1)S(1)}, u32[]{:S(2)}, u32[]{:S(2)}) collective-permute-start(bf16[32,6144]{1,0:T(8,128)(2,1)S(1)} %collective-permute-done.8.refs_2_), channel_id=1, source_target_pairs={{0,1},{1,0},{2,3},{3,2},{4,5},{5,4},{6,7},{7,6},{8,9},{9,8},{10,11... | collective-permute-start | bytes 1179656 | tf_op jit(solution)/shard_map/ppermute | solution.py:406
  40.8 2.5 %collective-permute-start.18 = (bf16[32,6144]{1,0:T(8,128)(2,1)S(1)}, bf16[32,6144]{1,0:T(8,128)(2,1)S(1)}, u32[]{:S(2)}, u32[]{:S(2)}) collective-permute-start(bf16[32,6144]{1,0:T(8,128)(2,1)S(1)} %collective-permute-done.16.refs_10_), channel_id=1, source_target_pairs={{0,1},{1,0},{2,3},{3,2},{4,5},{5,4},{6,7},{7,6},{8,9},{9,8},{10,11... | collective-permute-start | bytes 1179656 | tf_op jit(solution)/shard_map/ppermute | solution.py:406
  53.3 2.7 %collective-permute-start.19 = (f32[256,1024]{1,0:T(8,128)S(1)}, f32[256,1024]{1,0:T(8,128)S(1)}, u32[]{:S(2)}, u32[]{:S(2)}) collective-permute-start(f32[256,1024]{1,0:T(8,128)S(1)} %get-tuple-element.22), channel_id=1, source_target_pairs={{0,1},{1,0},{2,3},{3,2},{4,5},{5,4},{6,7},{7,6},{8,9},{9,8},{10,11... | collective-permute-start | bytes 3145736 | tf_op jit(solution)/shard_map/ppermute | solution.py:406

commit v5 on v4

--- a/solution.py
+++ b/solution.py
@@ -89,7 +89,7 @@
         functools.partial(pack_kernel, nirrep, cw),
         out_shape=(
             jax.ShapeDtypeStruct((rows, nirrep * cw * LANES), dtype),
-            jax.ShapeDtypeStruct((2 * rows, nirrep * cw * LANES), dtype),
+            pltpu.VMEM((2 * rows, nirrep * cw * LANES), dtype),
         ),
         in_specs=[
             pl.BlockSpec(memory_space=pltpu.SMEM),
@@ -99,6 +99,7 @@
             pl.BlockSpec(memory_space=pltpu.VMEM),
             pl.BlockSpec(memory_space=pltpu.VMEM),
         ),
+        compiler_params=pltpu.CompilerParams(vmem_limit_bytes=48 * 2**20),
         name="pack",
     )(block_sizes, amplitudes)
 

time: 57 us -> 57.3 us (level)
  Pallas kernels: 14.4 us -> 13.1 us
  starting transfers between devices: 23.6 us -> 24.9 us
  waiting for transfers between devices: 16.3 us -> 17.2 us
  other arithmetic: 0.73 us -> 0.08 us
    ppermute x9, starting transfers between devices: 9.94 us -> 12.7 us  [swap_cores(): return lax.ppermute(value, 'con', [(0, 1), (1, 0)])]
    ppermute x11, starting transfers between devices: 13.6 us -> 12.2 us  [move(): return lax.ppermute(value, ('out', 'con'), pairs)]
    pallas_call x1, Pallas kernels: 1.94 us -> 0.7 us  [pack(): pl.pallas_call(functools.partial(pack_kernel, nirrep, cw), out_shape=(jax...]
    ppermute x11, waiting for transfers between devices: 11.6 us -> 12.5 us  [move(): return lax.ppermute(value, ('out', 'con'), pairs)]
    dynamic_update_slice x1, local copies, waits for them, and re-layouts: 0.69 us -> 0.01 us  [get(): arrays[names] = lax.dynamic_update_slice(own_top, two, (ROWS, 0))]
    concatenate x1, other arithmetic: 0.73 us -> 0.08 us  [ladder_of_16(): numbers = jnp.concatenate([block_sizes, here])]
    unnamed x5 -> x7, local copies, waits for them, and re-layouts: 1.04 us -> 1.66 us
  transfers between devices with their start and end apart: 20 -> 20, of which waited for: 10 -> 9; matrix products, arithmetic and copies ran while one was open for 3% -> 0% of each run, Pallas kernels for 3% -> 3%
where the time goes in v5:
time: 57.3 us; the launch traced here: 57.1 us
  starting transfers between devices  24.9 us (43%)
  waiting for transfers between devices  17.2 us (30%)
  Pallas kernels  13.1 us (23%)
  local copies, waits for them, and re-layouts  1.71 us (3%)
    ppermute x9, starting transfers between devices, swap_cores(): return lax.ppermute(value, 'con', [(0, 1), (1, 0)])  12.7 us
    ppermute x11, waiting for transfers between devices, move(): return lax.ppermute(value, ('out', 'con'), pairs)  12.5 us
    ppermute x11, starting transfers between devices, move(): return lax.ppermute(value, ('out', 'con'), pairs)  12.2 us
    pallas_call x1, Pallas kernels, contract(): pl.pallas_call(functools.partial(contract_kernel, cw, nirrep, tuple(ready...  9.92 us
    ppermute x9, waiting for transfers between devices, swap_cores(): return lax.ppermute(value, 'con', [(0, 1), (1, 0)])  4.74 us
    pallas_call x1, Pallas kernels, unpack(): pl.pallas_call(functools.partial(unpack_kernel, cw, nirrep), out_shape=pl...  1.66 us
    unnamed x7, local copies, waits for them, and re-layouts  1.66 us
  transfers between devices with their start and end apart: 20, of which 9 were waited for; matrix products, arithmetic and copies ran while one was open for 0% of the time, Pallas kernels for 3%

profile of v5, /device:TPU:25, one launch (start us, length us, event | category | flops | bytes accessed | tf_op | source)
XLA Modules:
  0.0 57.1 jit_solution(16144581556271296898)
XLA Ops:
  0.0 1.0 %copy-done = bf16[16,9216]{1,0:T(8,128)(2,1)S(1)} copy-done((bf16[16,9216]{1,0:T(8,128)(2,1)S(1)}, bf16[16,9216]{1,0:T(8,128)(2,1)}, u32[]{:S(2)}) %copy-start) | copy-done | bytes 294936
  1.0 0.7 %copy-done.1 = s32[8]{0:T(128)S(1)} copy-done((s32[8]{0:T(128)S(1)}, s32[8]{0:T(128)}, u32[]{:S(2)}) %copy-start.1) | copy-done | bytes 56
  1.6 0.7 %pack.1 = (bf16[16,6144]{1,0:T(8,128)(2,1)S(1)}, bf16[32,6144]{1,0:T(8,128)(2,1)S(1)}) custom-call(s32[8]{0:T(128)S(1)} %copy-done.1, bf16[16,9216]{1,0:T(8,128)(2,1)S(1)} %copy-done), custom_call_target="tpu_custom_call" | custom-call | tf_op jit(solution)/shard_map/pack/pallas_call | solution.py:88
  2.3 1.3 %collective-permute-start = (bf16[16,6144]{1,0:T(8,128)(2,1)S(1)}, bf16[16,6144]{1,0:T(8,128)(2,1)S(1)}, u32[]{:S(2)}, u32[]{:S(2)}) collective-permute-start(bf16[16,6144]{1,0:T(8,128)(2,1)S(1)} %get-tuple-element.19), channel_id=1, source_target_pairs={{0,2},{1,5},{2,0},{3,7},{4,6},{5,1},{6,4},{7,3},{8,10},{9,13},{10,... | collective-permute-start | bytes 589832 | tf_op jit(solution)/shard_map/ppermute | solution.py:404
  3.6 0.2 collective-permute-start.4
  3.8 0.1 pad_add_fusion.numbers_ref
  3.9 3.3 %collective-permute-done = bf16[16,6144]{1,0:T(8,128)(2,1)S(1)} collective-permute-done((bf16[16,6144]{1,0:T(8,128)(2,1)S(1)}, bf16[16,6144]{1,0:T(8,128)(2,1)S(1)}, u32[]{:S(2)}, u32[]{:S(2)}) %collective-permute-start) | collective-permute-done | bytes 196640 | tf_op jit(solution)/shard_map/ppermute | solution.py:404
  7.2 1.6 %collective-permute-start.2 = (bf16[32,6144]{1,0:T(8,128)(2,1)S(1)}, bf16[32,6144]{1,0:T(8,128)(2,1)S(1)}, u32[]{:S(2)}, u32[]{:S(2)}) collective-permute-start(bf16[32,6144]{1,0:T(8,128)(2,1)S(1)} %constant_dynamic-update-slice_fusion.6.refs_0_), channel_id=1, source_target_pairs={{0,1},{1,0},{2,3},{3,2},{4,5},{5,4},{6,7},{7,6},{8,9},{9,8},{10,11... | collective-permute-start | bytes 1179656 | tf_op jit(solution)/shard_map/ppermute | solution.py:407
  8.8 1.2 %collective-permute-start.1 = (bf16[32,6144]{1,0:T(8,128)(2,1)S(1)}, bf16[32,6144]{1,0:T(8,128)(2,1)S(1)}, u32[]{:S(2)}, u32[]{:S(2)}) collective-permute-start(bf16[32,6144]{1,0:T(8,128)(2,1)S(1)} %constant_dynamic-update-slice_fusion.6.refs_0_), channel_id=1, source_target_pairs={{0,4},{1,3},{2,6},{3,1},{4,0},{5,7},{6,2},{7,5},{8,12},{9,11},{10,... | collective-permute-start | bytes 1179656 | tf_op jit(solution)/shard_map/ppermute | solution.py:404
  10.0 0.2 collective-permute-start.5
  10.2 2.2 %collective-permute-start.14 = (bf16[16,6144]{1,0:T(8,128)(2,1)S(1)}, bf16[16,6144]{1,0:T(8,128)(2,1)S(1)}, u32[]{:S(2)}, u32[]{:S(2)}) collective-permute-start(bf16[16,6144]{1,0:T(8,128)(2,1)S(1)} %get-tuple-element.19), channel_id=1, source_target_pairs={{0,16},{1,17},{2,18},{3,19},{4,20},{5,21},{6,22},{7,23},{8,0},{9,1... | collective-permute-start | bytes 589832 | tf_op jit(solution)/shard_map/ppermute | solution.py:404
  12.4 1.2 %collective-permute-start.6 = (bf16[16,6144]{1,0:T(8,128)(2,1)S(1)}, bf16[16,6144]{1,0:T(8,128)(2,1)S(1)}, u32[]{:S(2)}, u32[]{:S(2)}) collective-permute-start(bf16[16,6144]{1,0:T(8,128)(2,1)S(1)} %collective-permute-done.4), channel_id=1, source_target_pairs={{0,2},{1,5},{2,0},{3,7},{4,6},{5,1},{6,4},{7,3},{8,10},{9,13},{10,... | collective-permute-start | bytes 589832 | tf_op jit(solution)/shard_map/ppermute | solution.py:404
  13.7 3.1 %collective-permute-done.5 = bf16[16,6144]{1,0:T(8,128)(2,1)S(1)} collective-permute-done((bf16[16,6144]{1,0:T(8,128)(2,1)S(1)}, bf16[16,6144]{1,0:T(8,128)(2,1)S(1)}, u32[]{:S(2)}, u32[]{:S(2)}) %collective-permute-start.5) | collective-permute-done | bytes 196640 | tf_op jit(solution)/shard_map/ppermute | solution.py:404
  16.7 1.6 %collective-permute-done.6 = bf16[16,6144]{1,0:T(8,128)(2,1)S(1)} collective-permute-done((bf16[16,6144]{1,0:T(8,128)(2,1)S(1)}, bf16[16,6144]{1,0:T(8,128)(2,1)S(1)}, u32[]{:S(2)}, u32[]{:S(2)}) %collective-permute-start.6) | collective-permute-done | bytes 196640 | tf_op jit(solution)/shard_map/ppermute | solution.py:404
  18.4 1.2 %collective-permute-start.7 = (bf16[16,6144]{1,0:T(8,128)(2,1)S(1)}, bf16[16,6144]{1,0:T(8,128)(2,1)S(1)}, u32[]{:S(2)}, u32[]{:S(2)}) collective-permute-start(bf16[16,6144]{1,0:T(8,128)(2,1)S(1)} %collective-permute-done.5), channel_id=1, source_target_pairs={{0,2},{1,5},{2,0},{3,7},{4,6},{5,1},{6,4},{7,3},{8,10},{9,13},{10,... | collective-permute-start | bytes 589832 | tf_op jit(solution)/shard_map/ppermute | solution.py:404
  19.6 5.5 %collective-permute-start.12 = (bf16[32,6144]{1,0:T(8,128)(2,1)S(1)}, bf16[32,6144]{1,0:T(8,128)(2,1)S(1)}, u32[]{:S(2)}, u32[]{:S(2)}) collective-permute-start(bf16[32,6144]{1,0:T(8,128)(2,1)S(1)} %constant_dynamic-update-slice_fusion.2.refs_5_), channel_id=1, source_target_pairs={{0,1},{1,0},{2,3},{3,2},{4,5},{5,4},{6,7},{7,6},{8,9},{9,8},{10,11... | collective-permute-start | bytes 1179656 | tf_op jit(solution)/shard_map/ppermute | solution.py:407
  25.2 0.1 collective-permute-start.15
  25.3 2.8 %collective-permute-start.8 = (bf16[32,6144]{1,0:T(8,128)(2,1)S(1)}, bf16[32,6144]{1,0:T(8,128)(2,1)S(1)}, u32[]{:S(2)}, u32[]{:S(2)}) collective-permute-start(bf16[32,6144]{1,0:T(8,128)(2,1)S(1)} %constant_dynamic-update-slice_fusion.refs_1_), channel_id=1, source_target_pairs={{0,4},{1,3},{2,6},{3,1},{4,0},{5,7},{6,2},{7,5},{8,12},{9,11},{10,... | collective-permute-start | bytes 1179656 | tf_op jit(solution)/shard_map/ppermute | solution.py:404
  28.2 1.9 %collective-permute-done.15 = bf16[16,6144]{1,0:T(8,128)(2,1)S(1)} collective-permute-done((bf16[16,6144]{1,0:T(8,128)(2,1)S(1)}, bf16[16,6144]{1,0:T(8,128)(2,1)S(1)}, u32[]{:S(2)}, u32[]{:S(2)}) %collective-permute-start.15) | collective-permute-done | bytes 196640 | tf_op jit(solution)/shard_map/ppermute | solution.py:404
  30.1 2.0 %collective-permute-start.3 = (bf16[32,6144]{1,0:T(8,128)(2,1)S(1)}, bf16[32,6144]{1,0:T(8,128)(2,1)S(1)}, u32[]{:S(2)}, u32[]{:S(2)}) collective-permute-start(bf16[32,6144]{1,0:T(8,128)(2,1)S(1)} %collective-permute-done.1.refs_1_), channel_id=1, source_target_pairs={{0,1},{1,0},{2,3},{3,2},{4,5},{5,4},{6,7},{7,6},{8,9},{9,8},{10,11... | collective-permute-start | bytes 1179656 | tf_op jit(solution)/shard_map/ppermute | solution.py:407
  32.1 1.7 %collective-permute-start.16 = (bf16[32,6144]{1,0:T(8,128)(2,1)S(1)}, bf16[32,6144]{1,0:T(8,128)(2,1)S(1)}, u32[]{:S(2)}, u32[]{:S(2)}) collective-permute-start(bf16[32,6144]{1,0:T(8,128)(2,1)S(1)} %constant_dynamic-update-slice_fusion.4.refs_9_), channel_id=1, source_target_pairs={{0,4},{1,3},{2,6},{3,1},{4,0},{5,7},{6,2},{7,5},{8,12},{9,11},{10,... | collective-permute-start | bytes 1179656 | tf_op jit(solution)/shard_map/ppermute | solution.py:404
  33.9 1.7 %unpack.1.refs_0_ = bf16[128,4608]{1,0:T(8,128)(2,1)S(1)} custom-call(s32[10]{0:T(128)S(1)} %pad_add_fusion.numbers_ref, bf16[32,6144]{1,0:T(8,128)(2,1)S(1)} %constant_dynamic-update-slice_fusion.6.refs_0_, bf16[32,6144]{1,0:T(8,128)(2,1)S(1)} %collective-permute-done.1.refs_1_, bf16[32,6144]{1,0:T(8,128)(2,1)S(1)} %collective-permute-done.2.refs_2_, ...), custom_call_target="tpu_custom_call" | custom-call | flops 1000000000 | bytes 2359296 | tf_op jit(solution)/shard_map/unpack/pallas_call | solution.py:204
  35.6 2.5 %collective-permute-done.11.refs_6_ = bf16[32,6144]{1,0:T(8,128)(2,1)S(1)} collective-permute-done((bf16[32,6144]{1,0:T(8,128)(2,1)S(1)}, bf16[32,6144]{1,0:T(8,128)(2,1)S(1)}, u32[]{:S(2)}, u32[]{:S(2)}) %collective-permute-start.11) | collective-permute-done | bytes 393248 | tf_op jit(solution)/shard_map/ppermute | solution.py:404
  38.1 2.5 %collective-permute-start.17 = (bf16[32,6144]{1,0:T(8,128)(2,1)S(1)}, bf16[32,6144]{1,0:T(8,128)(2,1)S(1)}, u32[]{:S(2)}, u32[]{:S(2)}) collective-permute-start(bf16[32,6144]{1,0:T(8,128)(2,1)S(1)} %constant_dynamic-update-slice_fusion.4.refs_9_), channel_id=1, source_target_pairs={{0,1},{1,0},{2,3},{3,2},{4,5},{5,4},{6,7},{7,6},{8,9},{9,8},{10,11... | collective-permute-start | bytes 1179656 | tf_op jit(solution)/shard_map/ppermute | solution.py:407
  40.6 0.5 collective-permute-start.10
  41.2 0.8 %collective-permute-done.17.refs_11_ = bf16[32,6144]{1,0:T(8,128)(2,1)S(1)} collective-permute-done((bf16[32,6144]{1,0:T(8,128)(2,1)S(1)}, bf16[32,6144]{1,0:T(8,128)(2,1)S(1)}, u32[]{:S(2)}, u32[]{:S(2)}) %collective-permute-start.17) | collective-permute-done | bytes 393248 | tf_op jit(solution)/shard_map/ppermute | solution.py:407
  42.0 1.1 %collective-permute-done.10.refs_4_ = bf16[32,6144]{1,0:T(8,128)(2,1)S(1)} collective-permute-done((bf16[32,6144]{1,0:T(8,128)(2,1)S(1)}, bf16[32,6144]{1,0:T(8,128)(2,1)S(1)}, u32[]{:S(2)}, u32[]{:S(2)}) %collective-permute-start.10) | collective-permute-done | bytes 393248 | tf_op jit(solution)/shard_map/ppermute | solution.py:407
  43.1 0.6 collective-permute-done.18.refs_12_
  43.6 9.9 %contract.1 = (f32[256,1024]{1,0:T(8,128)S(1)}, f32[256,1024]{1,0:T(8,128)S(1)}) custom-call(s32[10]{0:T(128)S(1)} %pad_add_fusion.numbers_ref, bf16[128,4608]{1,0:T(8,128)(2,1)S(1)} %unpack.1.refs_0_, bf16[32,6144]{1,0:T(8,128)(2,1)S(1)} %constant_dynamic-update-slice_fusion.refs_1_, bf16[32,6144]{1,0:T(8,128)(2,1)S(1)} %collective-permute-done.8.refs_2_, ...), custom_call_target="tpu_custom_call" | custom-call | tf_op jit(solution)/shard_map/contract/pallas_call | solution.py:290
  53.6 0.4 collective-permute-start.19
  54.0 2.3 %collective-permute-done.19.got_ref = f32[256,1024]{1,0:T(8,128)S(1)} collective-permute-done((f32[256,1024]{1,0:T(8,128)S(1)}, f32[256,1024]{1,0:T(8,128)S(1)}, u32[]{:S(2)}, u32[]{:S(2)}) %collective-permute-start.19) | collective-permute-done | bytes 1048608 | tf_op jit(solution)/shard_map/ppermute | solution.py:407
  56.3 0.8 %add.5 = bf16[256,1024]{1,0:T(8,128)(2,1)} custom-call(f32[256,1024]{1,0:T(8,128)S(1)} %get-tuple-element.21.keep_ref, f32[256,1024]{1,0:T(8,128)S(1)} %collective-permute-done.19.got_ref), custom_call_target="tpu_custom_call" | custom-call | tf_op jit(solution)/shard_map/add/pallas_call | solution.py:335
  (24 shorter events, 0.2 us)
Async XLA Ops:
  0.0 1.0 %copy-start = (bf16[16,9216]{1,0:T(8,128)(2,1)S(1)}, bf16[16,9216]{1,0:T(8,128)(2,1)}, u32[]{:S(2)}) copy-start(bf16[16,9216]{1,0:T(8,128)(2,1)} %amp_ref.1) | copy-start | bytes 884740
  1.0 0.7 %copy-start.1 = (s32[8]{0:T(128)S(1)}, s32[8]{0:T(128)}, u32[]{:S(2)}) copy-start(s32[8]{0:T(128)} %sizes_ref.1) | copy-start | bytes 100
  2.3 4.9 %collective-permute-start = (bf16[16,6144]{1,0:T(8,128)(2,1)S(1)}, bf16[16,6144]{1,0:T(8,128)(2,1)S(1)}, u32[]{:S(2)}, u32[]{:S(2)}) collective-permute-start(bf16[16,6144]{1,0:T(8,128)(2,1)S(1)} %get-tuple-element.19), channel_id=1, source_target_pairs={{0,2},{1,5},{2,0},{3,7},{4,6},{5,1},{6,4},{7,3},{8,10},{9,13},{10,... | collective-permute-start | bytes 589832 | tf_op jit(solution)/shard_map/ppermute | solution.py:404
  3.6 6.4 %collective-permute-start.4 = (bf16[16,6144]{1,0:T(8,128)(2,1)S(1)}, bf16[16,6144]{1,0:T(8,128)(2,1)S(1)}, u32[]{:S(2)}, u32[]{:S(2)}) collective-permute-start(bf16[16,6144]{1,0:T(8,128)(2,1)S(1)} %get-tuple-element.19), channel_id=1, source_target_pairs={{0,8},{1,9},{2,10},{3,11},{4,12},{5,13},{6,14},{7,15},{8,24},{9,25... | collective-permute-start | bytes 589832 | tf_op jit(solution)/shard_map/ppermute | solution.py:404
  7.2 24.9 %collective-permute-start.2 = (bf16[32,6144]{1,0:T(8,128)(2,1)S(1)}, bf16[32,6144]{1,0:T(8,128)(2,1)S(1)}, u32[]{:S(2)}, u32[]{:S(2)}) collective-permute-start(bf16[32,6144]{1,0:T(8,128)(2,1)S(1)} %constant_dynamic-update-slice_fusion.6.refs_0_), channel_id=1, source_target_pairs={{0,1},{1,0},{2,3},{3,2},{4,5},{5,4},{6,7},{7,6},{8,9},{9,8},{10,11... | collective-permute-start | bytes 1179656 | tf_op jit(solution)/shard_map/ppermute | solution.py:407
  8.8 16.4 %collective-permute-start.1 = (bf16[32,6144]{1,0:T(8,128)(2,1)S(1)}, bf16[32,6144]{1,0:T(8,128)(2,1)S(1)}, u32[]{:S(2)}, u32[]{:S(2)}) collective-permute-start(bf16[32,6144]{1,0:T(8,128)(2,1)S(1)} %constant_dynamic-update-slice_fusion.6.refs_0_), channel_id=1, source_target_pairs={{0,4},{1,3},{2,6},{3,1},{4,0},{5,7},{6,2},{7,5},{8,12},{9,11},{10,... | collective-permute-start | bytes 1179656 | tf_op jit(solution)/shard_map/ppermute | solution.py:404
  10.0 6.7 %collective-permute-start.5 = (bf16[16,6144]{1,0:T(8,128)(2,1)S(1)}, bf16[16,6144]{1,0:T(8,128)(2,1)S(1)}, u32[]{:S(2)}, u32[]{:S(2)}) collective-permute-start(bf16[16,6144]{1,0:T(8,128)(2,1)S(1)} %collective-permute-done.4), channel_id=1, source_target_pairs={{0,8},{1,9},{2,10},{3,11},{4,12},{5,13},{6,14},{7,15},{8,24},{9,25... | collective-permute-start | bytes 589832 | tf_op jit(solution)/shard_map/ppermute | solution.py:404
  10.2 15.0 %collective-permute-start.14 = (bf16[16,6144]{1,0:T(8,128)(2,1)S(1)}, bf16[16,6144]{1,0:T(8,128)(2,1)S(1)}, u32[]{:S(2)}, u32[]{:S(2)}) collective-permute-start(bf16[16,6144]{1,0:T(8,128)(2,1)S(1)} %get-tuple-element.19), channel_id=1, source_target_pairs={{0,16},{1,17},{2,18},{3,19},{4,20},{5,21},{6,22},{7,23},{8,0},{9,1... | collective-permute-start | bytes 589832 | tf_op jit(solution)/shard_map/ppermute | solution.py:404
  12.4 6.0 %collective-permute-start.6 = (bf16[16,6144]{1,0:T(8,128)(2,1)S(1)}, bf16[16,6144]{1,0:T(8,128)(2,1)S(1)}, u32[]{:S(2)}, u32[]{:S(2)}) collective-permute-start(bf16[16,6144]{1,0:T(8,128)(2,1)S(1)} %collective-permute-done.4), channel_id=1, source_target_pairs={{0,2},{1,5},{2,0},{3,7},{4,6},{5,1},{6,4},{7,3},{8,10},{9,13},{10,... | collective-permute-start | bytes 589832 | tf_op jit(solution)/shard_map/ppermute | solution.py:404
  18.4 6.9 %collective-permute-start.7 = (bf16[16,6144]{1,0:T(8,128)(2,1)S(1)}, bf16[16,6144]{1,0:T(8,128)(2,1)S(1)}, u32[]{:S(2)}, u32[]{:S(2)}) collective-permute-start(bf16[16,6144]{1,0:T(8,128)(2,1)S(1)} %collective-permute-done.5), channel_id=1, source_target_pairs={{0,2},{1,5},{2,0},{3,7},{4,6},{5,1},{6,4},{7,3},{8,10},{9,13},{10,... | collective-permute-start | bytes 589832 | tf_op jit(solution)/shard_map/ppermute | solution.py:404
  19.6 21.0 %collective-permute-start.12 = (bf16[32,6144]{1,0:T(8,128)(2,1)S(1)}, bf16[32,6144]{1,0:T(8,128)(2,1)S(1)}, u32[]{:S(2)}, u32[]{:S(2)}) collective-permute-start(bf16[32,6144]{1,0:T(8,128)(2,1)S(1)} %constant_dynamic-update-slice_fusion.2.refs_5_), channel_id=1, source_target_pairs={{0,1},{1,0},{2,3},{3,2},{4,5},{5,4},{6,7},{7,6},{8,9},{9,8},{10,11... | collective-permute-start | bytes 1179656 | tf_op jit(solution)/shard_map/ppermute | solution.py:407
  25.2 4.9 %collective-permute-start.15 = (bf16[16,6144]{1,0:T(8,128)(2,1)S(1)}, bf16[16,6144]{1,0:T(8,128)(2,1)S(1)}, u32[]{:S(2)}, u32[]{:S(2)}) collective-permute-start(bf16[16,6144]{1,0:T(8,128)(2,1)S(1)} %collective-permute-done.14), channel_id=1, source_target_pairs={{0,2},{1,5},{2,0},{3,7},{4,6},{5,1},{6,4},{7,3},{8,10},{9,13},{10,... | collective-permute-start | bytes 589832 | tf_op jit(solution)/shard_map/ppermute | solution.py:404
  25.3 15.3 %collective-permute-start.8 = (bf16[32,6144]{1,0:T(8,128)(2,1)S(1)}, bf16[32,6144]{1,0:T(8,128)(2,1)S(1)}, u32[]{:S(2)}, u32[]{:S(2)}) collective-permute-start(bf16[32,6144]{1,0:T(8,128)(2,1)S(1)} %constant_dynamic-update-slice_fusion.refs_1_), channel_id=1, source_target_pairs={{0,4},{1,3},{2,6},{3,1},{4,0},{5,7},{6,2},{7,5},{8,12},{9,11},{10,... | collective-permute-start | bytes 1179656 | tf_op jit(solution)/shard_map/ppermute | solution.py:404
  28.2 9.9 %collective-permute-start.11 = (bf16[32,6144]{1,0:T(8,128)(2,1)S(1)}, bf16[32,6144]{1,0:T(8,128)(2,1)S(1)}, u32[]{:S(2)}, u32[]{:S(2)}) collective-permute-start(bf16[32,6144]{1,0:T(8,128)(2,1)S(1)} %collective-permute-done.1.refs_1_), channel_id=1, source_target_pairs={{0,8},{1,9},{2,10},{3,11},{4,12},{5,13},{6,14},{7,15},{8,24},{9,25... | collective-permute-start | bytes 1179656 | tf_op jit(solution)/shard_map/ppermute | solution.py:404
  30.1 3.8 %collective-permute-start.3 = (bf16[32,6144]{1,0:T(8,128)(2,1)S(1)}, bf16[32,6144]{1,0:T(8,128)(2,1)S(1)}, u32[]{:S(2)}, u32[]{:S(2)}) collective-permute-start(bf16[32,6144]{1,0:T(8,128)(2,1)S(1)} %collective-permute-done.1.refs_1_), channel_id=1, source_target_pairs={{0,1},{1,0},{2,3},{3,2},{4,5},{5,4},{6,7},{7,6},{8,9},{9,8},{10,11... | collective-permute-start | bytes 1179656 | tf_op jit(solution)/shard_map/ppermute | solution.py:407
  32.1 9.0 %collective-permute-start.16 = (bf16[32,6144]{1,0:T(8,128)(2,1)S(1)}, bf16[32,6144]{1,0:T(8,128)(2,1)S(1)}, u32[]{:S(2)}, u32[]{:S(2)}) collective-permute-start(bf16[32,6144]{1,0:T(8,128)(2,1)S(1)} %constant_dynamic-update-slice_fusion.4.refs_9_), channel_id=1, source_target_pairs={{0,4},{1,3},{2,6},{3,1},{4,0},{5,7},{6,2},{7,5},{8,12},{9,11},{10,... | collective-permute-start | bytes 1179656 | tf_op jit(solution)/shard_map/ppermute | solution.py:404
  33.9 7.3 %collective-permute-start.9 = (bf16[32,6144]{1,0:T(8,128)(2,1)S(1)}, bf16[32,6144]{1,0:T(8,128)(2,1)S(1)}, u32[]{:S(2)}, u32[]{:S(2)}) collective-permute-start(bf16[32,6144]{1,0:T(8,128)(2,1)S(1)} %constant_dynamic-update-slice_fusion.refs_1_), channel_id=1, source_target_pairs={{0,1},{1,0},{2,3},{3,2},{4,5},{5,4},{6,7},{7,6},{8,9},{9,8},{10,11... | collective-permute-start | bytes 1179656 | tf_op jit(solution)/shard_map/ppermute | solution.py:407
  38.1 3.9 %collective-permute-start.17 = (bf16[32,6144]{1,0:T(8,128)(2,1)S(1)}, bf16[32,6144]{1,0:T(8,128)(2,1)S(1)}, u32[]{:S(2)}, u32[]{:S(2)}) collective-permute-start(bf16[32,6144]{1,0:T(8,128)(2,1)S(1)} %constant_dynamic-update-slice_fusion.4.refs_9_), channel_id=1, source_target_pairs={{0,1},{1,0},{2,3},{3,2},{4,5},{5,4},{6,7},{7,6},{8,9},{9,8},{10,11... | collective-permute-start | bytes 1179656 | tf_op jit(solution)/shard_map/ppermute | solution.py:407
  40.6 2.5 %collective-permute-start.13 = (bf16[32,6144]{1,0:T(8,128)(2,1)S(1)}, bf16[32,6144]{1,0:T(8,128)(2,1)S(1)}, u32[]{:S(2)}, u32[]{:S(2)}) collective-permute-start(bf16[32,6144]{1,0:T(8,128)(2,1)S(1)} %collective-permute-done.11.refs_6_), channel_id=1, source_target_pairs={{0,1},{1,0},{2,3},{3,2},{4,5},{5,4},{6,7},{7,6},{8,9},{9,8},{10,11... | collective-permute-start | bytes 1179656 | tf_op jit(solution)/shard_map/ppermute | solution.py:407
  40.6 2.5 %collective-permute-start.10 = (bf16[32,6144]{1,0:T(8,128)(2,1)S(1)}, bf16[32,6144]{1,0:T(8,128)(2,1)S(1)}, u32[]{:S(2)}, u32[]{:S(2)}) collective-permute-start(bf16[32,6144]{1,0:T(8,128)(2,1)S(1)} %collective-permute-done.8.refs_2_), channel_id=1, source_target_pairs={{0,1},{1,0},{2,3},{3,2},{4,5},{5,4},{6,7},{7,6},{8,9},{9,8},{10,11... | collective-permute-start | bytes 1179656 | tf_op jit(solution)/shard_map/ppermute | solution.py:407
  41.1 2.5 %collective-permute-start.18 = (bf16[32,6144]{1,0:T(8,128)(2,1)S(1)}, bf16[32,6144]{1,0:T(8,128)(2,1)S(1)}, u32[]{:S(2)}, u32[]{:S(2)}) collective-permute-start(bf16[32,6144]{1,0:T(8,128)(2,1)S(1)} %collective-permute-done.16.refs_10_), channel_id=1, source_target_pairs={{0,1},{1,0},{2,3},{3,2},{4,5},{5,4},{6,7},{7,6},{8,9},{9,8},{10,11... | collective-permute-start | bytes 1179656 | tf_op jit(solution)/shard_map/ppermute | solution.py:407
  53.6 2.7 %collective-permute-start.19 = (f32[256,1024]{1,0:T(8,128)S(1)}, f32[256,1024]{1,0:T(8,128)S(1)}, u32[]{:S(2)}, u32[]{:S(2)}) collective-permute-start(f32[256,1024]{1,0:T(8,128)S(1)} %get-tuple-element.22), channel_id=1, source_target_pairs={{0,1},{1,0},{2,3},{3,2},{4,5},{5,4},{6,7},{7,6},{8,9},{9,8},{10,11... | collective-permute-start | bytes 3145736 | tf_op jit(solution)/shard_map/ppermute | solution.py:407
